TPU v7x, 32 devices: a whole 2x2x4 slice. The times are simulated.
32 devices in a mesh: parts: 2 (over y), blk: 4 (over z), sub: 4 (over x, core).
Axes of the slice: x: 2, y: 2, z: 4, core: 2. Of those that a mesh axis runs over, the one named last changes fastest.
Arguments:
- embeddings: bfloat16 [40, 512, 1024], P(('parts', 'blk'), 'sub'), parts along dimension 0, may hold values from -6 to 6
- row_count: int32 [40], P(('parts', 'blk')), parts along dimension 0, may hold values from 128 to 512, as said below
- fetch_list: int32 [8, 5], P('parts'), parts along dimension 0, may hold values from 0 to 19, as said below
- pair_left: int32 [8, 15], P(('parts', 'blk')), parts along dimension 0, may hold values from 0 to 4, as said below
- pair_right: int32 [8, 15], P(('parts', 'blk')), parts along dimension 0, may hold values from 0 to 4, as said below
- pair_count: int32 [8], P(('parts', 'blk')), parts along dimension 0, may hold values from 1 to 15, as said below
Outputs:
- density: float32 [40, 512], P(('parts', 'blk'), 'sub'), parts along dimension 0
There are 2 independent parts, one for each index of `parts`. A program takes and returns all parts, laid end to end along the dimension named above; each array names one. Nothing has to cross between parts.
Inputs may be any that keep to these rules, and one draw needn't show every extreme that they name: `fetch_list`: row s lists 5 blocks, each once, the blocks of one cluster at consecutive positions; every block is in exactly one row. A row holds at most 2 blocks of one index of blk (block b is owned by index b // 5), and 2 of some owner. Entries p < pair_count[s] list every pair of positions i <= j of one cluster of row s of fetch_list once (pair_left i, pair_right j); clusters hold 1 to 5 blocks; later entries are 0. `pair_right`: see pair_left. `pair_count`: some group has 15 pairs. Rows 0 to row_count - 1 of a block are in use; some block has all 512.
All inputs are finite; a program needn't handle non-finite values.
Results may differ from a plain program's by a relative error of at most 0.0003.
Values may be sent and summed in bfloat16 or wider, within the bound.
No kernel may reach another device: no remote copies, remote signals or barrier semaphores. Data moves between devices by JAX's collectives and lax.ppermute only.
A program may use at most 64 MiB of HBM per device.

v0:
```python
import functools
import itertools
import math

import jax
import jax.numpy as jnp
from jax import lax
from jax.experimental import pallas as pl
from jax.experimental.pallas import tpu as pltpu
from jax.sharding import PartitionSpec as P

kernel_scale = 24.0
norm_eps = 1e-06
VMEM_LIMIT = 48 * 1024 * 1024
ANY = pl.BlockSpec(memory_space=pl.ANY)
SMEM = pl.BlockSpec(memory_space=pltpu.SMEM)
VMEM = pl.BlockSpec(memory_space=pltpu.VMEM)


def block_patterns(places, capacity, blocks):
    if capacity < 2 or places > 4:
        return []
    cost = lambda counts: sum(c * min(k, places - k) for k, c in enumerate(counts))
    best = {}
    for counts in itertools.product(range(capacity + 1), repeat=places):
        if sum(counts) != blocks:
            continue
        turns = [counts[t:] + counts[:t] for t in range(places)]
        pick = min(turns, key=lambda c: (cost(c), c))
        best[min(turns)] = pick
    return sorted(best.values(), key=cost)


def unary(counts):
    return sum(((1 << c) - 1) << (2 * r) for r, c in enumerate(counts))


def plan_kernel(patterns, places, capacity, me_ref, fetch_ref, count_ref, left_ref, right_ref, pairs_ref,
                emb_ref, plan_ref, info_ref, *rest):
    slots, sems = rest[:-1], rest[-1]
    blocks = count_ref.shape[0]
    me = me_ref[0]
    used = jnp.int32(0)
    for s in range(places):
        seen = jnp.int32(0)
        for p in range(blocks):
            owner = lax.div(fetch_ref[s, p], blocks)
            bit = lax.shift_left(jnp.int32(1), 2 * lax.rem(owner + (places - s), places))
            seen = seen | bit | ((seen & bit) << 1)
        used = used | seen
    choice = jnp.int32(len(patterns))
    shift = jnp.int32(0)
    for m in reversed(range(len(patterns))):
        for t in range(places):
            allowed = unary([patterns[m][(t - r) % places] for r in range(places)])
            fits = (used & ~allowed) == 0
            choice = jnp.where(fits, m, choice)
            shift = jnp.where(fits, t, shift)
    plan_ref[0] = choice
    plan_ref[1] = shift
    mine = lax.rem(me + places - shift, places)
    total = places * capacity
    copies = []
    for k in range(places):
        owner = lax.rem(me + places - k, places)
        target = lax.rem(me + k + places - shift, places)
        place, lid, seen = [jnp.int32(0)] * capacity, [jnp.int32(0)] * capacity, jnp.int32(0)
        send, sent = [jnp.int32(0)] * capacity, jnp.int32(0)
        for p in range(blocks):
            listed = fetch_ref[mine, p]
            hit = lax.div(listed, blocks) == owner
            outward = fetch_ref[target, p]
            goes = lax.div(outward, blocks) == me
            for j in range(capacity):
                place[j] = jnp.where(hit & (seen == j), p, place[j])
                lid[j] = jnp.where(hit & (seen == j), listed - owner * blocks, lid[j])
                send[j] = jnp.where(goes & (sent == j), outward - me * blocks, send[j])
            seen = seen + hit.astype(jnp.int32)
            sent = sent + goes.astype(jnp.int32)
        for j in range(capacity):
            at = k * capacity + j
            copy = pltpu.make_async_copy(emb_ref.at[send[j]], slots[at], sems.at[at])
            pl.when(sent > j)(copy.start)
            copies.append((sent > j, copy))
            plan_ref[2 + at] = send[j]
            plan_ref[2 + total + at] = place[j]
            plan_ref[2 + 2 * total + at] = lid[j]
    bits = jnp.int32(0)
    for p in range(left_ref.shape[1]):
        a, b = left_ref[0, p], right_ref[0, p]
        both = lax.shift_left(jnp.int32(1), a * blocks + b) | lax.shift_left(jnp.int32(1), b * blocks + a)
        bits = bits | jnp.where(p < pairs_ref[0], both, 0)
    for b in range(blocks):
        info_ref[b] = count_ref[b]
    info_ref[blocks] = bits
    for filled, copy in copies:
        pl.when(filled)(copy.wait)


def make_plan(patterns, places, capacity, me, embeddings, row_count, fetch_list, left, right, pairs):
    blocks, rows, width = embeddings.shape
    total = places * capacity
    slot = jax.ShapeDtypeStruct((rows, width), embeddings.dtype)
    out = pl.pallas_call(
        functools.partial(plan_kernel, patterns, places, capacity),
        out_shape=[jax.ShapeDtypeStruct((2 + 3 * total,), jnp.int32),
                   jax.ShapeDtypeStruct((blocks + 1,), jnp.int32)] + [slot] * total,
        in_specs=[SMEM] * 6 + [ANY],
        out_specs=[SMEM, SMEM] + [VMEM] * total,
        scratch_shapes=[pltpu.SemaphoreType.DMA((total,))],
        name="plan_and_gather",
    )(me, fetch_list, row_count, left, right, pairs, embeddings)
    return out[0], out[1], out[2:]


def meta_kernel(slots, total, plan_ref, sub_ref, *refs):
    infos, meta_ref = refs[:-1], refs[-1]
    blocks = len(slots)
    bits = jnp.int32(0)
    for k, info in enumerate(infos):
        bits = jnp.where(plan_ref[1] == k, info[blocks], bits)
    for b, (k, at) in enumerate(slots):
        meta_ref[b] = infos[k][plan_ref[2 + 2 * total + at]]
        meta_ref[blocks + b] = plan_ref[2 + total + at]
    meta_ref[2 * blocks] = bits
    meta_ref[2 * blocks + 1] = sub_ref[0]


def make_meta(slots, total, plan, sub, infos):
    blocks = len(slots)
    return pl.pallas_call(
        functools.partial(meta_kernel, slots, total),
        out_shape=jax.ShapeDtypeStruct((2 * blocks + 2,), jnp.int32),
        in_specs=[SMEM] * (2 + len(infos)),
        out_specs=SMEM,
        name="block_meta",
    )(plan, sub, *infos)


def score_kernel(blocks, rows, width, pieces, owned, runs, steps, first, outs, meta_ref, *refs):
    refs = list(refs)
    left_in = [refs.pop(0) for _ in owned]
    right_in = [refs.pop(0) for _ in range(2 * len(runs))]
    acc_in = None if first else refs.pop(0)
    out_refs = [refs.pop(0) for _ in (outs or (0,))]
    left, right, acc, left_scale, gram, left_sems, right_sems = refs
    per = pieces // 2
    copies = []
    for i, a in enumerate(owned):
        copies.append(pltpu.make_async_copy(left_in[i], left.at[pl.ds(a * rows, rows)], left_sems.at[i]))
    for i in range(2 * len(runs)):
        copies.append(pltpu.make_async_copy(right_in[i], right.at[i], right_sems.at[i]))
    for copy in copies:
        copy.start()
    eye = lax.broadcasted_iota(jnp.int32, (rows, rows), 0) == lax.broadcasted_iota(jnp.int32, (rows, rows), 1)
    column = lax.broadcasted_iota(jnp.int32, (1, rows), 1)
    row = lax.broadcasted_iota(jnp.int32, (rows, 1), 0)
    sub = meta_ref[2 * blocks + 1]
    bits = meta_ref[2 * blocks]

    def squares(block):
        wide = block.astype(jnp.float32)
        return jnp.sum(wide * wide, axis=1, keepdims=True)

    def lanes(col):
        return jnp.sum(jnp.where(eye, col, 0.0), axis=0, keepdims=True)

    if first:
        acc[...] = jnp.zeros_like(acc)
    else:
        acc[...] = acc_in[...]
    for i, a in enumerate(owned):
        copies[i].wait()

    @pl.loop(0, len(owned))
    def _(i):
        here = pl.ds((owned[0] + i) * rows, rows)
        inv = lax.rsqrt(squares(left[here, :]) * (1.0 / width) + norm_eps)
        left_scale[here, :] = jnp.broadcast_to(inv * (kernel_scale / width * math.log2(math.e)), (rows, rows))

    arrived = 0
    for lo, hi, start, end in steps:
        fresh = end > arrived

        @pl.loop(start, end)
        def _(run):
            if fresh:
                for h in range(2):
                    pltpu.make_async_copy(right_in[0], right.at[2 * run + h], right_sems.at[2 * run + h]).wait()
            flat = runs[0] + run
            b = lax.div(flat, per)
            q = 2 * lax.rem(flat, per)
            scale_row, valid = [], []
            for h in range(2):
                scale_row.append(lax.rsqrt(lanes(squares(right[2 * run + h])) * (1.0 / width) + norm_eps))
                valid.append((column + (sub ^ (q + h)) * rows < meta_ref[b]).astype(jnp.float32))
            both = jnp.concatenate([right[2 * run], right[2 * run + 1]], axis=0)
            gram[:(hi - lo) * rows, :] = lax.dot_general(
                left[lo * rows:hi * rows, :], both, (((1,), (1,)), ((), ())), preferred_element_type=jnp.float32)
            for a in range(lo, hi):
                here = slice(a * rows, (a + 1) * rows)
                there = slice((a - lo) * rows, (a - lo + 1) * rows)
                paired = (bits >> (meta_ref[blocks + a] * blocks + meta_ref[blocks + b])) & 1
                weight = paired.astype(jnp.float32)
                scale = left_scale[here, :]
                same = eye & ((b == a) & (q == 0))
                near = jnp.exp2(gram[there, :rows] * scale * scale_row[0]) * (valid[0] * weight)
                far = jnp.exp2(gram[there, rows:] * scale * scale_row[1]) * (valid[1] * weight)
                acc[here, :] += jnp.where(same, 0.0, near) + far

        arrived = max(arrived, end)
    if outs is None:
        out_refs[0][...] = acc[...]
        return
    for ref, group in zip(out_refs, outs):
        for n, a in enumerate(group):
            total = jnp.sum(acc[a * rows:(a + 1) * rows, :], axis=1, keepdims=True)
            total = jnp.where(row + sub * rows < meta_ref[a], total, 0.0)
            ref[n:n + 1, :] = jnp.log1p(lanes(total) / (pieces * rows))


def score(blocks, pieces, held, meta, owned, runs, steps, acc=None, outs=None, name="score"):
    rows, width = held[0, 0].shape
    per = pieces // 2
    rights = [held[run // per, 2 * (run % per) + h] for run in runs for h in range(2)]
    tall = max(hi - lo for lo, hi, _, _ in steps) * rows
    sums = jax.ShapeDtypeStruct((blocks * rows, rows), jnp.float32)
    out_shape = [sums] if outs is None else [jax.ShapeDtypeStruct((len(g), rows), jnp.float32) for g in outs]
    flops = sum(4 * (hi - lo) * (end - start) * rows * rows * width for lo, hi, start, end in steps)
    moved = (len(owned) + len(rights)) * rows * width * 2
    result = pl.pallas_call(
        functools.partial(score_kernel, blocks, rows, width, pieces, owned, runs, steps, acc is None, outs),
        out_shape=out_shape,
        in_specs=[SMEM] + [ANY] * (len(owned) + len(rights)) + ([] if acc is None else [VMEM]),
        out_specs=[VMEM] * len(out_shape),
        scratch_shapes=[
            pltpu.VMEM((blocks * rows, width), jnp.bfloat16),
            pltpu.VMEM((len(rights), rows, width), jnp.bfloat16),
            pltpu.VMEM((blocks * rows, rows), jnp.float32),
            pltpu.VMEM((blocks * rows, rows), jnp.float32),
            pltpu.VMEM((tall, 2 * rows), jnp.float32),
            pltpu.SemaphoreType.DMA((len(owned),)),
            pltpu.SemaphoreType.DMA((len(rights),)),
        ],
        compiler_params=pltpu.CompilerParams(vmem_limit_bytes=VMEM_LIMIT),
        cost_estimate=pl.CostEstimate(flops=flops, bytes_accessed=moved, transcendentals=0),
        name=name,
    )(meta, *[held[a, 0] for a in owned], *rights, *([] if acc is None else [acc]))
    return result[0] if outs is None else result


def place_kernel(slots, plan_ref, *refs):
    out_ref = refs[-1]
    for ref, (group) in zip(refs[:-1], slots):
        for n, at in enumerate(group):
            out_ref[pl.ds(plan_ref[2 + at], 1), :] = ref[n:n + 1, :]


def place_rows(slots, plan, returned, blocks, rows):
    return pl.pallas_call(
        functools.partial(place_kernel, slots),
        out_shape=jax.ShapeDtypeStruct((blocks, rows), jnp.float32),
        in_specs=[SMEM] + [VMEM] * len(returned),
        out_specs=VMEM,
        name="place_rows",
    )(plan, *returned)


def shift_by(array, k, places):
    return lax.ppermute(array, "blk", [(i, (i + k) % places) for i in range(places)])


def swap_with(array, q, pieces):
    return lax.ppermute(array, "sub", [(i, i ^ q) for i in range(pieces)])


def pattern_path(counts, capacity, pieces, sub, plan, info, slots):
    places = len(counts)
    order = sorted((k for k in range(places) if counts[k]), key=lambda k: (k * (places - k), k))
    taken = [(k, k * capacity + j) for k in order for j in range(counts[k])]
    blocks = len(taken)
    rows = slots[0].shape[0]
    infos = [info if k == 0 else shift_by(info, k, places) for k in range(places)]
    meta = make_meta(taken, places * capacity, plan, sub, infos)
    held = {}
    for b, (k, at) in enumerate(taken):
        held[b, 0] = slots[at] if k == 0 else shift_by(slots[at], k, places)
    for b in range(blocks):
        held[b, 2] = swap_with(held[b, 0], 2, pieces)
        held[b, 1] = swap_with(held[b, 0], 1, pieces)
        held[b, 3] = swap_with(held[b, 2], 1, pieces)
    end = blocks - 1
    per = pieces // 2
    early = range(end * per)
    acc = score(blocks, pieces, held, meta, range(end), early, [(0, end, 0, len(early))], name="score_early")
    most = range(end * per + per - 1)
    acc = score(blocks, pieces, held, meta, range(blocks), most,
                [(end, blocks, 0, len(early)), (0, blocks, len(early), len(most))], acc, name="score_middle")
    groups = [[b for b in range(blocks) if taken[b][0] == k] for k in order]
    sums = score(blocks, pieces, held, meta, range(blocks), range(len(most), blocks * per), [(0, blocks, 0, 1)], acc, groups,
                 name="score_late")
    returned = [s if k == 0 else shift_by(s, places - k, places) for k, s in zip(order, sums)]
    return place_rows([[taken[b][1] for b in g] for g in groups], plan, returned, blocks, rows)


def general_path(capacity, pieces, embeddings, row_count, fetch_list, left, right, pairs):
    places = lax.axis_size("blk")
    me = lax.axis_index("blk")
    sub = lax.axis_index("sub")
    blocks, rows, width = embeddings.shape
    total = places * capacity
    local_ids = jnp.arange(blocks, dtype=jnp.int32)
    slot_ids = jnp.arange(total, dtype=jnp.int32)
    owned = me * blocks + local_ids
    here = fetch_list[:, :, None] == owned[None, None, :]
    scorer = jnp.sum(jnp.where(here, jnp.arange(places, dtype=jnp.int32)[:, None, None], 0), axis=(0, 1))
    same = scorer[:, None] == scorer[None, :]
    rank = jnp.sum(same & (local_ids[None, :] < local_ids[:, None]), axis=1)
    send_slot = scorer * capacity + rank
    placing = send_slot[:, None] == slot_ids[None, :]
    source = jnp.sum(jnp.where(placing, local_ids[:, None], 0), axis=0)
    out_counts = jnp.where(jnp.any(placing, axis=0), jnp.take(row_count, source), 0)
    exchange = lambda x: lax.all_to_all(x, "blk", split_axis=0, concat_axis=0, tiled=True)
    incoming = exchange(jnp.take(embeddings, source, axis=0))
    in_counts = exchange(out_counts)
    wanted = lax.dynamic_index_in_dim(fetch_list, me, 0, keepdims=False)
    owner, local = wanted // blocks, wanted % blocks
    together = owner[:, None] == owner[None, :]
    recv_rank = jnp.sum(together & (local[None, :] < local[:, None]), axis=1)
    recv_slot = owner * capacity + recv_rank
    counts = jnp.take(in_counts, recv_slot, axis=0)
    live = jnp.arange(left.shape[1], dtype=jnp.int32) < pairs[0]
    one = jnp.int32(1)
    hot = lambda at: jnp.where(live[:, None], (at[:, None] == jnp.arange(blocks * blocks)).astype(jnp.int32), 0)
    listed = jnp.max(hot(left[0] * blocks + right[0]) | hot(right[0] * blocks + left[0]), axis=0)
    bits = jnp.sum(listed * lax.shift_left(one, jnp.arange(blocks * blocks, dtype=jnp.int32)))
    meta = jnp.concatenate([counts, local_ids, bits[None], sub[None].astype(jnp.int32)]).astype(jnp.int32)
    held = {}
    for b in range(blocks):
        held[b, 0] = lax.dynamic_index_in_dim(incoming, recv_slot[b], 0, keepdims=False)
        for q in range(1, pieces):
            held[b, q] = swap_with(held[b, 0], q, pieces)
    runs = range(blocks * pieces // 2)
    (dense,) = score(blocks, pieces, held, meta, range(blocks), runs, [(0, blocks, 0, len(runs))], None,
                     [list(range(blocks))], name="score_all")
    back = (recv_slot[None, :] == slot_ids[:, None]).astype(jnp.float32)
    returned = exchange(jnp.sum(back[:, :, None] * dense[None, :, :], axis=1))
    return jnp.take(returned, send_slot, axis=0)


def body(embeddings, row_count, fetch_list, pair_left, pair_right, pair_count):
    places = lax.axis_size("blk")
    pieces = lax.axis_size("sub")
    blocks = embeddings.shape[0]
    capacity = (blocks + places - 1) // places
    given = (embeddings, row_count, fetch_list, pair_left, pair_right, pair_count)
    general = functools.partial(general_path, capacity, pieces)
    patterns = block_patterns(places, capacity, blocks)
    if not patterns or pieces != 4:
        return general(*given)
    me = lax.axis_index("blk").astype(jnp.int32)[None]
    sub = lax.axis_index("sub").astype(jnp.int32)[None]
    plan, info, slots = make_plan(patterns, places, capacity, me, *given)
    branches = [
        lambda plan, info, slots, given, counts=counts: pattern_path(counts, capacity, pieces, sub, plan, info, slots)
        for counts in patterns
    ] + [lambda plan, info, slots, given: general(*given)]
    return lax.switch(plan[0], branches, plan, info, slots, given)


def solution(mesh):
    in_specs = (
        P(("parts", "blk"), "sub", None),
        P(("parts", "blk")),
        P("parts", None),
        P(("parts", "blk"), None),
        P(("parts", "blk"), None),
        P(("parts", "blk")),
    )
    out_specs = P(("parts", "blk"), "sub")
    return jax.shard_map(body, mesh=mesh, in_specs=in_specs, out_specs=out_specs, check_vma=False)
```

profile of v0, /device:TPU:0, one launch (start us, length us, event | category | flops | bytes accessed | tf_op | source)
XLA Modules:
  0.0 77.0 jit_solution(13677890717002392469)
XLA Ops:
  0.7 3.4 %plan_and_gather.1 = (s32[26]{0:T(128)S(1)}, s32[6]{0:T(128)S(1)}, bf16[128,1024]{1,0:T(8,128)(2,1)}, bf16[128,1024]{1,0:T(8,128)(2,1)}, bf16[128,1024]{1,0:T(8,...) custom-call(s32[1]{0:T(128)} %bitcast.33.me_ref, ...), custom_call_target="tpu_custom_call" | custom-call | tf_op jit(solution)/shard_map/plan_and_gather/pallas_call | solution.py:104
  4.1 72.3 %conditional.1 = (f32[5,128]{1,0:T(8,128)S(1)}) conditional(s32[]{:T(128)} %bitcast.34, (s32[6]{0:T(128)S(1)}, s32[26]{0:T(128)S(1)}, s32[1]{0:T(128)}, bf16[128,1024]{1,0:T(8,128)(2,1)S(1)}, bf16[128,1024]{1,0:T(8,128)(2,1)S(1)}, /*index=5*/bf16[128,1024]{1,0:T(8,128)(2,1)S(1)}, bf16[128,1024]{1,0:T(8,128)(2,1)}, ...), branch_computations={%region_0.0_spmd, %region_1.0_spmd, %region_2.0_spmd, %region_3.0_... | conditional | flops 3356509184 | bytes 43828260 | solution.py:368
  4.3 3.1 %collective-permute-start.73 = (bf16[128,1024]{1,0:T(8,128)(2,1)S(1)}, bf16[128,1024]{1,0:T(8,128)(2,1)S(1)}, u32[]{:S(2)}, u32[]{:S(2)}) collective-permute-start(bf16[128,1024]{1,0:T(8,128)(2,1)S(1)} %get-tuple-element.125), channel_id=1, source_target_pairs={{0,4},{4,8},{8,12},{12,0},{1,5},{5,9},{9,13},{13,1},{2,6},{6,10},{... | collective-permute-start | bytes 786440 | tf_op jit(solution)/shard_map/cond/branch_3_fun/ppermute | solution.py:270
  7.4 2.1 %collective-permute-start.74 = (bf16[128,1024]{1,0:T(8,128)(2,1)S(1)}, bf16[128,1024]{1,0:T(8,128)(2,1)S(1)}, u32[]{:S(2)}, u32[]{:S(2)}) collective-permute-start(bf16[128,1024]{1,0:T(8,128)(2,1)S(1)} %get-tuple-element.126), channel_id=1, source_target_pairs={{0,12},{4,0},{8,4},{12,8},{1,13},{5,1},{9,5},{13,9},{2,14},{6,2},{... | collective-permute-start | bytes 786440 | tf_op jit(solution)/shard_map/cond/branch_3_fun/ppermute | solution.py:270
  9.5 0.0 collective-permute-start.70
  9.5 2.5 %collective-permute-start.71 = (s32[6]{0:T(128)S(1)}, s32[6]{0:T(128)S(1)}, u32[]{:S(2)}, u32[]{:S(2)}) collective-permute-start(s32[6]{0:T(128)S(1)} %get-tuple-element.122.refs_0_), channel_id=1, source_target_pairs={{0,8},{4,12},{8,0},{12,4},{1,9},{5,13},{9,1},{13,5},{2,10},{6,14},... | collective-permute-start | bytes 80 | tf_op jit(solution)/shard_map/cond/branch_3_fun/ppermute | solution.py:270
  12.0 1.3 %collective-permute-start.72 = (s32[6]{0:T(128)S(1)}, s32[6]{0:T(128)S(1)}, u32[]{:S(2)}, u32[]{:S(2)}) collective-permute-start(s32[6]{0:T(128)S(1)} %get-tuple-element.122.refs_0_), channel_id=1, source_target_pairs={{0,12},{4,0},{8,4},{12,8},{1,13},{5,1},{9,5},{13,9},{2,14},{6,2},{... | collective-permute-start | bytes 80 | tf_op jit(solution)/shard_map/cond/branch_3_fun/ppermute | solution.py:270
  13.4 8.0 %collective-permute-done.70.refs_1_ = s32[6]{0:T(128)S(1)} collective-permute-done((s32[6]{0:T(128)S(1)}, s32[6]{0:T(128)S(1)}, u32[]{:S(2)}, u32[]{:S(2)}) %collective-permute-start.70) | collective-permute-done | bytes 56 | tf_op jit(solution)/shard_map/cond/branch_3_fun/ppermute | solution.py:270
  21.4 1.5 %collective-permute-start.79 = (bf16[128,1024]{1,0:T(8,128)(2,1)}, bf16[128,1024]{1,0:T(8,128)(2,1)S(1)}, u32[]{:S(2)}, u32[]{:S(2)}) collective-permute-start(bf16[128,1024]{1,0:T(8,128)(2,1)} %get-tuple-element.123.refs_0_.refs_4_.refs_5_), channel_id=1, source_target_pairs={{0,2},{1,3},{2,0},{3,1},{4,6},{5,7},{6,4},{7,5},{8,10},{9,11},{10,... | collective-permute-start | bytes 786440 | tf_op jit(solution)/shard_map/cond/branch_3_fun/ppermute | solution.py:274
  22.9 0.0 collective-permute-done.71.refs_2_
  22.9 0.5 collective-permute-start.82
  23.4 0.0 collective-permute-done.72.refs_3_
  23.4 0.0 collective-permute-start.78
  23.4 0.0 collective-permute-done.73.refs_2_.refs_12_.refs_13_
  23.4 0.5 collective-permute-start.81
  23.9 0.0 collective-permute-done.74.refs_3_.refs_16_.refs_17_
  24.0 0.8 %collective-permute-start.75 = (bf16[128,1024]{1,0:T(8,128)(2,1)}, bf16[128,1024]{1,0:T(8,128)(2,1)S(1)}, u32[]{:S(2)}, u32[]{:S(2)}) collective-permute-start(bf16[128,1024]{1,0:T(8,128)(2,1)} %get-tuple-element.127), channel_id=1, source_target_pairs={{0,8},{4,12},{8,0},{12,4},{1,9},{5,13},{9,1},{13,5},{2,10},{6,14},... | collective-permute-start | bytes 786440 | tf_op jit(solution)/shard_map/cond/branch_3_fun/ppermute | solution.py:270
  24.7 6.1 %collective-permute-done.79.refs_6_.refs_7_ = bf16[128,1024]{1,0:T(8,128)(2,1)S(1)} collective-permute-done((bf16[128,1024]{1,0:T(8,128)(2,1)}, bf16[128,1024]{1,0:T(8,128)(2,1)S(1)}, u32[]{:S(2)}, u32[]{:S(2)}) %collective-permute-start.79) | collective-permute-done | bytes 262176 | tf_op jit(solution)/shard_map/cond/branch_3_fun/ppermute | solution.py:274
  30.9 1.5 %collective-permute-start.85 = (bf16[128,1024]{1,0:T(8,128)(2,1)S(1)}, bf16[128,1024]{1,0:T(8,128)(2,1)S(1)}, u32[]{:S(2)}, u32[]{:S(2)}) collective-permute-start(bf16[128,1024]{1,0:T(8,128)(2,1)S(1)} %collective-permute-done.73.refs_2_.refs_12_.refs_13_), channel_id=1, source_target_pairs={{0,2},{1,3},{2,0},{3,1},{4,6},{5,7},{6,4},{7,5},{8,10},{9,11},{10,... | collective-permute-start | bytes 786440 | tf_op jit(solution)/shard_map/cond/branch_3_fun/ppermute | solution.py:274
  32.3 4.1 %collective-permute-done.82.refs_10_.refs_11_ = bf16[128,1024]{1,0:T(8,128)(2,1)S(1)} collective-permute-done((bf16[128,1024]{1,0:T(8,128)(2,1)}, bf16[128,1024]{1,0:T(8,128)(2,1)S(1)}, u32[]{:S(2)}, u32[]{:S(2)}) %collective-permute-start.82) | collective-permute-done | bytes 262176 | tf_op jit(solution)/shard_map/cond/branch_3_fun/ppermute | solution.py:274
  36.5 1.5 %collective-permute-start.88 = (bf16[128,1024]{1,0:T(8,128)(2,1)S(1)}, bf16[128,1024]{1,0:T(8,128)(2,1)S(1)}, u32[]{:S(2)}, u32[]{:S(2)}) collective-permute-start(bf16[128,1024]{1,0:T(8,128)(2,1)S(1)} %collective-permute-done.74.refs_3_.refs_16_.refs_17_), channel_id=1, source_target_pairs={{0,2},{1,3},{2,0},{3,1},{4,6},{5,7},{6,4},{7,5},{8,10},{9,11},{10,... | collective-permute-start | bytes 786440 | tf_op jit(solution)/shard_map/cond/branch_3_fun/ppermute | solution.py:274
  38.0 0.0 collective-permute-done.78.refs_5_.refs_6_
  38.0 0.0 collective-permute-start.80
  38.0 0.0 collective-permute-done.81.refs_9_.refs_10_
  38.0 0.5 collective-permute-start.83
  38.5 0.0 collective-permute-done.75.refs_4_.refs_21_
  38.5 0.1 collective-permute-start.84
  38.6 3.5 %collective-permute-done.85.refs_14_.refs_15_ = bf16[128,1024]{1,0:T(8,128)(2,1)S(1)} collective-permute-done((bf16[128,1024]{1,0:T(8,128)(2,1)S(1)}, bf16[128,1024]{1,0:T(8,128)(2,1)S(1)}, u32[]{:S(2)}, u32[]{:S(2)}) %collective-permute-start.85) | collective-permute-done | bytes 262176 | tf_op jit(solution)/shard_map/cond/branch_3_fun/ppermute | solution.py:274
  42.1 0.0 collective-permute-start.87
  42.1 3.6 %collective-permute-done.88.refs_18_.refs_19_ = bf16[128,1024]{1,0:T(8,128)(2,1)S(1)} collective-permute-done((bf16[128,1024]{1,0:T(8,128)(2,1)S(1)}, bf16[128,1024]{1,0:T(8,128)(2,1)S(1)}, u32[]{:S(2)}, u32[]{:S(2)}) %collective-permute-start.88) | collective-permute-done | bytes 262176 | tf_op jit(solution)/shard_map/cond/branch_3_fun/ppermute | solution.py:274
  45.6 1.2 %collective-permute-start.76 = (bf16[128,1024]{1,0:T(8,128)(2,1)S(1)}, bf16[128,1024]{1,0:T(8,128)(2,1)S(1)}, u32[]{:S(2)}, u32[]{:S(2)}) collective-permute-start(bf16[128,1024]{1,0:T(8,128)(2,1)S(1)} %collective-permute-done.75.refs_4_.refs_21_), channel_id=1, source_target_pairs={{0,2},{1,3},{2,0},{3,1},{4,6},{5,7},{6,4},{7,5},{8,10},{9,11},{10,... | collective-permute-start | bytes 786440 | tf_op jit(solution)/shard_map/cond/branch_3_fun/ppermute | solution.py:274
  46.9 0.0 collective-permute-done.80.refs_7_.refs_8_
  46.9 0.0 collective-permute-start.86
  46.9 0.0 collective-permute-done.83.refs_11_.refs_12_
  46.9 0.5 collective-permute-start.89
  47.4 0.0 collective-permute-done.84.refs_13_.refs_14_
  47.4 0.1 collective-permute-start.90
  47.5 0.0 copy-done.31
  47.5 0.0 copy-done.38
  47.5 1.2 %block_meta.7.meta_ref = s32[12]{0:T(128)} custom-call(s32[26]{0:T(128)S(1)} %get-tuple-element.120.plan_ref, s32[1]{0:T(128)} %get-tuple-element.121.sub_ref, s32[6]{0:T(128)S(1)} %get-tuple-element.122.refs_0_, s32[6]{0:T(128)} %copy-done.31, s32[6]{0:T(128)} %copy-done.34, s32[6]{0:T(128)} %copy-done.38), custom_call_target="tpu_custom_call" | custom-call | tf_op jit(solution)/shard_map/cond/branch_3_fun/block_meta/pallas_call | solution.py:131
  48.7 3.3 %collective-permute-done.76.refs_5_ = bf16[128,1024]{1,0:T(8,128)(2,1)S(1)} collective-permute-done((bf16[128,1024]{1,0:T(8,128)(2,1)S(1)}, bf16[128,1024]{1,0:T(8,128)(2,1)S(1)}, u32[]{:S(2)}, u32[]{:S(2)}) %collective-permute-start.76) | collective-permute-done | bytes 262176 | tf_op jit(solution)/shard_map/cond/branch_3_fun/ppermute | solution.py:274
  52.0 0.0 collective-permute-start.77
  52.0 0.0 collective-permute-done.87.refs_17_.refs_18_
  52.0 0.0 collective-permute-done.86.refs_15_.refs_16_
  52.0 0.0 collective-permute-done.89.refs_19_.refs_20_
  52.0 0.0 copy-start.4
  52.1 0.6 copy-done.4
  52.6 6.4 %score_early.7.refs_23_ = f32[640,128]{1,0:T(8,128)S(1)} custom-call(s32[12]{0:T(128)S(1)} %copy-done.4, bf16[128,1024]{1,0:T(8,128)(2,1)} %get-tuple-element.123.refs_0_.refs_4_.refs_5_, bf16[128,1024]{1,0:T(8,128)(2,1)} %get-tuple-element.124.refs_1_.refs_8_.refs_9_, bf16[128,1024]{1,0:T(8,128)(2,1)S(1)} %collective-permute-done.73.refs_2_.refs_12_.refs_13_, ...), custom_call_target="tpu_custom_call" | custom-call | flops 2147483648 | bytes 5242880 | tf_op jit(solution)/shard_map/cond/branch_3_fun/score_early/pallas_call | solution.py:231
  59.1 0.0 collective-permute-done.90.refs_22_
  59.1 5.8 %score_middle.7.refs_7_ = f32[640,128]{1,0:T(8,128)S(1)} custom-call(s32[12]{0:T(128)S(1)} %copy-done.4, bf16[128,1024]{1,0:T(8,128)(2,1)} %get-tuple-element.123.refs_0_.refs_4_.refs_5_, bf16[128,1024]{1,0:T(8,128)(2,1)} %get-tuple-element.124.refs_1_.refs_8_.refs_9_, bf16[128,1024]{1,0:T(8,128)(2,1)S(1)} %collective-permute-done.73.refs_2_.refs_12_.refs_13_, ...), custom_call_target="tpu_custom_call" | custom-call | flops 872415232 | bytes 6029312 | tf_op jit(solution)/shard_map/cond/branch_3_fun/score_middle/pallas_call | solution.py:231
  64.8 0.0 collective-permute-done.77.refs_6_
  64.8 3.0 %score_late.7 = (f32[2,128]{1,0:T(2,128)S(1)}, f32[1,128]{1,0:T(1,128)S(1)}, f32[1,128]{1,0:T(1,128)S(1)}, f32[1,128]{1,0:T(1,128)S(1)}) custom-call(s32[12]{0:T(128)S(1)} %copy-done.4, bf16[128,1024]{1,0:T(8,128)(2,1)} %get-tuple-element.123.refs_0_.refs_4_.refs_5_, bf16[128,1024]{1,0:T(8,128)(2,1)} %get-tuple-element.124.refs_1_.refs_8_.refs_9_, ...), custom_call_target="tpu_custom_call" | custom-call | flops 335544320 | bytes 1835008 | tf_op jit(solution)/shard_map/cond/branch_3_fun/score_late/pallas_call | solution.py:231
  67.8 0.0 copy-start.7
  67.8 0.6 copy-done.7
  68.4 0.0 collective-permute-start.91
  68.4 2.0 %collective-permute-start.92 = (f32[1,128]{1,0:T(1,128)S(1)}, f32[1,128]{1,0:T(1,128)S(1)}, u32[]{:S(2)}, u32[]{:S(2)}) collective-permute-start(f32[1,128]{1,0:T(1,128)S(1)} %get-tuple-element.130), channel_id=1, source_target_pairs={{0,4},{4,8},{8,12},{12,0},{1,5},{5,9},{9,13},{13,1},{2,6},{6,10},{... | collective-permute-start | bytes 1544 | tf_op jit(solution)/shard_map/cond/branch_3_fun/ppermute | solution.py:270
  70.4 0.0 collective-permute-start.93
  70.4 1.5 %collective-permute-done.91.refs_1_ = f32[1,128]{1,0:T(1,128)S(1)} collective-permute-done((f32[1,128]{1,0:T(1,128)S(1)}, f32[1,128]{1,0:T(1,128)S(1)}, u32[]{:S(2)}, u32[]{:S(2)}) %collective-permute-start.91) | collective-permute-done | bytes 544 | tf_op jit(solution)/shard_map/cond/branch_3_fun/ppermute | solution.py:270
  71.9 1.8 %collective-permute-done.92.refs_2_ = f32[1,128]{1,0:T(1,128)S(1)} collective-permute-done((f32[1,128]{1,0:T(1,128)S(1)}, f32[1,128]{1,0:T(1,128)S(1)}, u32[]{:S(2)}, u32[]{:S(2)}) %collective-permute-start.92) | collective-permute-done | bytes 544 | tf_op jit(solution)/shard_map/cond/branch_3_fun/ppermute | solution.py:270
  73.7 1.1 %collective-permute-done.93.refs_3_ = f32[1,128]{1,0:T(1,128)S(1)} collective-permute-done((f32[1,128]{1,0:T(1,128)S(1)}, f32[1,128]{1,0:T(1,128)S(1)}, u32[]{:S(2)}, u32[]{:S(2)}) %collective-permute-start.93) | collective-permute-done | bytes 544 | tf_op jit(solution)/shard_map/cond/branch_3_fun/ppermute | solution.py:270
  74.9 0.6 copy-done.24
  75.4 0.7 place_rows.7
  76.4 0.0 copy-start.15
  76.4 0.6 copy-done.15
  (9 shorter events, 0.0 us)
Async XLA Ops:
  4.3 19.1 %collective-permute-start.73 = (bf16[128,1024]{1,0:T(8,128)(2,1)S(1)}, bf16[128,1024]{1,0:T(8,128)(2,1)S(1)}, u32[]{:S(2)}, u32[]{:S(2)}) collective-permute-start(bf16[128,1024]{1,0:T(8,128)(2,1)S(1)} %get-tuple-element.125), channel_id=1, source_target_pairs={{0,4},{4,8},{8,12},{12,0},{1,5},{5,9},{9,13},{13,1},{2,6},{6,10},{... | collective-permute-start | bytes 786440 | tf_op jit(solution)/shard_map/cond/branch_3_fun/ppermute | solution.py:270
  7.4 16.5 %collective-permute-start.74 = (bf16[128,1024]{1,0:T(8,128)(2,1)S(1)}, bf16[128,1024]{1,0:T(8,128)(2,1)S(1)}, u32[]{:S(2)}, u32[]{:S(2)}) collective-permute-start(bf16[128,1024]{1,0:T(8,128)(2,1)S(1)} %get-tuple-element.126), channel_id=1, source_target_pairs={{0,12},{4,0},{8,4},{12,8},{1,13},{5,1},{9,5},{13,9},{2,14},{6,2},{... | collective-permute-start | bytes 786440 | tf_op jit(solution)/shard_map/cond/branch_3_fun/ppermute | solution.py:270
  9.5 11.9 %collective-permute-start.70 = (s32[6]{0:T(128)S(1)}, s32[6]{0:T(128)S(1)}, u32[]{:S(2)}, u32[]{:S(2)}) collective-permute-start(s32[6]{0:T(128)S(1)} %get-tuple-element.122.refs_0_), channel_id=1, source_target_pairs={{0,4},{4,8},{8,12},{12,0},{1,5},{5,9},{9,13},{13,1},{2,6},{6,10},{... | collective-permute-start | bytes 80 | tf_op jit(solution)/shard_map/cond/branch_3_fun/ppermute | solution.py:270
  9.5 13.4 %collective-permute-start.71 = (s32[6]{0:T(128)S(1)}, s32[6]{0:T(128)S(1)}, u32[]{:S(2)}, u32[]{:S(2)}) collective-permute-start(s32[6]{0:T(128)S(1)} %get-tuple-element.122.refs_0_), channel_id=1, source_target_pairs={{0,8},{4,12},{8,0},{12,4},{1,9},{5,13},{9,1},{13,5},{2,10},{6,14},... | collective-permute-start | bytes 80 | tf_op jit(solution)/shard_map/cond/branch_3_fun/ppermute | solution.py:270
  12.0 11.4 %collective-permute-start.72 = (s32[6]{0:T(128)S(1)}, s32[6]{0:T(128)S(1)}, u32[]{:S(2)}, u32[]{:S(2)}) collective-permute-start(s32[6]{0:T(128)S(1)} %get-tuple-element.122.refs_0_), channel_id=1, source_target_pairs={{0,12},{4,0},{8,4},{12,8},{1,13},{5,1},{9,5},{13,9},{2,14},{6,2},{... | collective-permute-start | bytes 80 | tf_op jit(solution)/shard_map/cond/branch_3_fun/ppermute | solution.py:270
  21.4 26.1 %copy-start.31 = (s32[6]{0:T(128)}, s32[6]{0:T(128)S(1)}, u32[]{:S(2)}) copy-start(s32[6]{0:T(128)S(1)} %collective-permute-done.70.refs_1_) | copy-start | bytes 76 | tf_op jit(solution)/shard_map/cond
  21.4 9.5 %collective-permute-start.79 = (bf16[128,1024]{1,0:T(8,128)(2,1)}, bf16[128,1024]{1,0:T(8,128)(2,1)S(1)}, u32[]{:S(2)}, u32[]{:S(2)}) collective-permute-start(bf16[128,1024]{1,0:T(8,128)(2,1)} %get-tuple-element.123.refs_0_.refs_4_.refs_5_), channel_id=1, source_target_pairs={{0,2},{1,3},{2,0},{3,1},{4,6},{5,7},{6,4},{7,5},{8,10},{9,11},{10,... | collective-permute-start | bytes 786440 | tf_op jit(solution)/shard_map/cond/branch_3_fun/ppermute | solution.py:274
  22.9 24.6 %copy-start.34 = (s32[6]{0:T(128)}, s32[6]{0:T(128)S(1)}, u32[]{:S(2)}) copy-start(s32[6]{0:T(128)S(1)} %collective-permute-done.71.refs_2_) | copy-start | bytes 76 | tf_op jit(solution)/shard_map/cond
  22.9 13.6 %collective-permute-start.82 = (bf16[128,1024]{1,0:T(8,128)(2,1)}, bf16[128,1024]{1,0:T(8,128)(2,1)S(1)}, u32[]{:S(2)}, u32[]{:S(2)}) collective-permute-start(bf16[128,1024]{1,0:T(8,128)(2,1)} %get-tuple-element.124.refs_1_.refs_8_.refs_9_), channel_id=1, source_target_pairs={{0,2},{1,3},{2,0},{3,1},{4,6},{5,7},{6,4},{7,5},{8,10},{9,11},{10,... | collective-permute-start | bytes 786440 | tf_op jit(solution)/shard_map/cond/branch_3_fun/ppermute | solution.py:274
  23.4 24.1 %copy-start.38 = (s32[6]{0:T(128)}, s32[6]{0:T(128)S(1)}, u32[]{:S(2)}) copy-start(s32[6]{0:T(128)S(1)} %collective-permute-done.72.refs_3_) | copy-start | bytes 76 | tf_op jit(solution)/shard_map/cond
  23.4 14.5 %collective-permute-start.78 = (bf16[128,1024]{1,0:T(8,128)(2,1)}, bf16[128,1024]{1,0:T(8,128)(2,1)S(1)}, u32[]{:S(2)}, u32[]{:S(2)}) collective-permute-start(bf16[128,1024]{1,0:T(8,128)(2,1)} %get-tuple-element.123.refs_0_.refs_4_.refs_5_), channel_id=1, source_target_pairs={{0,1},{1,0},{2,3},{3,2},{4,5},{5,4},{6,7},{7,6},{8,9},{9,8},{10,11... | collective-permute-start | bytes 786440 | tf_op jit(solution)/shard_map/cond/branch_3_fun/ppermute | solution.py:274
  23.4 14.5 %collective-permute-start.81 = (bf16[128,1024]{1,0:T(8,128)(2,1)}, bf16[128,1024]{1,0:T(8,128)(2,1)S(1)}, u32[]{:S(2)}, u32[]{:S(2)}) collective-permute-start(bf16[128,1024]{1,0:T(8,128)(2,1)} %get-tuple-element.124.refs_1_.refs_8_.refs_9_), channel_id=1, source_target_pairs={{0,1},{1,0},{2,3},{3,2},{4,5},{5,4},{6,7},{7,6},{8,9},{9,8},{10,11... | collective-permute-start | bytes 786440 | tf_op jit(solution)/shard_map/cond/branch_3_fun/ppermute | solution.py:274
  24.0 14.5 %collective-permute-start.75 = (bf16[128,1024]{1,0:T(8,128)(2,1)}, bf16[128,1024]{1,0:T(8,128)(2,1)S(1)}, u32[]{:S(2)}, u32[]{:S(2)}) collective-permute-start(bf16[128,1024]{1,0:T(8,128)(2,1)} %get-tuple-element.127), channel_id=1, source_target_pairs={{0,8},{4,12},{8,0},{12,4},{1,9},{5,13},{9,1},{13,5},{2,10},{6,14},... | collective-permute-start | bytes 786440 | tf_op jit(solution)/shard_map/cond/branch_3_fun/ppermute | solution.py:270
  30.9 11.2 %collective-permute-start.85 = (bf16[128,1024]{1,0:T(8,128)(2,1)S(1)}, bf16[128,1024]{1,0:T(8,128)(2,1)S(1)}, u32[]{:S(2)}, u32[]{:S(2)}) collective-permute-start(bf16[128,1024]{1,0:T(8,128)(2,1)S(1)} %collective-permute-done.73.refs_2_.refs_12_.refs_13_), channel_id=1, source_target_pairs={{0,2},{1,3},{2,0},{3,1},{4,6},{5,7},{6,4},{7,5},{8,10},{9,11},{10,... | collective-permute-start | bytes 786440 | tf_op jit(solution)/shard_map/cond/branch_3_fun/ppermute | solution.py:274
  36.5 9.2 %collective-permute-start.88 = (bf16[128,1024]{1,0:T(8,128)(2,1)S(1)}, bf16[128,1024]{1,0:T(8,128)(2,1)S(1)}, u32[]{:S(2)}, u32[]{:S(2)}) collective-permute-start(bf16[128,1024]{1,0:T(8,128)(2,1)S(1)} %collective-permute-done.74.refs_3_.refs_16_.refs_17_), channel_id=1, source_target_pairs={{0,2},{1,3},{2,0},{3,1},{4,6},{5,7},{6,4},{7,5},{8,10},{9,11},{10,... | collective-permute-start | bytes 786440 | tf_op jit(solution)/shard_map/cond/branch_3_fun/ppermute | solution.py:274
  38.0 8.9 %collective-permute-start.80 = (bf16[128,1024]{1,0:T(8,128)(2,1)S(1)}, bf16[128,1024]{1,0:T(8,128)(2,1)S(1)}, u32[]{:S(2)}, u32[]{:S(2)}) collective-permute-start(bf16[128,1024]{1,0:T(8,128)(2,1)S(1)} %collective-permute-done.79.refs_6_.refs_7_), channel_id=1, source_target_pairs={{0,1},{1,0},{2,3},{3,2},{4,5},{5,4},{6,7},{7,6},{8,9},{9,8},{10,11... | collective-permute-start | bytes 786440 | tf_op jit(solution)/shard_map/cond/branch_3_fun/ppermute | solution.py:274
  38.0 8.9 %collective-permute-start.83 = (bf16[128,1024]{1,0:T(8,128)(2,1)S(1)}, bf16[128,1024]{1,0:T(8,128)(2,1)S(1)}, u32[]{:S(2)}, u32[]{:S(2)}) collective-permute-start(bf16[128,1024]{1,0:T(8,128)(2,1)S(1)} %collective-permute-done.82.refs_10_.refs_11_), channel_id=1, source_target_pairs={{0,1},{1,0},{2,3},{3,2},{4,5},{5,4},{6,7},{7,6},{8,9},{9,8},{10,11... | collective-permute-start | bytes 786440 | tf_op jit(solution)/shard_map/cond/branch_3_fun/ppermute | solution.py:274
  38.5 8.9 %collective-permute-start.84 = (bf16[128,1024]{1,0:T(8,128)(2,1)S(1)}, bf16[128,1024]{1,0:T(8,128)(2,1)S(1)}, u32[]{:S(2)}, u32[]{:S(2)}) collective-permute-start(bf16[128,1024]{1,0:T(8,128)(2,1)S(1)} %collective-permute-done.73.refs_2_.refs_12_.refs_13_), channel_id=1, source_target_pairs={{0,1},{1,0},{2,3},{3,2},{4,5},{5,4},{6,7},{7,6},{8,9},{9,8},{10,11... | collective-permute-start | bytes 786440 | tf_op jit(solution)/shard_map/cond/branch_3_fun/ppermute | solution.py:274
  42.1 9.9 %collective-permute-start.87 = (bf16[128,1024]{1,0:T(8,128)(2,1)S(1)}, bf16[128,1024]{1,0:T(8,128)(2,1)}, u32[]{:S(2)}, u32[]{:S(2)}) collective-permute-start(bf16[128,1024]{1,0:T(8,128)(2,1)S(1)} %collective-permute-done.74.refs_3_.refs_16_.refs_17_), channel_id=1, source_target_pairs={{0,1},{1,0},{2,3},{3,2},{4,5},{5,4},{6,7},{7,6},{8,9},{9,8},{10,11... | collective-permute-start | bytes 786440 | tf_op jit(solution)/shard_map/cond/branch_3_fun/ppermute | solution.py:274
  45.6 6.4 %collective-permute-start.76 = (bf16[128,1024]{1,0:T(8,128)(2,1)S(1)}, bf16[128,1024]{1,0:T(8,128)(2,1)S(1)}, u32[]{:S(2)}, u32[]{:S(2)}) collective-permute-start(bf16[128,1024]{1,0:T(8,128)(2,1)S(1)} %collective-permute-done.75.refs_4_.refs_21_), channel_id=1, source_target_pairs={{0,2},{1,3},{2,0},{3,1},{4,6},{5,7},{6,4},{7,5},{8,10},{9,11},{10,... | collective-permute-start | bytes 786440 | tf_op jit(solution)/shard_map/cond/branch_3_fun/ppermute | solution.py:274
  46.9 5.1 %collective-permute-start.86 = (bf16[128,1024]{1,0:T(8,128)(2,1)S(1)}, bf16[128,1024]{1,0:T(8,128)(2,1)}, u32[]{:S(2)}, u32[]{:S(2)}) collective-permute-start(bf16[128,1024]{1,0:T(8,128)(2,1)S(1)} %collective-permute-done.85.refs_14_.refs_15_), channel_id=1, source_target_pairs={{0,1},{1,0},{2,3},{3,2},{4,5},{5,4},{6,7},{7,6},{8,9},{9,8},{10,11... | collective-permute-start | bytes 786440 | tf_op jit(solution)/shard_map/cond/branch_3_fun/ppermute | solution.py:274
  46.9 5.1 %collective-permute-start.89 = (bf16[128,1024]{1,0:T(8,128)(2,1)S(1)}, bf16[128,1024]{1,0:T(8,128)(2,1)}, u32[]{:S(2)}, u32[]{:S(2)}) collective-permute-start(bf16[128,1024]{1,0:T(8,128)(2,1)S(1)} %collective-permute-done.88.refs_18_.refs_19_), channel_id=1, source_target_pairs={{0,1},{1,0},{2,3},{3,2},{4,5},{5,4},{6,7},{7,6},{8,9},{9,8},{10,11... | collective-permute-start | bytes 786440 | tf_op jit(solution)/shard_map/cond/branch_3_fun/ppermute | solution.py:274
  47.4 11.6 %collective-permute-start.90 = (bf16[128,1024]{1,0:T(8,128)(2,1)S(1)}, bf16[128,1024]{1,0:T(8,128)(2,1)}, u32[]{:S(2)}, u32[]{:S(2)}) collective-permute-start(bf16[128,1024]{1,0:T(8,128)(2,1)S(1)} %collective-permute-done.75.refs_4_.refs_21_), channel_id=1, source_target_pairs={{0,1},{1,0},{2,3},{3,2},{4,5},{5,4},{6,7},{7,6},{8,9},{9,8},{10,11... | collective-permute-start | bytes 786440 | tf_op jit(solution)/shard_map/cond/branch_3_fun/ppermute | solution.py:274
  52.0 12.8 %collective-permute-start.77 = (bf16[128,1024]{1,0:T(8,128)(2,1)S(1)}, bf16[128,1024]{1,0:T(8,128)(2,1)S(1)}, u32[]{:S(2)}, u32[]{:S(2)}) collective-permute-start(bf16[128,1024]{1,0:T(8,128)(2,1)S(1)} %collective-permute-done.76.refs_5_), channel_id=1, source_target_pairs={{0,1},{1,0},{2,3},{3,2},{4,5},{5,4},{6,7},{7,6},{8,9},{9,8},{10,11... | collective-permute-start | bytes 786440 | tf_op jit(solution)/shard_map/cond/branch_3_fun/ppermute | solution.py:274
  52.0 0.6 copy-start.4
  67.8 0.6 copy-start.7
  68.4 3.5 %collective-permute-start.91 = (f32[1,128]{1,0:T(1,128)S(1)}, f32[1,128]{1,0:T(1,128)S(1)}, u32[]{:S(2)}, u32[]{:S(2)}) collective-permute-start(f32[1,128]{1,0:T(1,128)S(1)} %get-tuple-element.129), channel_id=1, source_target_pairs={{0,12},{4,0},{8,4},{12,8},{1,13},{5,1},{9,5},{13,9},{2,14},{6,2},{... | collective-permute-start | bytes 1544 | tf_op jit(solution)/shard_map/cond/branch_3_fun/ppermute | solution.py:270
  68.4 5.3 %collective-permute-start.92 = (f32[1,128]{1,0:T(1,128)S(1)}, f32[1,128]{1,0:T(1,128)S(1)}, u32[]{:S(2)}, u32[]{:S(2)}) collective-permute-start(f32[1,128]{1,0:T(1,128)S(1)} %get-tuple-element.130), channel_id=1, source_target_pairs={{0,4},{4,8},{8,12},{12,0},{1,5},{5,9},{9,13},{13,1},{2,6},{6,10},{... | collective-permute-start | bytes 1544 | tf_op jit(solution)/shard_map/cond/branch_3_fun/ppermute | solution.py:270
  70.4 4.4 %collective-permute-start.93 = (f32[1,128]{1,0:T(1,128)S(1)}, f32[1,128]{1,0:T(1,128)S(1)}, u32[]{:S(2)}, u32[]{:S(2)}) collective-permute-start(f32[1,128]{1,0:T(1,128)S(1)} %get-tuple-element.131), channel_id=1, source_target_pairs={{0,8},{4,12},{8,0},{12,4},{1,9},{5,13},{9,1},{13,5},{2,10},{6,14},... | collective-permute-start | bytes 1544 | tf_op jit(solution)/shard_map/cond/branch_3_fun/ppermute | solution.py:270
  71.9 2.9 %copy-start.22 = (f32[1,128]{1,0:T(1,128)}, f32[1,128]{1,0:T(1,128)S(1)}, u32[]{:S(2)}) copy-start(f32[1,128]{1,0:T(1,128)S(1)} %collective-permute-done.91.refs_1_) | copy-start | bytes 1540 | tf_op jit(solution)/shard_map/cond
  73.7 1.1 %copy-start.23 = (f32[1,128]{1,0:T(1,128)}, f32[1,128]{1,0:T(1,128)S(1)}, u32[]{:S(2)}) copy-start(f32[1,128]{1,0:T(1,128)S(1)} %collective-permute-done.92.refs_2_) | copy-start | bytes 1540 | tf_op jit(solution)/shard_map/cond
  74.8 0.6 copy-start.24
  76.4 0.6 copy-start.15
where the time goes:
time: 77.3 us; the launch traced here: 77 us
  waiting for transfers between devices  33.1 us (43%)
  Pallas kernels  20.4 us (26%)
  starting transfers between devices  19.8 us (26%)
  local copies, waits for them, and re-layouts  2.33 us (3%)
    ppermute x15, waiting for transfers between devices, swap_with(): return lax.ppermute(array, 'sub', [(i, i ^ q) for i in range(pieces)])  20.6 us
    pallas_call x3, Pallas kernels, score(): pl.pallas_call(functools.partial(score_kernel, blocks, rows, width, piece...  15.1 us
    ppermute x9, waiting for transfers between devices, shift_by(): lax.ppermute(array, 'blk', [(i, (i + k) % places) for i in range(places)])  12.5 us
    ppermute x9, starting transfers between devices, shift_by(): lax.ppermute(array, 'blk', [(i, (i + k) % places) for i in range(places)])  11.9 us
    ppermute x15, starting transfers between devices, swap_with(): return lax.ppermute(array, 'sub', [(i, i ^ q) for i in range(pieces)])  7.92 us
    pallas_call x1, Pallas kernels, make_plan(): pl.pallas_call(functools.partial(plan_kernel, patterns, places, capacity)...  3.37 us
    cond x16, local copies, waits for them, and re-layouts  1.75 us
  transfers between devices with their start and end apart: 24, of which 9 were waited for; matrix products, arithmetic and copies ran while one was open for 0% of the time, Pallas kernels for 17%

commit v1 on v0

v1 whole, which is shorter than its diff:
```python
import functools
import itertools
import math

import jax
import jax.numpy as jnp
from jax import lax
from jax.experimental import pallas as pl
from jax.experimental.pallas import tpu as pltpu
from jax.sharding import PartitionSpec as P

kernel_scale = 24.0
norm_eps = 1e-06
LANES = 128
FLOPS = 4
UNUSED = 2.0 ** 60
UNUSED_SQUARES = 2.0 ** 100
SCALE_IN_USE = 2.0 ** -30
VMEM_LIMIT = 24 * 1024 * 1024
ANY = pl.BlockSpec(memory_space=pl.ANY)
SMEM = pl.BlockSpec(memory_space=pltpu.SMEM)
VMEM = pl.BlockSpec(memory_space=pltpu.VMEM)


def block_patterns(places, capacity, blocks):
    if capacity < 2 or places > 4:
        return []
    cost = lambda counts: sum(c * min(k, places - k) for k, c in enumerate(counts))
    best = {}
    for counts in itertools.product(range(capacity + 1), repeat=places):
        if sum(counts) != blocks:
            continue
        turns = [counts[t:] + counts[:t] for t in range(places)]
        pick = min(turns, key=lambda c: (cost(c), c))
        best[min(turns)] = pick
    return sorted(best.values(), key=cost)


def unary(counts):
    return sum(((1 << c) - 1) << (2 * r) for r, c in enumerate(counts))


def marked(first_lanes, sub, count):
    rows, lanes = first_lanes.shape
    row = lax.broadcasted_iota(jnp.int32, (rows, lanes), 0) + sub * rows
    lane = lax.broadcasted_iota(jnp.int32, (rows, lanes), 1)
    return jnp.where((row >= count) & (lane == 0), UNUSED, first_lanes.astype(jnp.float32)).astype(first_lanes.dtype)


def plan_kernel(patterns, places, capacity, me_ref, sub_ref, fetch_ref, count_ref, left_ref, right_ref, pairs_ref,
                emb_ref, plan_ref, bits_ref, *rest):
    slots, sems = rest[:-1], rest[-1]
    blocks = count_ref.shape[0]
    rows = emb_ref.shape[1]
    views = [slots[0].at[pl.ds(j * rows, rows)] for j in range(capacity)] + list(slots[1:])
    me = me_ref[0]
    used = jnp.int32(0)
    for s in range(places):
        seen = jnp.int32(0)
        for p in range(blocks):
            owner = lax.div(fetch_ref[s, p], blocks)
            bit = lax.shift_left(jnp.int32(1), 2 * lax.rem(owner + (places - s), places))
            seen = seen | bit | ((seen & bit) << 1)
        used = used | seen
    choice = jnp.int32(len(patterns))
    shift = jnp.int32(0)
    for m in reversed(range(len(patterns))):
        for t in range(places):
            allowed = unary([patterns[m][(t - r) % places] for r in range(places)])
            fits = (used & ~allowed) == 0
            choice = jnp.where(fits, m, choice)
            shift = jnp.where(fits, t, shift)
    plan_ref[0] = choice
    plan_ref[1] = shift
    mine = lax.rem(me + places - shift, places)
    total = places * capacity
    copies = []
    for k in range(places):
        owner = lax.rem(me + places - k, places)
        target = lax.rem(me + k + places - shift, places)
        place, lid, seen = [jnp.int32(0)] * capacity, [jnp.int32(0)] * capacity, jnp.int32(0)
        send, sent = [jnp.int32(0)] * capacity, jnp.int32(0)
        for p in range(blocks):
            listed = fetch_ref[mine, p]
            hit = lax.div(listed, blocks) == owner
            outward = fetch_ref[target, p]
            goes = lax.div(outward, blocks) == me
            for j in range(capacity):
                place[j] = jnp.where(hit & (seen == j), p, place[j])
                lid[j] = jnp.where(hit & (seen == j), listed - owner * blocks, lid[j])
                send[j] = jnp.where(goes & (sent == j), outward - me * blocks, send[j])
            seen = seen + hit.astype(jnp.int32)
            sent = sent + goes.astype(jnp.int32)
        for j in range(capacity):
            at = k * capacity + j
            copy = pltpu.make_async_copy(emb_ref.at[send[j]], views[at], sems.at[at])
            pl.when(sent > j)(copy.start)
            copies.append((sent > j, copy))
            plan_ref[2 + at] = send[j]
            plan_ref[2 + total + at] = place[j]
            plan_ref[2 + 2 * total + at] = lid[j]
    bits = jnp.int32(0)
    for p in range(left_ref.shape[1]):
        a, b = left_ref[0, p], right_ref[0, p]
        both = lax.shift_left(jnp.int32(1), a * blocks + b) | lax.shift_left(jnp.int32(1), b * blocks + a)
        bits = bits | jnp.where(p < pairs_ref[0], both, 0)
    bits_ref[0] = bits
    for at, (filled, copy) in enumerate(copies):
        pl.when(filled)(copy.wait)
        views[at][:, :LANES] = marked(views[at][:, :LANES], sub_ref[0], count_ref[plan_ref[2 + at]])


def make_plan(patterns, places, capacity, me, sub, embeddings, row_count, fetch_list, left, right, pairs):
    blocks, rows, width = embeddings.shape
    total = places * capacity
    slot = jax.ShapeDtypeStruct((rows, width), embeddings.dtype)
    own = jax.ShapeDtypeStruct((capacity * rows, width), embeddings.dtype)
    others = total - capacity
    out = pl.pallas_call(
        functools.partial(plan_kernel, patterns, places, capacity),
        out_shape=[jax.ShapeDtypeStruct((2 + 3 * total,), jnp.int32),
                   jax.ShapeDtypeStruct((1,), jnp.int32), own] + [slot] * others,
        in_specs=[SMEM] * 7 + [ANY],
        out_specs=[SMEM, SMEM] + [VMEM] * (1 + others),
        scratch_shapes=[pltpu.SemaphoreType.DMA((total,))],
        name="plan_and_gather",
    )(me, sub, fetch_list, row_count, left, right, pairs, embeddings)
    return out[0], out[1], out[2], out[3:]


def pairs_of(per, runs, steps):
    return [(a, b) for lo, hi, start, end in steps
            for b in sorted({runs[run] // per for run in range(start, end)}) for a in range(lo, hi)]


def score_kernel(rows, width, pieces, wheres, owned, runs, steps, places, *refs):
    refs = list(refs)
    arrays = [refs.pop(0) for _ in range(1 + max(i for i, _ in wheres))]
    spots_in = [arrays[i].at[pl.ds(n * rows, rows)] for i, n in wheres]
    left_in, right_in = spots_in[:len(owned)], spots_in[len(owned):]
    finish = None
    if places is not None:
        finish = [refs.pop(0) for _ in range(2 + places[0])]
    out_refs = [refs.pop(0) for _ in (places[2] if places else (0,))]
    left, right, left_scale, gram, left_sems, right_sems = refs[:6]
    sums = refs[6] if places else out_refs[0]
    per = pieces // 2
    copies = []
    for i, a in enumerate(owned):
        copies.append(pltpu.make_async_copy(left_in[i], left.at[pl.ds(a * rows, rows)], left_sems.at[i]))
    for i in range(2 * len(runs)):
        copies.append(pltpu.make_async_copy(right_in[i], right.at[pl.ds(i * rows, rows)], right_sems.at[i]))
    for copy in copies:
        copy.start()
    eye = lax.broadcasted_iota(jnp.int32, (rows, rows), 0) == lax.broadcasted_iota(jnp.int32, (rows, rows), 1)

    def squares(block):
        wide = block.astype(jnp.float32)
        return jnp.sum(wide * wide, axis=1, keepdims=True)

    def lanes(col):
        return jnp.sum(jnp.where(eye, col, 0.0), axis=0, keepdims=True)

    for i in range(len(owned)):
        copies[i].wait()

    @pl.loop(0, len(owned))
    def _(i):
        here = pl.ds((owned[0] + i) * rows, rows)
        inv = lax.rsqrt(squares(left[here, :]) * (1.0 / width) + norm_eps)
        left_scale[here, :] = jnp.broadcast_to(inv * (kernel_scale / width * math.log2(math.e)), (rows, rows))

    arrived = base = 0
    for lo, hi, start, end in steps:
        fresh = end > arrived
        first_block = runs[start] // per

        @pl.loop(start, end)
        def _(run):
            if fresh:
                for h in range(2):
                    pltpu.make_async_copy(
                        right_in[0], right.at[pl.ds((2 * run + h) * rows, rows)], right_sems.at[2 * run + h]).wait()
            flat = runs[0] + run
            b = lax.div(flat, per)
            q = 2 * lax.rem(flat, per)
            scale_row, valid = [], []
            for h in range(2):
                here = pl.ds(pl.multiple_of((2 * run + h) * rows, rows), rows)
                total = lanes(squares(right[here, :]))
                scale_row.append(lax.rsqrt(total * (1.0 / width) + norm_eps))
                valid.append((total < UNUSED_SQUARES).astype(jnp.float32))
            both = right[pl.ds(pl.multiple_of(2 * run * rows, rows), 2 * rows), :]
            gram[:(hi - lo) * rows, :] = lax.dot_general(
                left[lo * rows:hi * rows, :], both, (((1,), (1,)), ((), ())), preferred_element_type=jnp.float32)
            for a in range(lo, hi):
                there = slice((a - lo) * rows, (a - lo + 1) * rows)
                scale = left_scale[a * rows:(a + 1) * rows, :]
                same = eye & ((b == a) & (q == 0))
                near = jnp.exp2(gram[there, :rows] * scale * scale_row[0]) * valid[0]
                far = jnp.exp2(gram[there, rows:] * scale * scale_row[1]) * valid[1]
                tile = jnp.where(same, 0.0, near) + far
                pair = base + (b - first_block) * (hi - lo) + a - lo
                if end - start > 1:
                    tile = tile + jnp.where(q == 0, 0.0, sums[pair])
                sums[pair] = tile

        arrived = max(arrived, end)
        base += (runs[end - 1] // per + 1 - first_block) * (hi - lo)
    if places is None:
        return
    count, spots, groups, listed = places
    plan_ref, bits_ref = finish[:2]
    bits = bits_ref[0]
    spot = [plan_ref[at] for at in spots]
    blocks = len(spots)
    for ref, group in zip(out_refs, groups):
        for n, a in enumerate(group):
            total = jnp.zeros((rows, rows), jnp.float32)
            for source, at, right_block in listed[a]:
                paired = (bits >> (spot[a] * blocks + spot[right_block])) & 1
                total = total + (sums if source < 0 else finish[2 + source])[at] * paired.astype(jnp.float32)
            total = jnp.sum(total, axis=1, keepdims=True)
            total = jnp.where(left_scale[a * rows:(a + 1) * rows, :1] > SCALE_IN_USE, total, 0.0)
            ref[n:n + 1, :] = jnp.log1p(lanes(total) / (pieces * rows))


def score(pieces, held, owned, runs, steps, meta=None, name="score"):
    width = held[owned[0], 0][0].shape[1]
    rows = held[owned[0], 0][2]
    per = pieces // 2
    rights = [held[run // per, 2 * (run % per) + h] for run in runs for h in range(2)]
    arrays, wheres = [], []
    for array, n, _ in [held[a, 0] for a in owned] + rights:
        known = [i for i, other in enumerate(arrays) if other is array]
        if not known:
            arrays.append(array)
        wheres.append((known[0] if known else len(arrays) - 1, n))
    tall = max(hi - lo for lo, hi, _, _ in steps) * rows
    pairs = pairs_of(per, runs, steps)
    sums = jax.ShapeDtypeStruct((len(pairs), rows, rows), jnp.float32)
    places, extra, extra_specs, out_shape, scratch = None, [], [], [sums], []
    if meta is not None:
        plan, spots, bits, groups, earlier = meta
        listed = [[] for _ in spots]
        for source, (_, known) in enumerate(earlier + [(None, pairs)]):
            for at, (a, b) in enumerate(known):
                listed[a].append((source if source < len(earlier) else -1, at, b))
        places = len(earlier), spots, groups, listed
        extra = [plan, bits] + [array for array, _ in earlier]
        extra_specs = [SMEM, SMEM] + [VMEM] * len(earlier)
        out_shape = [jax.ShapeDtypeStruct((len(g), rows), jnp.float32) for g in groups]
        scratch = [pltpu.VMEM(sums.shape, jnp.float32)]
    flops = sum(4 * (hi - lo) * (end - start) * rows * rows * width for lo, hi, start, end in steps)
    moved = (len(owned) + len(rights)) * rows * width * 2
    result = pl.pallas_call(
        functools.partial(score_kernel, rows, width, pieces, wheres, owned, runs, steps, places),
        out_shape=out_shape,
        in_specs=[ANY] * len(arrays) + extra_specs,
        out_specs=[VMEM] * len(out_shape),
        scratch_shapes=[
            pltpu.VMEM((owned[-1] * rows + rows, width), jnp.bfloat16),
            pltpu.VMEM((len(rights) * rows, width), jnp.bfloat16),
            pltpu.VMEM((owned[-1] * rows + rows, rows), jnp.float32),
            pltpu.VMEM((tall, 2 * rows), jnp.float32),
            pltpu.SemaphoreType.DMA((len(owned),)),
            pltpu.SemaphoreType.DMA((len(rights),)),
        ] + scratch,
        compiler_params=pltpu.CompilerParams(vmem_limit_bytes=VMEM_LIMIT),
        cost_estimate=pl.CostEstimate(flops=FLOPS * flops, bytes_accessed=moved, transcendentals=0),
        name=name,
    )(*arrays, *extra)
    return (result[0], pairs) if meta is None else result


def place_kernel(slots, plan_ref, *refs):
    out_ref = refs[-1]
    for ref, (group) in zip(refs[:-1], slots):
        for n, at in enumerate(group):
            out_ref[pl.ds(plan_ref[2 + at], 1), :] = ref[n:n + 1, :]


def place_rows(slots, plan, returned, blocks, rows):
    return pl.pallas_call(
        functools.partial(place_kernel, slots),
        out_shape=jax.ShapeDtypeStruct((blocks, rows), jnp.float32),
        in_specs=[SMEM] + [VMEM] * len(returned),
        out_specs=VMEM,
        name="place_rows",
    )(plan, *returned)


def shift_by(array, k, places):
    return lax.ppermute(array, "blk", [(i, (i + k) % places) for i in range(places)])


def swap_with(array, q, pieces):
    return lax.ppermute(array, "sub", [(i, i ^ q) for i in range(pieces)])


def after(array, *others):
    return lax.optimization_barrier((array,) + others)[0]


def pattern_path(counts, capacity, pieces, rows, plan, bits, own, slots):
    places = len(counts)
    nearest = sorted((k for k in range(1, places) if counts[k]), key=lambda k: min(k, places - k))
    sets = [[(0, j) for j in range(counts[0])], [(k, 0) for k in nearest[:2]],
            [(k, 0) for k in nearest[2:]] + [(k, 1) for k in nearest if counts[k] > 1]]
    taken = [(k, k * capacity + j) for group in sets for k, j in group]
    blocks = len(taken)
    per = pieces // 2
    sends = [lambda x: x] + [functools.partial(shift_by, k=k, places=places) for k in range(1, places)]
    moved = [shift_by(slots[at - capacity], k, places) for k, at in taken if k]
    here = lax.switch(plan[1], sends, after(bits, moved[0]))
    arrived = [own if len(sets[0]) == capacity else own[:rows], jnp.concatenate(moved[:2], axis=0),
               moved[2] if len(moved) == 3 else jnp.concatenate(moved[2:], axis=0)]
    held = {}
    first = [0, len(sets[0]), len(sets[0]) + 2, blocks]
    ready, end = first[1], first[2]
    for g, array in enumerate(arrived):
        across = swap_with(array, 2, pieces)
        beside = swap_with(array, 1, pieces)
        if g == 2:
            near = score(pieces, held, range(end), range(ready * per, end * per), [(0, end, 0, (end - ready) * per)],
                         name="score_near")
        for n, b in enumerate(range(first[g], first[g + 1])):
            held[b, 0], held[b, 1], held[b, 2] = (array, n, rows), (beside, n, rows), (across, n, rows)
        if g == 1:
            early = score(pieces, held, range(end), range(ready * per), [(0, end, 0, ready * per)], name="score_early")
        if g == 2:
            steps = [(end, blocks, 0, end * per)]
            runs = range(end * per)
            if blocks - end == 1:
                runs = range(end * per + per - 1)
                steps.append((0, blocks, end * per, len(runs)))
            far = score(pieces, held, range(blocks), runs, steps, name="score_far")
            across = after(across, early[0], near[0], far[0], here)
        corner = swap_with(across, 1, pieces)
        for n, b in enumerate(range(first[g], first[g + 1])):
            held[b, 3] = (corner, n, rows)
    order = sorted({k for k, _ in taken})
    groups = [[b for b in range(blocks) if taken[b][0] == k] for k in order]
    sums = score(pieces, held, range(blocks), range(len(runs), blocks * per), [(0, blocks, 0, blocks * per - len(runs))],
                 (plan, [2 + places * capacity + at for _, at in taken], here, groups, [early, near, far]), name="score_late")
    returned = [s if k == 0 else shift_by(s, places - k, places) for k, s in zip(order, sums)]
    return place_rows([[taken[b][1] for b in g] for g in groups], plan, returned, blocks, rows)


def general_path(capacity, pieces, embeddings, row_count, fetch_list, left, right, pairs):
    places = lax.axis_size("blk")
    me = lax.axis_index("blk")
    sub = lax.axis_index("sub")
    blocks, rows, width = embeddings.shape
    total = places * capacity
    local_ids = jnp.arange(blocks, dtype=jnp.int32)
    slot_ids = jnp.arange(total, dtype=jnp.int32)
    owned = me * blocks + local_ids
    here = fetch_list[:, :, None] == owned[None, None, :]
    scorer = jnp.sum(jnp.where(here, jnp.arange(places, dtype=jnp.int32)[:, None, None], 0), axis=(0, 1))
    same = scorer[:, None] == scorer[None, :]
    rank = jnp.sum(same & (local_ids[None, :] < local_ids[:, None]), axis=1)
    send_slot = scorer * capacity + rank
    placing = send_slot[:, None] == slot_ids[None, :]
    source = jnp.sum(jnp.where(placing, local_ids[:, None], 0), axis=0)
    exchange = lambda x: lax.all_to_all(x, "blk", split_axis=0, concat_axis=0, tiled=True)
    mark = jax.vmap(lambda block, count: block.at[:, :LANES].set(marked(block[:, :LANES], sub, count)))
    incoming = exchange(jnp.take(mark(embeddings, row_count), source, axis=0))
    wanted = lax.dynamic_index_in_dim(fetch_list, me, 0, keepdims=False)
    owner, local = wanted // blocks, wanted % blocks
    together = owner[:, None] == owner[None, :]
    recv_rank = jnp.sum(together & (local[None, :] < local[:, None]), axis=1)
    recv_slot = owner * capacity + recv_rank
    live = jnp.arange(left.shape[1], dtype=jnp.int32) < pairs[0]
    one = jnp.int32(1)
    hot = lambda at: jnp.where(live[:, None], (at[:, None] == jnp.arange(blocks * blocks)).astype(jnp.int32), 0)
    listed = jnp.max(hot(left[0] * blocks + right[0]) | hot(right[0] * blocks + left[0]), axis=0)
    bits = jnp.sum(listed * lax.shift_left(one, jnp.arange(blocks * blocks, dtype=jnp.int32)))
    held = {}
    for b in range(blocks):
        block = lax.dynamic_index_in_dim(incoming, recv_slot[b], 0, keepdims=False)
        for q in range(pieces):
            held[b, q] = (swap_with(block, q, pieces) if q else block), 0, rows
    runs = range(blocks * pieces // 2)
    meta = local_ids, range(blocks), bits[None].astype(jnp.int32), [list(range(blocks))], []
    (dense,) = score(pieces, held, range(blocks), runs, [(0, blocks, 0, len(runs))], meta, name="score_all")
    back = (recv_slot[None, :] == slot_ids[:, None]).astype(jnp.float32)
    returned = exchange(jnp.sum(back[:, :, None] * dense[None, :, :], axis=1))
    return jnp.take(returned, send_slot, axis=0)


def body(embeddings, row_count, fetch_list, pair_left, pair_right, pair_count):
    places = lax.axis_size("blk")
    pieces = lax.axis_size("sub")
    blocks = embeddings.shape[0]
    capacity = (blocks + places - 1) // places
    given = (embeddings, row_count, fetch_list, pair_left, pair_right, pair_count)
    general = functools.partial(general_path, capacity, pieces)
    patterns = block_patterns(places, capacity, blocks)
    if not patterns or pieces != 4:
        return general(*given)
    me = lax.axis_index("blk").astype(jnp.int32)[None]
    sub = lax.axis_index("sub").astype(jnp.int32)[None]
    plan, bits, own, slots = make_plan(patterns, places, capacity, me, sub, *given)
    rows = embeddings.shape[1]
    branches = [
        lambda plan, bits, own, slots, given, counts=counts: pattern_path(counts, capacity, pieces, rows, plan, bits, own, slots)
        for counts in patterns
    ] + [lambda plan, bits, own, slots, given: general(*given)]
    return lax.switch(plan[0], branches, plan, bits, own, slots, given)


def solution(mesh):
    in_specs = (
        P(("parts", "blk"), "sub", None),
        P(("parts", "blk")),
        P("parts", None),
        P(("parts", "blk"), None),
        P(("parts", "blk"), None),
        P(("parts", "blk")),
    )
    out_specs = P(("parts", "blk"), "sub")
    return jax.shard_map(body, mesh=mesh, in_specs=in_specs, out_specs=out_specs, check_vma=False)
```

time: 77.3 us -> 66.1 us (0.86); the launches traced: 77 us -> 66.6 us
  waiting for transfers between devices: 33.1 us -> 26.1 us
  Pallas kernels: 20.4 us -> 16.7 us
  starting transfers between devices: 19.8 us -> 16.8 us
  loops' own time: 0.65 us -> 2.5 us
  local copies, waits for them, and re-layouts: 2.33 us -> 3.74 us
    ppermute x15 -> x9, waiting for transfers between devices: 20.6 us -> 5.13 us  [swap_with(): return lax.ppermute(array, 'sub', [(i, i ^ q) for i in range(pieces)])]
    ppermute x9 -> x7, waiting for transfers between devices: 12.5 us -> 21 us  [shift_by(): lax.ppermute(array, 'blk', [(i, (i + k) % places) for i in range(places)])]
    ppermute x15 -> x9, starting transfers between devices: 7.92 us -> 4.4 us  [swap_with(): return lax.ppermute(array, 'sub', [(i, i ^ q) for i in range(pieces)])]
    pallas_call x4, Pallas kernels: 16.4 us -> 13.7 us  [score(): pl.pallas_call(functools.partial(score_kernel, rows, width, pieces, where...]
    another operation x1 -> x2, loops' own time: 0.65 us -> 2.5 us  [the longest x1 1.32 us: body(): return lax.switch(plan[0], branches, plan, bits, own, slots, given)]
    unnamed x2 -> x11, local copies, waits for them, and re-layouts: 0.59 us -> 1.97 us
    pallas_call x1, Pallas kernels: 3.37 us -> 2.34 us  [make_plan(): pl.pallas_call(functools.partial(plan_kernel, patterns, places, capacity)...]
    ppermute x9 -> x7, starting transfers between devices: 11.9 us -> 12.4 us  [shift_by(): lax.ppermute(array, 'blk', [(i, (i + k) % places) for i in range(places)])]
  transfers between devices with their start and end apart: 24 -> 16, of which waited for: 9 -> 9; matrix products, arithmetic and copies ran while one was open for 0% -> 1% of each run, Pallas kernels for 17% -> 16%
where the time goes in v1:
time: 66.1 us; the launch traced here: 66.6 us
  waiting for transfers between devices  26.1 us (39%)
  starting transfers between devices  16.8 us (25%)
  Pallas kernels  16.7 us (25%)
  local copies, waits for them, and re-layouts  3.74 us (6%)
  loops' own time  2.5 us (4%)
  between operations  0.75 us (1%)
    ppermute x7, waiting for transfers between devices, shift_by(): lax.ppermute(array, 'blk', [(i, (i + k) % places) for i in range(places)])  21 us
    pallas_call x4, Pallas kernels, score(): pl.pallas_call(functools.partial(score_kernel, rows, width, pieces, where...  13.7 us
    ppermute x7, starting transfers between devices, shift_by(): lax.ppermute(array, 'blk', [(i, (i + k) % places) for i in range(places)])  12.4 us
    ppermute x9, waiting for transfers between devices, swap_with(): return lax.ppermute(array, 'sub', [(i, i ^ q) for i in range(pieces)])  5.13 us
    ppermute x9, starting transfers between devices, swap_with(): return lax.ppermute(array, 'sub', [(i, i ^ q) for i in range(pieces)])  4.4 us
    pallas_call x1, Pallas kernels, make_plan(): pl.pallas_call(functools.partial(plan_kernel, patterns, places, capacity)...  2.34 us
    unnamed x11, local copies, waits for them, and re-layouts  1.97 us
  transfers between devices with their start and end apart: 16, of which 9 were waited for; matrix products, arithmetic and copies ran while one was open for 1% of the time, Pallas kernels for 16%

profile of v1, /device:TPU:0, one launch (start us, length us, event | category | flops | bytes accessed | tf_op | source)
XLA Modules:
  0.0 66.6 jit_solution(3149550752923796157)
XLA Ops:
  0.0 0.0 copy-start.6
  0.0 0.0 copy-start.4
  0.0 0.0 copy-start.7
  0.0 0.0 copy-start.8
  0.0 1.4 %copy.42.emb_ref = bf16[5,128,1024]{2,1,0:T(8,128)(2,1)S(1)} copy(bf16[5,128,1024]{2,1,0:T(8,128)(2,1)} %param.29) | data formatting | bytes 2621440
  2.0 0.0 copy-done.6
  2.0 0.0 copy-done.4
  2.1 0.0 copy-done.7
  2.1 0.0 copy-done.8
  2.1 2.3 %plan_and_gather.1 = (s32[26]{0:T(128)S(1)}, s32[1]{0:T(128)}, bf16[256,1024]{1,0:T(8,128)(2,1)S(1)}, bf16[128,1024]{1,0:T(8,128)(2,1)S(1)}, bf16[128,1024]{1,0:...) custom-call(s32[1]{0:T(128)} %bitcast.31.me_ref, ...), custom_call_target="tpu_custom_call" | custom-call | tf_op jit(solution)/shard_map/plan_and_gather/pallas_call | solution.py:119
  4.5 61.6 %conditional.5 = (f32[5,128]{1,0:T(8,128)S(1)}) conditional(s32[]{:T(128)} %bitcast.33, (bf16[128,1024]{1,0:T(8,128)(2,1)S(1)}, bf16[128,1024]{1,0:T(8,128)(2,1)S(1)}, bf16[128,1024]{1,0:T(8,128)(2,1)}, bf16[256,1024]{1,0:T(8,128)(2,1)S(1)}, s32[26]{0:T(128)S(1)}, /*index=5*/s32[1]{0:T(128)}) %tuple.80, ...), branch_computations={%region_0.0_spmd, %region_5.0_spmd, %region_10.0_spmd, %region_15.... | conditional | flops 13423247360 | bytes 39954096 | solution.py:410
  4.7 3.1 %collective-permute-start.55 = (bf16[128,1024]{1,0:T(8,128)(2,1)S(1)}, bf16[128,1024]{1,0:T(8,128)(2,1)S(1)}, u32[]{:S(2)}, u32[]{:S(2)}) collective-permute-start(bf16[128,1024]{1,0:T(8,128)(2,1)S(1)} %get-tuple-element.157), channel_id=1, source_target_pairs={{0,4},{4,8},{8,12},{12,0},{1,5},{5,9},{9,13},{13,1},{2,6},{6,10},{... | collective-permute-start | bytes 786440 | tf_op jit(solution)/shard_map/cond/branch_3_fun/ppermute | solution.py:294
  7.8 1.5 %collective-permute-start.60 = (bf16[256,1024]{1,0:T(8,128)(2,1)S(1)}, bf16[256,1024]{1,0:T(8,128)(2,1)S(1)}, u32[]{:S(2)}, u32[]{:S(2)}) collective-permute-start(bf16[256,1024]{1,0:T(8,128)(2,1)S(1)} %get-tuple-element.156.refs_0_), channel_id=1, source_target_pairs={{0,2},{1,3},{2,0},{3,1},{4,6},{5,7},{6,4},{7,5},{8,10},{9,11},{10,... | collective-permute-start | bytes 1572872 | tf_op jit(solution)/shard_map/cond/branch_3_fun/ppermute | solution.py:298
  9.3 2.2 %collective-permute-start.56 = (bf16[128,1024]{1,0:T(8,128)(2,1)S(1)}, bf16[128,1024]{1,0:T(8,128)(2,1)S(1)}, u32[]{:S(2)}, u32[]{:S(2)}) collective-permute-start(bf16[128,1024]{1,0:T(8,128)(2,1)S(1)} %get-tuple-element.158), channel_id=1, source_target_pairs={{0,12},{4,0},{8,4},{12,8},{1,13},{5,1},{9,5},{13,9},{2,14},{6,2},{... | collective-permute-start | bytes 786440 | tf_op jit(solution)/shard_map/cond/branch_3_fun/ppermute | solution.py:294
  11.5 5.5 %collective-permute-done.55 = bf16[128,1024]{1,0:T(8,128)(2,1)S(1)} collective-permute-done((bf16[128,1024]{1,0:T(8,128)(2,1)S(1)}, bf16[128,1024]{1,0:T(8,128)(2,1)S(1)}, u32[]{:S(2)}, u32[]{:S(2)}) %collective-permute-start.55) | collective-permute-done | bytes 262176 | tf_op jit(solution)/shard_map/cond/branch_3_fun/ppermute | solution.py:294
  17.0 4.7 %collective-permute-done.56 = bf16[128,1024]{1,0:T(8,128)(2,1)S(1)} collective-permute-done((bf16[128,1024]{1,0:T(8,128)(2,1)S(1)}, bf16[128,1024]{1,0:T(8,128)(2,1)S(1)}, u32[]{:S(2)}, u32[]{:S(2)}) %collective-permute-start.56) | collective-permute-done | bytes 262176 | tf_op jit(solution)/shard_map/cond/branch_3_fun/ppermute | solution.py:294
  21.8 1.2 %collective-permute-start.63 = (bf16[256,1024]{1,0:T(8,128)(2,1)S(1)}, bf16[256,1024]{1,0:T(8,128)(2,1)S(1)}, u32[]{:S(2)}, u32[]{:S(2)}) collective-permute-start(bf16[256,1024]{1,0:T(8,128)(2,1)S(1)} %constant_dynamic-update-slice_fusion.8.refs_1_), channel_id=1, source_target_pairs={{0,2},{1,3},{2,0},{3,1},{4,6},{5,7},{6,4},{7,5},{8,10},{9,11},{10,... | collective-permute-start | bytes 1572872 | tf_op jit(solution)/shard_map/cond/branch_3_fun/ppermute | solution.py:298
  23.0 0.0 collective-permute-start.59
  23.0 0.0 collective-permute-done.60.refs_3_.refs_4_
  23.0 0.5 collective-permute-start.61
  23.5 1.1 %collective-permute-start.57 = (bf16[128,1024]{1,0:T(8,128)(2,1)}, bf16[128,1024]{1,0:T(8,128)(2,1)S(1)}, u32[]{:S(2)}, u32[]{:S(2)}) collective-permute-start(bf16[128,1024]{1,0:T(8,128)(2,1)} %get-tuple-element.159), channel_id=1, source_target_pairs={{0,8},{4,12},{8,0},{12,4},{1,9},{5,13},{9,1},{13,5},{2,10},{6,14},... | collective-permute-start | bytes 786440 | tf_op jit(solution)/shard_map/cond/branch_3_fun/ppermute | solution.py:294
  24.6 0.6 slice.50
  25.8 6.0 %conditional.3 = (s32[1]{0:T(128)}) conditional(s32[]{:T(128)} %bitcast.3, s32[1]{0:T(128)} %get-tuple-element.161, s32[1]{0:T(128)} %get-tuple-element.161, s32[1]{0:T(128)} %get-tuple-element.161, s32[1]{0:T(128)} %get-tuple-element.161), branch_computations={%region_16.0_spmd, %region_17.0_spmd, %region_18.0_spmd, %region_1... | conditional | bytes 72 | solution.py:315
  25.9 2.2 %collective-permute-start.11 = (s32[1]{0:T(128)}, s32[1]{0:T(128)}, u32[]{:S(2)}, u32[]{:S(2)}) collective-permute-start(s32[1]{0:T(128)} %param.20), channel_id=1, source_target_pairs={{0,12},{4,0},{8,4},{12,8},{1,13},{5,1},{9,5},{13,9},{2,14},{6,2},{... | collective-permute-start | bytes 20 | tf_op jit(solution)/shard_map/cond/branch_3_fun/cond/branch_3_fun/ppermute | solution.py:294
  28.1 2.6 %collective-permute-done.11 = s32[1]{0:T(128)} collective-permute-done((s32[1]{0:T(128)}, s32[1]{0:T(128)}, u32[]{:S(2)}, u32[]{:S(2)}) %collective-permute-start.11) | collective-permute-done | bytes 36 | tf_op jit(solution)/shard_map/cond/branch_3_fun/cond/branch_3_fun/ppermute | solution.py:294
  31.9 0.0 collective-permute-start.62
  31.9 3.8 %collective-permute-done.63.refs_3_.refs_7_ = bf16[256,1024]{1,0:T(8,128)(2,1)S(1)} collective-permute-done((bf16[256,1024]{1,0:T(8,128)(2,1)S(1)}, bf16[256,1024]{1,0:T(8,128)(2,1)S(1)}, u32[]{:S(2)}, u32[]{:S(2)}) %collective-permute-start.63) | collective-permute-done | bytes 524320 | tf_op jit(solution)/shard_map/cond/branch_3_fun/ppermute | solution.py:298
  35.7 0.0 collective-permute-start.64
  35.7 2.8 %collective-permute-done.57.refs_2_ = bf16[128,1024]{1,0:T(8,128)(2,1)S(1)} collective-permute-done((bf16[128,1024]{1,0:T(8,128)(2,1)}, bf16[128,1024]{1,0:T(8,128)(2,1)S(1)}, u32[]{:S(2)}, u32[]{:S(2)}) %collective-permute-start.57) | collective-permute-done | bytes 262176 | tf_op jit(solution)/shard_map/cond/branch_3_fun/ppermute | solution.py:294
  38.5 0.0 collective-permute-start.65
  38.5 0.0 collective-permute-done.59.refs_2_.refs_3_
  38.5 0.9 %collective-permute-start.58 = (bf16[128,1024]{1,0:T(8,128)(2,1)S(1)}, bf16[128,1024]{1,0:T(8,128)(2,1)S(1)}, u32[]{:S(2)}, u32[]{:S(2)}) collective-permute-start(bf16[128,1024]{1,0:T(8,128)(2,1)S(1)} %collective-permute-done.57.refs_2_), channel_id=1, source_target_pairs={{0,2},{1,3},{2,0},{3,1},{4,6},{5,7},{6,4},{7,5},{8,10},{9,11},{10,... | collective-permute-start | bytes 786440 | tf_op jit(solution)/shard_map/cond/branch_3_fun/ppermute | solution.py:298
  39.3 0.0 collective-permute-done.61.refs_4_.refs_5_
  39.3 2.9 %score_early.7.refs_7_ = f32[8,128,128]{2,1,0:T(8,128)S(1)} custom-call(bf16[256,1024]{1,0:T(8,128)(2,1)S(1)} %get-tuple-element.156.refs_0_, bf16[256,1024]{1,0:T(8,128)(2,1)S(1)} %constant_dynamic-update-slice_fusion.8.refs_1_, bf16[256,1024]{1,0:T(8,128)(2,1)S(1)} %collective-permute-done.59.refs_2_.refs_3_, ...), custom_call_target="tpu_custom_call" | custom-call | flops 4294967296 | bytes 3145728 | tf_op jit(solution)/shard_map/cond/branch_3_fun/score_early/pallas_call | solution.py:256
  42.2 0.0 collective-permute-done.62.refs_2_.refs_6_
  42.2 0.0 collective-permute-done.64.refs_4_.refs_8_
  42.2 2.9 %score_near.7.refs_8_ = f32[8,128,128]{2,1,0:T(8,128)S(1)} custom-call(bf16[256,1024]{1,0:T(8,128)(2,1)S(1)} %get-tuple-element.156.refs_0_, bf16[256,1024]{1,0:T(8,128)(2,1)S(1)} %constant_dynamic-update-slice_fusion.8.refs_1_, bf16[256,1024]{1,0:T(8,128)(2,1)S(1)} %collective-permute-done.62.refs_2_.refs_6_, ...), custom_call_target="tpu_custom_call" | custom-call | flops 4294967296 | bytes 3145728 | tf_op jit(solution)/shard_map/cond/branch_3_fun/score_near/pallas_call | solution.py:256
  45.1 0.0 collective-permute-done.65.refs_9_
  45.1 4.6 %score_far.7.refs_9_ = f32[9,128,128]{2,1,0:T(8,128)S(1)} custom-call(bf16[256,1024]{1,0:T(8,128)(2,1)S(1)} %get-tuple-element.156.refs_0_, bf16[256,1024]{1,0:T(8,128)(2,1)S(1)} %constant_dynamic-update-slice_fusion.8.refs_1_, bf16[128,1024]{1,0:T(8,128)(2,1)S(1)} %collective-permute-done.57.refs_2_, ...), custom_call_target="tpu_custom_call" | custom-call | flops 3489660928 | bytes 6029312 | tf_op jit(solution)/shard_map/cond/branch_3_fun/score_far/pallas_call | solution.py:256
  49.7 0.0 collective-permute-done.58.refs_3_
  49.7 0.3 collective-permute-start.66
  50.0 1.3 %collective-permute-done.66.refs_4_ = bf16[128,1024]{1,0:T(8,128)(2,1)S(1)} collective-permute-done((bf16[128,1024]{1,0:T(8,128)(2,1)S(1)}, bf16[128,1024]{1,0:T(8,128)(2,1)S(1)}, u32[]{:S(2)}, u32[]{:S(2)}) %collective-permute-start.66) | collective-permute-done | bytes 262176 | tf_op jit(solution)/shard_map/cond/branch_3_fun/ppermute | solution.py:298
  51.3 3.3 %score_late.7 = (f32[2,128]{1,0:T(2,128)S(1)}, f32[1,128]{1,0:T(1,128)S(1)}, f32[1,128]{1,0:T(1,128)S(1)}, f32[1,128]{1,0:T(1,128)S(1)}) custom-call(bf16[256,1024]{1,0:T(8,128)(2,1)S(1)} %get-tuple-element.156.refs_0_, bf16[256,1024]{1,0:T(8,128)(2,1)S(1)} %constant_dynamic-update-slice_fusion.8.refs_1_, ...), custom_call_target="tpu_custom_call" | custom-call | flops 1342177280 | bytes 1835008 | tf_op jit(solution)/shard_map/cond/branch_3_fun/score_late/pallas_call | solution.py:256
  54.7 0.0 copy-start
  54.7 0.6 copy-done
  55.2 1.8 %collective-permute-start.67 = (f32[1,128]{1,0:T(1,128)S(1)}, f32[1,128]{1,0:T(1,128)S(1)}, u32[]{:S(2)}, u32[]{:S(2)}) collective-permute-start(f32[1,128]{1,0:T(1,128)S(1)} %get-tuple-element.164), channel_id=1, source_target_pairs={{0,12},{4,0},{8,4},{12,8},{1,13},{5,1},{9,5},{13,9},{2,14},{6,2},{... | collective-permute-start | bytes 1544 | tf_op jit(solution)/shard_map/cond/branch_3_fun/ppermute | solution.py:294
  57.0 2.1 %collective-permute-start.68 = (f32[1,128]{1,0:T(1,128)S(1)}, f32[1,128]{1,0:T(1,128)S(1)}, u32[]{:S(2)}, u32[]{:S(2)}) collective-permute-start(f32[1,128]{1,0:T(1,128)S(1)} %get-tuple-element.165), channel_id=1, source_target_pairs={{0,8},{4,12},{8,0},{12,4},{1,9},{5,13},{9,1},{13,5},{2,10},{6,14},... | collective-permute-start | bytes 1544 | tf_op jit(solution)/shard_map/cond/branch_3_fun/ppermute | solution.py:294
  59.1 0.0 collective-permute-start.69
  59.1 0.1 collective-permute-done.67.refs_1_
  59.1 0.0 copy-start.13
  59.1 2.3 %collective-permute-done.68.refs_2_ = f32[1,128]{1,0:T(1,128)S(1)} collective-permute-done((f32[1,128]{1,0:T(1,128)S(1)}, f32[1,128]{1,0:T(1,128)S(1)}, u32[]{:S(2)}, u32[]{:S(2)}) %collective-permute-start.68) | collective-permute-done | bytes 544 | tf_op jit(solution)/shard_map/cond/branch_3_fun/ppermute | solution.py:294
  61.5 0.0 copy-start.14
  61.5 3.0 %collective-permute-done.69.refs_3_ = f32[1,128]{1,0:T(1,128)S(1)} collective-permute-done((f32[1,128]{1,0:T(1,128)S(1)}, f32[1,128]{1,0:T(1,128)S(1)}, u32[]{:S(2)}, u32[]{:S(2)}) %collective-permute-start.69) | collective-permute-done | bytes 544 | tf_op jit(solution)/shard_map/cond/branch_3_fun/ppermute | solution.py:294
  64.4 0.0 copy-start.15
  64.4 0.0 copy-done.13
  64.4 0.0 copy-done.14
  64.4 0.6 copy-done.15
  65.0 0.7 %place_rows.7 = f32[5,128]{1,0:T(8,128)S(1)} custom-call(s32[26]{0:T(128)S(1)} %get-tuple-element.155.refs_5_.plan_ref, f32[2,128]{1,0:T(2,128)} %copy-done, f32[1,128]{1,0:T(1,128)} %copy-done.13, f32[1,128]{1,0:T(1,128)} %copy-done.14, f32[1,128]{1,0:T(1,128)} %copy-done.15), custom_call_target="tpu_custom_call" | custom-call | tf_op jit(solution)/shard_map/cond/branch_3_fun/place_rows/pallas_call | solution.py:284
  66.1 0.0 copy-start.5
  66.1 0.6 copy-done.5
  (2 shorter events, 0.0 us)
Async XLA Ops:
  0.0 2.0 %copy-start.6 = (s32[5]{0:T(128)S(1)}, s32[5]{0:T(128)}, u32[]{:S(2)}) copy-start(s32[5]{0:T(128)} %count_ref.1) | copy-start | bytes 64
  0.0 2.0 %copy-start.4 = (s32[4,5]{1,0:T(4,128)S(1)}, s32[4,5]{1,0:T(4,128)}, u32[]{:S(2)}) copy-start(s32[4,5]{1,0:T(4,128)} %fetch_ref.1) | copy-start | bytes 244
  0.0 2.0 %copy-start.7 = (s32[1,15]{1,0:T(1,128)S(1)}, s32[1,15]{1,0:T(1,128)}, u32[]{:S(2)}) copy-start(s32[1,15]{1,0:T(1,128)} %left_ref.1) | copy-start | bytes 184
  0.0 2.1 %copy-start.8 = (s32[1,15]{1,0:T(1,128)S(1)}, s32[1,15]{1,0:T(1,128)}, u32[]{:S(2)}) copy-start(s32[1,15]{1,0:T(1,128)} %right_ref.1) | copy-start | bytes 184
  4.7 12.3 %collective-permute-start.55 = (bf16[128,1024]{1,0:T(8,128)(2,1)S(1)}, bf16[128,1024]{1,0:T(8,128)(2,1)S(1)}, u32[]{:S(2)}, u32[]{:S(2)}) collective-permute-start(bf16[128,1024]{1,0:T(8,128)(2,1)S(1)} %get-tuple-element.157), channel_id=1, source_target_pairs={{0,4},{4,8},{8,12},{12,0},{1,5},{5,9},{9,13},{13,1},{2,6},{6,10},{... | collective-permute-start | bytes 786440 | tf_op jit(solution)/shard_map/cond/branch_3_fun/ppermute | solution.py:294
  7.8 15.2 %collective-permute-start.60 = (bf16[256,1024]{1,0:T(8,128)(2,1)S(1)}, bf16[256,1024]{1,0:T(8,128)(2,1)S(1)}, u32[]{:S(2)}, u32[]{:S(2)}) collective-permute-start(bf16[256,1024]{1,0:T(8,128)(2,1)S(1)} %get-tuple-element.156.refs_0_), channel_id=1, source_target_pairs={{0,2},{1,3},{2,0},{3,1},{4,6},{5,7},{6,4},{7,5},{8,10},{9,11},{10,... | collective-permute-start | bytes 1572872 | tf_op jit(solution)/shard_map/cond/branch_3_fun/ppermute | solution.py:298
  9.3 12.5 %collective-permute-start.56 = (bf16[128,1024]{1,0:T(8,128)(2,1)S(1)}, bf16[128,1024]{1,0:T(8,128)(2,1)S(1)}, u32[]{:S(2)}, u32[]{:S(2)}) collective-permute-start(bf16[128,1024]{1,0:T(8,128)(2,1)S(1)} %get-tuple-element.158), channel_id=1, source_target_pairs={{0,12},{4,0},{8,4},{12,8},{1,13},{5,1},{9,5},{13,9},{2,14},{6,2},{... | collective-permute-start | bytes 786440 | tf_op jit(solution)/shard_map/cond/branch_3_fun/ppermute | solution.py:294
  21.8 13.9 %collective-permute-start.63 = (bf16[256,1024]{1,0:T(8,128)(2,1)S(1)}, bf16[256,1024]{1,0:T(8,128)(2,1)S(1)}, u32[]{:S(2)}, u32[]{:S(2)}) collective-permute-start(bf16[256,1024]{1,0:T(8,128)(2,1)S(1)} %constant_dynamic-update-slice_fusion.8.refs_1_), channel_id=1, source_target_pairs={{0,2},{1,3},{2,0},{3,1},{4,6},{5,7},{6,4},{7,5},{8,10},{9,11},{10,... | collective-permute-start | bytes 1572872 | tf_op jit(solution)/shard_map/cond/branch_3_fun/ppermute | solution.py:298
  23.0 15.5 %collective-permute-start.59 = (bf16[256,1024]{1,0:T(8,128)(2,1)S(1)}, bf16[256,1024]{1,0:T(8,128)(2,1)S(1)}, u32[]{:S(2)}, u32[]{:S(2)}) collective-permute-start(bf16[256,1024]{1,0:T(8,128)(2,1)S(1)} %get-tuple-element.156.refs_0_), channel_id=1, source_target_pairs={{0,1},{1,0},{2,3},{3,2},{4,5},{5,4},{6,7},{7,6},{8,9},{9,8},{10,11... | collective-permute-start | bytes 1572872 | tf_op jit(solution)/shard_map/cond/branch_3_fun/ppermute | solution.py:298
  23.0 16.3 %collective-permute-start.61 = (bf16[256,1024]{1,0:T(8,128)(2,1)S(1)}, bf16[256,1024]{1,0:T(8,128)(2,1)S(1)}, u32[]{:S(2)}, u32[]{:S(2)}) collective-permute-start(bf16[256,1024]{1,0:T(8,128)(2,1)S(1)} %collective-permute-done.60.refs_3_.refs_4_), channel_id=1, source_target_pairs={{0,1},{1,0},{2,3},{3,2},{4,5},{5,4},{6,7},{7,6},{8,9},{9,8},{10,11... | collective-permute-start | bytes 1572872 | tf_op jit(solution)/shard_map/cond/branch_3_fun/ppermute | solution.py:298
  23.5 14.9 %collective-permute-start.57 = (bf16[128,1024]{1,0:T(8,128)(2,1)}, bf16[128,1024]{1,0:T(8,128)(2,1)S(1)}, u32[]{:S(2)}, u32[]{:S(2)}) collective-permute-start(bf16[128,1024]{1,0:T(8,128)(2,1)} %get-tuple-element.159), channel_id=1, source_target_pairs={{0,8},{4,12},{8,0},{12,4},{1,9},{5,13},{9,1},{13,5},{2,10},{6,14},... | collective-permute-start | bytes 786440 | tf_op jit(solution)/shard_map/cond/branch_3_fun/ppermute | solution.py:294
  25.9 4.8 %collective-permute-start.11 = (s32[1]{0:T(128)}, s32[1]{0:T(128)}, u32[]{:S(2)}, u32[]{:S(2)}) collective-permute-start(s32[1]{0:T(128)} %param.20), channel_id=1, source_target_pairs={{0,12},{4,0},{8,4},{12,8},{1,13},{5,1},{9,5},{13,9},{2,14},{6,2},{... | collective-permute-start | bytes 20 | tf_op jit(solution)/shard_map/cond/branch_3_fun/cond/branch_3_fun/ppermute | solution.py:294
  31.9 10.4 %collective-permute-start.62 = (bf16[256,1024]{1,0:T(8,128)(2,1)S(1)}, bf16[256,1024]{1,0:T(8,128)(2,1)S(1)}, u32[]{:S(2)}, u32[]{:S(2)}) collective-permute-start(bf16[256,1024]{1,0:T(8,128)(2,1)S(1)} %constant_dynamic-update-slice_fusion.8.refs_1_), channel_id=1, source_target_pairs={{0,1},{1,0},{2,3},{3,2},{4,5},{5,4},{6,7},{7,6},{8,9},{9,8},{10,11... | collective-permute-start | bytes 1572872 | tf_op jit(solution)/shard_map/cond/branch_3_fun/ppermute | solution.py:298
  35.7 6.6 %collective-permute-start.64 = (bf16[256,1024]{1,0:T(8,128)(2,1)S(1)}, bf16[256,1024]{1,0:T(8,128)(2,1)S(1)}, u32[]{:S(2)}, u32[]{:S(2)}) collective-permute-start(bf16[256,1024]{1,0:T(8,128)(2,1)S(1)} %collective-permute-done.63.refs_3_.refs_7_), channel_id=1, source_target_pairs={{0,1},{1,0},{2,3},{3,2},{4,5},{5,4},{6,7},{7,6},{8,9},{9,8},{10,11... | collective-permute-start | bytes 1572872 | tf_op jit(solution)/shard_map/cond/branch_3_fun/ppermute | solution.py:298
  38.5 6.7 %collective-permute-start.65 = (bf16[128,1024]{1,0:T(8,128)(2,1)S(1)}, bf16[128,1024]{1,0:T(8,128)(2,1)S(1)}, u32[]{:S(2)}, u32[]{:S(2)}) collective-permute-start(bf16[128,1024]{1,0:T(8,128)(2,1)S(1)} %collective-permute-done.57.refs_2_), channel_id=1, source_target_pairs={{0,1},{1,0},{2,3},{3,2},{4,5},{5,4},{6,7},{7,6},{8,9},{9,8},{10,11... | collective-permute-start | bytes 786440 | tf_op jit(solution)/shard_map/cond/branch_3_fun/ppermute | solution.py:298
  38.5 11.2 %collective-permute-start.58 = (bf16[128,1024]{1,0:T(8,128)(2,1)S(1)}, bf16[128,1024]{1,0:T(8,128)(2,1)S(1)}, u32[]{:S(2)}, u32[]{:S(2)}) collective-permute-start(bf16[128,1024]{1,0:T(8,128)(2,1)S(1)} %collective-permute-done.57.refs_2_), channel_id=1, source_target_pairs={{0,2},{1,3},{2,0},{3,1},{4,6},{5,7},{6,4},{7,5},{8,10},{9,11},{10,... | collective-permute-start | bytes 786440 | tf_op jit(solution)/shard_map/cond/branch_3_fun/ppermute | solution.py:298
  49.7 1.6 %collective-permute-start.66 = (bf16[128,1024]{1,0:T(8,128)(2,1)S(1)}, bf16[128,1024]{1,0:T(8,128)(2,1)S(1)}, u32[]{:S(2)}, u32[]{:S(2)}) collective-permute-start(bf16[128,1024]{1,0:T(8,128)(2,1)S(1)} %collective-permute-done.58.refs_3_), channel_id=1, source_target_pairs={{0,1},{1,0},{2,3},{3,2},{4,5},{5,4},{6,7},{7,6},{8,9},{9,8},{10,11... | collective-permute-start | bytes 786440 | tf_op jit(solution)/shard_map/cond/branch_3_fun/ppermute | solution.py:298
  54.7 0.6 copy-start
  55.2 3.9 %collective-permute-start.67 = (f32[1,128]{1,0:T(1,128)S(1)}, f32[1,128]{1,0:T(1,128)S(1)}, u32[]{:S(2)}, u32[]{:S(2)}) collective-permute-start(f32[1,128]{1,0:T(1,128)S(1)} %get-tuple-element.164), channel_id=1, source_target_pairs={{0,12},{4,0},{8,4},{12,8},{1,13},{5,1},{9,5},{13,9},{2,14},{6,2},{... | collective-permute-start | bytes 1544 | tf_op jit(solution)/shard_map/cond/branch_3_fun/ppermute | solution.py:294
  57.0 4.4 %collective-permute-start.68 = (f32[1,128]{1,0:T(1,128)S(1)}, f32[1,128]{1,0:T(1,128)S(1)}, u32[]{:S(2)}, u32[]{:S(2)}) collective-permute-start(f32[1,128]{1,0:T(1,128)S(1)} %get-tuple-element.165), channel_id=1, source_target_pairs={{0,8},{4,12},{8,0},{12,4},{1,9},{5,13},{9,1},{13,5},{2,10},{6,14},... | collective-permute-start | bytes 1544 | tf_op jit(solution)/shard_map/cond/branch_3_fun/ppermute | solution.py:294
  59.1 5.3 %collective-permute-start.69 = (f32[1,128]{1,0:T(1,128)S(1)}, f32[1,128]{1,0:T(1,128)S(1)}, u32[]{:S(2)}, u32[]{:S(2)}) collective-permute-start(f32[1,128]{1,0:T(1,128)S(1)} %get-tuple-element.166), channel_id=1, source_target_pairs={{0,4},{4,8},{8,12},{12,0},{1,5},{5,9},{9,13},{13,1},{2,6},{6,10},{... | collective-permute-start | bytes 1544 | tf_op jit(solution)/shard_map/cond/branch_3_fun/ppermute | solution.py:294
  59.1 5.3 %copy-start.13 = (f32[1,128]{1,0:T(1,128)}, f32[1,128]{1,0:T(1,128)S(1)}, u32[]{:S(2)}) copy-start(f32[1,128]{1,0:T(1,128)S(1)} %collective-permute-done.67.refs_1_) | copy-start | bytes 1540 | tf_op jit(solution)/shard_map/cond
  61.5 3.0 %copy-start.14 = (f32[1,128]{1,0:T(1,128)}, f32[1,128]{1,0:T(1,128)S(1)}, u32[]{:S(2)}) copy-start(f32[1,128]{1,0:T(1,128)S(1)} %collective-permute-done.68.refs_2_) | copy-start | bytes 1540 | tf_op jit(solution)/shard_map/cond
  64.4 0.6 copy-start.15
  66.1 0.6 copy-start.5

commit v2 on v1

--- a/solution.py
+++ b/solution.py
@@ -31,7 +31,7 @@
         if sum(counts) != blocks:
             continue
         turns = [counts[t:] + counts[:t] for t in range(places)]
-        pick = min(turns, key=lambda c: (cost(c), c))
+        pick = min(turns, key=lambda c: (-c[0], cost(c), c))
         best[min(turns)] = pick
     return sorted(best.values(), key=cost)
 
@@ -305,44 +305,38 @@
 def pattern_path(counts, capacity, pieces, rows, plan, bits, own, slots):
     places = len(counts)
     nearest = sorted((k for k in range(1, places) if counts[k]), key=lambda k: min(k, places - k))
-    sets = [[(0, j) for j in range(counts[0])], [(k, 0) for k in nearest[:2]],
+    sets = [[(0, j) for j in range(counts[0])], [(nearest[0], 0)], [(nearest[1], 0)],
             [(k, 0) for k in nearest[2:]] + [(k, 1) for k in nearest if counts[k] > 1]]
     taken = [(k, k * capacity + j) for group in sets for k, j in group]
     blocks = len(taken)
     per = pieces // 2
     sends = [lambda x: x] + [functools.partial(shift_by, k=k, places=places) for k in range(1, places)]
     moved = [shift_by(slots[at - capacity], k, places) for k, at in taken if k]
-    here = lax.switch(plan[1], sends, after(bits, moved[0]))
-    arrived = [own if len(sets[0]) == capacity else own[:rows], jnp.concatenate(moved[:2], axis=0),
+    arrived = [own if len(sets[0]) == capacity else own[:rows], moved[0], moved[1],
                moved[2] if len(moved) == 3 else jnp.concatenate(moved[2:], axis=0)]
     held = {}
-    first = [0, len(sets[0]), len(sets[0]) + 2, blocks]
-    ready, end = first[1], first[2]
+    first = [0, len(sets[0]), len(sets[0]) + 1, len(sets[0]) + 2, blocks]
+    ready, end = first[1], first[3]
+    acrosses = []
     for g, array in enumerate(arrived):
         across = swap_with(array, 2, pieces)
+        acrosses.append(across)
+        if g == 1:
+            here = lax.switch(plan[1], sends, after(bits, across))
         beside = swap_with(array, 1, pieces)
-        if g == 2:
-            near = score(pieces, held, range(end), range(ready * per, end * per), [(0, end, 0, (end - ready) * per)],
-                         name="score_near")
         for n, b in enumerate(range(first[g], first[g + 1])):
             held[b, 0], held[b, 1], held[b, 2] = (array, n, rows), (beside, n, rows), (across, n, rows)
-        if g == 1:
-            early = score(pieces, held, range(end), range(ready * per), [(0, end, 0, ready * per)], name="score_early")
-        if g == 2:
-            steps = [(end, blocks, 0, end * per)]
-            runs = range(end * per)
-            if blocks - end == 1:
-                runs = range(end * per + per - 1)
-                steps.append((0, blocks, end * per, len(runs)))
-            far = score(pieces, held, range(blocks), runs, steps, name="score_far")
-            across = after(across, early[0], near[0], far[0], here)
+        if g == 3:
+            runs = range(end * per + (per - 1) * (blocks - end == 1))
+            most = score(pieces, held, range(blocks), runs, [(0, blocks, 0, len(runs))], name="score_most")
+            across = after(across, most[0], here)
         corner = swap_with(across, 1, pieces)
         for n, b in enumerate(range(first[g], first[g + 1])):
             held[b, 3] = (corner, n, rows)
     order = sorted({k for k, _ in taken})
     groups = [[b for b in range(blocks) if taken[b][0] == k] for k in order]
     sums = score(pieces, held, range(blocks), range(len(runs), blocks * per), [(0, blocks, 0, blocks * per - len(runs))],
-                 (plan, [2 + places * capacity + at for _, at in taken], here, groups, [early, near, far]), name="score_late")
+                 (plan, [2 + places * capacity + at for _, at in taken], here, groups, [most]), name="score_late")
     returned = [s if k == 0 else shift_by(s, places - k, places) for k, s in zip(order, sums)]
     return place_rows([[taken[b][1] for b in g] for g in groups], plan, returned, blocks, rows)
 

time: 66.1 us -> 62 us (0.938); the launches traced: 66.6 us -> 61.8 us
  waiting for transfers between devices: 26.1 us -> 18.2 us
  starting transfers between devices: 16.8 us -> 24 us
  Pallas kernels: 16.7 us -> 12.7 us
    ppermute x7, waiting for transfers between devices: 21 us -> 14.1 us  [shift_by(): lax.ppermute(array, 'blk', [(i, (i + k) % places) for i in range(places)])]
    ppermute x7, starting transfers between devices: 12.4 us -> 17.6 us  [shift_by(): lax.ppermute(array, 'blk', [(i, (i + k) % places) for i in range(places)])]
    pallas_call x4 -> x2, Pallas kernels: 13.7 us -> 9.73 us  [score(): pl.pallas_call(functools.partial(score_kernel, rows, width, pieces, where...]
    ppermute x9 -> x12, starting transfers between devices: 4.4 us -> 6.37 us  [swap_with(): return lax.ppermute(array, 'sub', [(i, i ^ q) for i in range(pieces)])]
    ppermute x9 -> x12, waiting for transfers between devices: 5.13 us -> 4.11 us  [swap_with(): return lax.ppermute(array, 'sub', [(i, i ^ q) for i in range(pieces)])]
  transfers between devices with their start and end apart: 16 -> 19, of which waited for: 9 -> 8; matrix products, arithmetic and copies ran while one was open for 1% -> 1% of each run, Pallas kernels for 16% -> 10%
where the time goes in v2:
time: 62 us; the launch traced here: 61.8 us
  starting transfers between devices  24 us (39%)
  waiting for transfers between devices  18.2 us (29%)
  Pallas kernels  12.7 us (20%)
  local copies, waits for them, and re-layouts  3.69 us (6%)
  loops' own time  2.45 us (4%)
  between operations  0.75 us (1%)
    ppermute x7, starting transfers between devices, shift_by(): lax.ppermute(array, 'blk', [(i, (i + k) % places) for i in range(places)])  17.6 us
    ppermute x7, waiting for transfers between devices, shift_by(): lax.ppermute(array, 'blk', [(i, (i + k) % places) for i in range(places)])  14.1 us
    pallas_call x2, Pallas kernels, score(): pl.pallas_call(functools.partial(score_kernel, rows, width, pieces, where...  9.73 us
    ppermute x12, starting transfers between devices, swap_with(): return lax.ppermute(array, 'sub', [(i, i ^ q) for i in range(pieces)])  6.37 us
    ppermute x12, waiting for transfers between devices, swap_with(): return lax.ppermute(array, 'sub', [(i, i ^ q) for i in range(pieces)])  4.11 us
    pallas_call x1, Pallas kernels, make_plan(): pl.pallas_call(functools.partial(plan_kernel, patterns, places, capacity)...  2.25 us
    unnamed x11, local copies, waits for them, and re-layouts  1.97 us
  transfers between devices with their start and end apart: 19, of which 8 were waited for; matrix products, arithmetic and copies ran while one was open for 1% of the time, Pallas kernels for 10%

profile of v2, /device:TPU:0, one launch (start us, length us, event | category | flops | bytes accessed | tf_op | source)
XLA Modules:
  0.0 61.8 jit_solution(188606176475153432)
XLA Ops:
  0.0 0.0 copy-start.6
  0.0 0.0 copy-start.4
  0.0 0.0 copy-start.7
  0.0 0.0 copy-start.8
  0.0 1.4 %copy.37.emb_ref = bf16[5,128,1024]{2,1,0:T(8,128)(2,1)S(1)} copy(bf16[5,128,1024]{2,1,0:T(8,128)(2,1)} %param.29) | data formatting | bytes 2621440
  2.0 0.0 copy-done.6
  2.0 0.0 copy-done.4
  2.1 0.0 copy-done.7
  2.1 0.0 copy-done.8
  2.1 2.3 %plan_and_gather.1 = (s32[26]{0:T(128)S(1)}, s32[1]{0:T(128)}, bf16[256,1024]{1,0:T(8,128)(2,1)S(1)}, bf16[128,1024]{1,0:T(8,128)(2,1)S(1)}, bf16[128,1024]{1,0:...) custom-call(s32[1]{0:T(128)} %bitcast.31.me_ref, ...), custom_call_target="tpu_custom_call" | custom-call | tf_op jit(solution)/shard_map/plan_and_gather/pallas_call | solution.py:119
  4.4 56.8 %conditional.5 = (f32[5,128]{1,0:T(8,128)S(1)}) conditional(s32[]{:T(128)} %bitcast.33, (bf16[128,1024]{1,0:T(8,128)(2,1)S(1)}, bf16[128,1024]{1,0:T(8,128)(2,1)S(1)}, bf16[128,1024]{1,0:T(8,128)(2,1)S(1)}, bf16[256,1024]{1,0:T(8,128)(2,1)S(1)}, s32[26]{0:T(128)S(1)}, /*index=5*/s32[1]{0:T(128)}) %tuple.80, ...), branch_computations={%region_0.0_spmd, %region_5.0_spmd, %region_10.0_spmd, %region_15.... | conditional | flops 13423247360 | bytes 39954096 | solution.py:404
  4.4 3.1 %collective-permute-start.43 = (bf16[128,1024]{1,0:T(8,128)(2,1)S(1)}, bf16[128,1024]{1,0:T(8,128)(2,1)S(1)}, u32[]{:S(2)}, u32[]{:S(2)}) collective-permute-start(bf16[128,1024]{1,0:T(8,128)(2,1)S(1)} %get-tuple-element.143), channel_id=1, source_target_pairs={{0,4},{4,8},{8,12},{12,0},{1,5},{5,9},{9,13},{13,1},{2,6},{6,10},{... | collective-permute-start | bytes 786440 | tf_op jit(solution)/shard_map/cond/branch_2_fun/ppermute | solution.py:294
  7.5 1.5 %collective-permute-start.48 = (bf16[256,1024]{1,0:T(8,128)(2,1)S(1)}, bf16[256,1024]{1,0:T(8,128)(2,1)S(1)}, u32[]{:S(2)}, u32[]{:S(2)}) collective-permute-start(bf16[256,1024]{1,0:T(8,128)(2,1)S(1)} %get-tuple-element.142.refs_0_), channel_id=1, source_target_pairs={{0,2},{1,3},{2,0},{3,1},{4,6},{5,7},{6,4},{7,5},{8,10},{9,11},{10,... | collective-permute-start | bytes 1572872 | tf_op jit(solution)/shard_map/cond/branch_2_fun/ppermute | solution.py:298
  9.0 2.2 %collective-permute-start.44 = (bf16[128,1024]{1,0:T(8,128)(2,1)S(1)}, bf16[128,1024]{1,0:T(8,128)(2,1)S(1)}, u32[]{:S(2)}, u32[]{:S(2)}) collective-permute-start(bf16[128,1024]{1,0:T(8,128)(2,1)S(1)} %get-tuple-element.144), channel_id=1, source_target_pairs={{0,12},{4,0},{8,4},{12,8},{1,13},{5,1},{9,5},{13,9},{2,14},{6,2},{... | collective-permute-start | bytes 786440 | tf_op jit(solution)/shard_map/cond/branch_2_fun/ppermute | solution.py:294
  11.2 5.5 %collective-permute-done.43.refs_1_ = bf16[128,1024]{1,0:T(8,128)(2,1)S(1)} collective-permute-done((bf16[128,1024]{1,0:T(8,128)(2,1)S(1)}, bf16[128,1024]{1,0:T(8,128)(2,1)S(1)}, u32[]{:S(2)}, u32[]{:S(2)}) %collective-permute-start.43) | collective-permute-done | bytes 262176 | tf_op jit(solution)/shard_map/cond/branch_2_fun/ppermute | solution.py:294
  16.7 1.7 %collective-permute-start.51 = (bf16[128,1024]{1,0:T(8,128)(2,1)S(1)}, bf16[128,1024]{1,0:T(8,128)(2,1)S(1)}, u32[]{:S(2)}, u32[]{:S(2)}) collective-permute-start(bf16[128,1024]{1,0:T(8,128)(2,1)S(1)} %collective-permute-done.43.refs_1_), channel_id=1, source_target_pairs={{0,2},{1,3},{2,0},{3,1},{4,6},{5,7},{6,4},{7,5},{8,10},{9,11},{10,... | collective-permute-start | bytes 786440 | tf_op jit(solution)/shard_map/cond/branch_2_fun/ppermute | solution.py:298
  18.4 8.0 %collective-permute-start.45 = (bf16[128,1024]{1,0:T(8,128)(2,1)}, bf16[128,1024]{1,0:T(8,128)(2,1)S(1)}, u32[]{:S(2)}, u32[]{:S(2)}) collective-permute-start(bf16[128,1024]{1,0:T(8,128)(2,1)} %get-tuple-element.145), channel_id=1, source_target_pairs={{0,8},{4,12},{8,0},{12,4},{1,9},{5,13},{9,1},{13,5},{2,10},{6,14},... | collective-permute-start | bytes 786440 | tf_op jit(solution)/shard_map/cond/branch_2_fun/ppermute | solution.py:294
  26.4 0.0 collective-permute-start.47
  26.4 0.6 slice.46
  27.7 0.0 collective-permute-done.44.refs_2_
  27.7 0.6 collective-permute-start.54
  28.3 0.0 collective-permute-done.51.refs_8_
  28.3 6.6 %conditional.2 = (s32[1]{0:T(128)}) conditional(s32[]{:T(128)} %bitcast.2, s32[1]{0:T(128)} %get-tuple-element.147, s32[1]{0:T(128)} %get-tuple-element.147, s32[1]{0:T(128)} %get-tuple-element.147, s32[1]{0:T(128)} %get-tuple-element.147), branch_computations={%region_11.0_spmd, %region_12.0_spmd, %region_13.0_spmd, %region_1... | conditional | bytes 72 | solution.py:325
  28.3 0.0 collective-permute-start.40
  28.3 5.3 %collective-permute-done.40 = s32[1]{0:T(128)} collective-permute-done((s32[1]{0:T(128)}, s32[1]{0:T(128)}, u32[]{:S(2)}, u32[]{:S(2)}) %collective-permute-start.40) | collective-permute-done | bytes 36 | tf_op jit(solution)/shard_map/cond/branch_2_fun/cond/branch_1_fun/ppermute | solution.py:294
  34.9 0.0 collective-permute-start.50
  34.9 0.0 collective-permute-done.45.refs_3_
  34.9 0.5 collective-permute-start.53
  35.4 0.0 collective-permute-done.48.refs_5_
  35.4 0.1 collective-permute-start.49
  35.5 1.0 %collective-permute-done.54.refs_11_ = bf16[128,1024]{1,0:T(8,128)(2,1)S(1)} collective-permute-done((bf16[128,1024]{1,0:T(8,128)(2,1)S(1)}, bf16[128,1024]{1,0:T(8,128)(2,1)S(1)}, u32[]{:S(2)}, u32[]{:S(2)}) %collective-permute-start.54) | collective-permute-done | bytes 262176 | tf_op jit(solution)/shard_map/cond/branch_2_fun/ppermute | solution.py:298
  36.5 0.0 collective-permute-start.56
  36.5 0.0 collective-permute-done.50.refs_7_
  36.5 0.5 collective-permute-start.52
  37.0 0.0 collective-permute-done.53.refs_10_
  37.0 0.1 collective-permute-start.55
  37.1 0.9 %collective-permute-done.56.refs_13_ = bf16[128,1024]{1,0:T(8,128)(2,1)S(1)} collective-permute-done((bf16[128,1024]{1,0:T(8,128)(2,1)S(1)}, bf16[128,1024]{1,0:T(8,128)(2,1)S(1)}, u32[]{:S(2)}, u32[]{:S(2)}) %collective-permute-start.56) | collective-permute-done | bytes 262176 | tf_op jit(solution)/shard_map/cond/branch_2_fun/ppermute | solution.py:298
  38.0 1.4 %collective-permute-start.46 = (bf16[128,1024]{1,0:T(8,128)(2,1)S(1)}, bf16[128,1024]{1,0:T(8,128)(2,1)S(1)}, u32[]{:S(2)}, u32[]{:S(2)}) collective-permute-start(bf16[128,1024]{1,0:T(8,128)(2,1)S(1)} %collective-permute-done.45.refs_3_), channel_id=1, source_target_pairs={{0,2},{1,3},{2,0},{3,1},{4,6},{5,7},{6,4},{7,5},{8,10},{9,11},{10,... | collective-permute-start | bytes 786440 | tf_op jit(solution)/shard_map/cond/branch_2_fun/ppermute | solution.py:298
  39.4 0.0 collective-permute-done.47.refs_4_
  39.4 0.0 collective-permute-done.52.refs_9_
  39.4 0.0 collective-permute-done.55.refs_12_
  39.4 0.0 collective-permute-done.49.refs_6_
  39.4 6.4 %score_most.6.refs_8_ = f32[25,128,128]{2,1,0:T(8,128)S(1)} custom-call(bf16[256,1024]{1,0:T(8,128)(2,1)S(1)} %get-tuple-element.142.refs_0_, bf16[128,1024]{1,0:T(8,128)(2,1)S(1)} %collective-permute-done.43.refs_1_, bf16[128,1024]{1,0:T(8,128)(2,1)S(1)} %collective-permute-done.44.refs_2_, bf16[128,1024]{1,0:T(8,128)(2,1)S(1)} %collective-permute-done.45.refs_3_, ...), custom_call_target="tpu_custom_call" | custom-call | flops 12079595520 | bytes 6029312 | tf_op jit(solution)/shard_map/cond/branch_2_fun/score_most/pallas_call | solution.py:256
  45.8 0.6 collective-permute-done.46.refs_4_
  46.4 0.0 collective-permute-start.57
  46.4 1.5 %collective-permute-done.57.refs_5_ = bf16[128,1024]{1,0:T(8,128)(2,1)S(1)} collective-permute-done((bf16[128,1024]{1,0:T(8,128)(2,1)S(1)}, bf16[128,1024]{1,0:T(8,128)(2,1)S(1)}, u32[]{:S(2)}, u32[]{:S(2)}) %collective-permute-start.57) | collective-permute-done | bytes 262176 | tf_op jit(solution)/shard_map/cond/branch_2_fun/ppermute | solution.py:298
  47.9 3.4 %score_late.6 = (f32[2,128]{1,0:T(2,128)S(1)}, f32[1,128]{1,0:T(1,128)S(1)}, f32[1,128]{1,0:T(1,128)S(1)}, f32[1,128]{1,0:T(1,128)S(1)}) custom-call(bf16[256,1024]{1,0:T(8,128)(2,1)S(1)} %get-tuple-element.142.refs_0_, bf16[128,1024]{1,0:T(8,128)(2,1)S(1)} %collective-permute-done.43.refs_1_, bf16[128,1024]{1,0:T(8,128)(2,1)S(1)} %collective-permute-done.44.refs_2_, ...), custom_call_target="tpu_custom_call" | custom-call | flops 1342177280 | bytes 1835008 | tf_op jit(solution)/shard_map/cond/branch_2_fun/score_late/pallas_call | solution.py:256
  51.3 0.0 copy-start
  51.3 0.6 copy-done
  51.9 1.7 %collective-permute-start.58 = (f32[1,128]{1,0:T(1,128)S(1)}, f32[1,128]{1,0:T(1,128)S(1)}, u32[]{:S(2)}, u32[]{:S(2)}) collective-permute-start(f32[1,128]{1,0:T(1,128)S(1)} %get-tuple-element.150), channel_id=1, source_target_pairs={{0,12},{4,0},{8,4},{12,8},{1,13},{5,1},{9,5},{13,9},{2,14},{6,2},{... | collective-permute-start | bytes 1544 | tf_op jit(solution)/shard_map/cond/branch_2_fun/ppermute | solution.py:294
  53.5 0.6 collective-permute-start.59
  54.1 2.0 %collective-permute-start.60 = (f32[1,128]{1,0:T(1,128)S(1)}, f32[1,128]{1,0:T(1,128)S(1)}, u32[]{:S(2)}, u32[]{:S(2)}) collective-permute-start(f32[1,128]{1,0:T(1,128)S(1)} %get-tuple-element.152), channel_id=1, source_target_pairs={{0,4},{4,8},{8,12},{12,0},{1,5},{5,9},{9,13},{13,1},{2,6},{6,10},{... | collective-permute-start | bytes 1544 | tf_op jit(solution)/shard_map/cond/branch_2_fun/ppermute | solution.py:294
  56.1 0.0 collective-permute-done.58.refs_1_
  56.1 0.0 copy-start.12
  56.1 1.8 %collective-permute-done.59.refs_2_ = f32[1,128]{1,0:T(1,128)S(1)} collective-permute-done((f32[1,128]{1,0:T(1,128)S(1)}, f32[1,128]{1,0:T(1,128)S(1)}, u32[]{:S(2)}, u32[]{:S(2)}) %collective-permute-start.59) | collective-permute-done | bytes 544 | tf_op jit(solution)/shard_map/cond/branch_2_fun/ppermute | solution.py:294
  58.0 0.0 copy-start.13
  58.0 1.5 %collective-permute-done.60.refs_3_ = f32[1,128]{1,0:T(1,128)S(1)} collective-permute-done((f32[1,128]{1,0:T(1,128)S(1)}, f32[1,128]{1,0:T(1,128)S(1)}, u32[]{:S(2)}, u32[]{:S(2)}) %collective-permute-start.60) | collective-permute-done | bytes 544 | tf_op jit(solution)/shard_map/cond/branch_2_fun/ppermute | solution.py:294
  59.4 0.0 copy-start.14
  59.4 0.0 copy-done.12
  59.4 0.0 copy-done.13
  59.4 0.6 copy-done.14
  60.0 0.7 %place_rows.6 = f32[5,128]{1,0:T(8,128)S(1)} custom-call(s32[26]{0:T(128)S(1)} %get-tuple-element.141.refs_6_.plan_ref, f32[2,128]{1,0:T(2,128)} %copy-done, f32[1,128]{1,0:T(1,128)} %copy-done.12, f32[1,128]{1,0:T(1,128)} %copy-done.13, f32[1,128]{1,0:T(1,128)} %copy-done.14), custom_call_target="tpu_custom_call" | custom-call | tf_op jit(solution)/shard_map/cond/branch_2_fun/place_rows/pallas_call | solution.py:284
  61.2 0.0 copy-start.5
  61.2 0.6 copy-done.5
Async XLA Ops:
  0.0 2.0 %copy-start.6 = (s32[5]{0:T(128)S(1)}, s32[5]{0:T(128)}, u32[]{:S(2)}) copy-start(s32[5]{0:T(128)} %count_ref.1) | copy-start | bytes 64
  0.0 2.0 %copy-start.4 = (s32[4,5]{1,0:T(4,128)S(1)}, s32[4,5]{1,0:T(4,128)}, u32[]{:S(2)}) copy-start(s32[4,5]{1,0:T(4,128)} %fetch_ref.1) | copy-start | bytes 244
  0.0 2.0 %copy-start.7 = (s32[1,15]{1,0:T(1,128)S(1)}, s32[1,15]{1,0:T(1,128)}, u32[]{:S(2)}) copy-start(s32[1,15]{1,0:T(1,128)} %left_ref.1) | copy-start | bytes 184
  0.0 2.1 %copy-start.8 = (s32[1,15]{1,0:T(1,128)S(1)}, s32[1,15]{1,0:T(1,128)}, u32[]{:S(2)}) copy-start(s32[1,15]{1,0:T(1,128)} %right_ref.1) | copy-start | bytes 184
  4.4 12.3 %collective-permute-start.43 = (bf16[128,1024]{1,0:T(8,128)(2,1)S(1)}, bf16[128,1024]{1,0:T(8,128)(2,1)S(1)}, u32[]{:S(2)}, u32[]{:S(2)}) collective-permute-start(bf16[128,1024]{1,0:T(8,128)(2,1)S(1)} %get-tuple-element.143), channel_id=1, source_target_pairs={{0,4},{4,8},{8,12},{12,0},{1,5},{5,9},{9,13},{13,1},{2,6},{6,10},{... | collective-permute-start | bytes 786440 | tf_op jit(solution)/shard_map/cond/branch_2_fun/ppermute | solution.py:294
  7.5 27.9 %collective-permute-start.48 = (bf16[256,1024]{1,0:T(8,128)(2,1)S(1)}, bf16[256,1024]{1,0:T(8,128)(2,1)S(1)}, u32[]{:S(2)}, u32[]{:S(2)}) collective-permute-start(bf16[256,1024]{1,0:T(8,128)(2,1)S(1)} %get-tuple-element.142.refs_0_), channel_id=1, source_target_pairs={{0,2},{1,3},{2,0},{3,1},{4,6},{5,7},{6,4},{7,5},{8,10},{9,11},{10,... | collective-permute-start | bytes 1572872 | tf_op jit(solution)/shard_map/cond/branch_2_fun/ppermute | solution.py:298
  9.0 18.7 %collective-permute-start.44 = (bf16[128,1024]{1,0:T(8,128)(2,1)S(1)}, bf16[128,1024]{1,0:T(8,128)(2,1)S(1)}, u32[]{:S(2)}, u32[]{:S(2)}) collective-permute-start(bf16[128,1024]{1,0:T(8,128)(2,1)S(1)} %get-tuple-element.144), channel_id=1, source_target_pairs={{0,12},{4,0},{8,4},{12,8},{1,13},{5,1},{9,5},{13,9},{2,14},{6,2},{... | collective-permute-start | bytes 786440 | tf_op jit(solution)/shard_map/cond/branch_2_fun/ppermute | solution.py:294
  16.7 11.6 %collective-permute-start.51 = (bf16[128,1024]{1,0:T(8,128)(2,1)S(1)}, bf16[128,1024]{1,0:T(8,128)(2,1)S(1)}, u32[]{:S(2)}, u32[]{:S(2)}) collective-permute-start(bf16[128,1024]{1,0:T(8,128)(2,1)S(1)} %collective-permute-done.43.refs_1_), channel_id=1, source_target_pairs={{0,2},{1,3},{2,0},{3,1},{4,6},{5,7},{6,4},{7,5},{8,10},{9,11},{10,... | collective-permute-start | bytes 786440 | tf_op jit(solution)/shard_map/cond/branch_2_fun/ppermute | solution.py:298
  18.4 16.5 %collective-permute-start.45 = (bf16[128,1024]{1,0:T(8,128)(2,1)}, bf16[128,1024]{1,0:T(8,128)(2,1)S(1)}, u32[]{:S(2)}, u32[]{:S(2)}) collective-permute-start(bf16[128,1024]{1,0:T(8,128)(2,1)} %get-tuple-element.145), channel_id=1, source_target_pairs={{0,8},{4,12},{8,0},{12,4},{1,9},{5,13},{9,1},{13,5},{2,10},{6,14},... | collective-permute-start | bytes 786440 | tf_op jit(solution)/shard_map/cond/branch_2_fun/ppermute | solution.py:294
  26.4 12.9 %collective-permute-start.47 = (bf16[256,1024]{1,0:T(8,128)(2,1)S(1)}, bf16[256,1024]{1,0:T(8,128)(2,1)S(1)}, u32[]{:S(2)}, u32[]{:S(2)}) collective-permute-start(bf16[256,1024]{1,0:T(8,128)(2,1)S(1)} %get-tuple-element.142.refs_0_), channel_id=1, source_target_pairs={{0,1},{1,0},{2,3},{3,2},{4,5},{5,4},{6,7},{7,6},{8,9},{9,8},{10,11... | collective-permute-start | bytes 1572872 | tf_op jit(solution)/shard_map/cond/branch_2_fun/ppermute | solution.py:298
  27.7 8.8 %collective-permute-start.54 = (bf16[128,1024]{1,0:T(8,128)(2,1)S(1)}, bf16[128,1024]{1,0:T(8,128)(2,1)S(1)}, u32[]{:S(2)}, u32[]{:S(2)}) collective-permute-start(bf16[128,1024]{1,0:T(8,128)(2,1)S(1)} %collective-permute-done.44.refs_2_), channel_id=1, source_target_pairs={{0,2},{1,3},{2,0},{3,1},{4,6},{5,7},{6,4},{7,5},{8,10},{9,11},{10,... | collective-permute-start | bytes 786440 | tf_op jit(solution)/shard_map/cond/branch_2_fun/ppermute | solution.py:298
  28.3 5.3 %collective-permute-start.40 = (s32[1]{0:T(128)}, s32[1]{0:T(128)}, u32[]{:S(2)}, u32[]{:S(2)}) collective-permute-start(s32[1]{0:T(128)} %param.13), channel_id=1, source_target_pairs={{0,4},{4,8},{8,12},{12,0},{1,5},{5,9},{9,13},{13,1},{2,6},{6,10},{... | collective-permute-start | bytes 20 | tf_op jit(solution)/shard_map/cond/branch_2_fun/cond/branch_1_fun/ppermute | solution.py:294
  34.9 1.6 %collective-permute-start.50 = (bf16[128,1024]{1,0:T(8,128)(2,1)S(1)}, bf16[128,1024]{1,0:T(8,128)(2,1)S(1)}, u32[]{:S(2)}, u32[]{:S(2)}) collective-permute-start(bf16[128,1024]{1,0:T(8,128)(2,1)S(1)} %collective-permute-done.43.refs_1_), channel_id=1, source_target_pairs={{0,1},{1,0},{2,3},{3,2},{4,5},{5,4},{6,7},{7,6},{8,9},{9,8},{10,11... | collective-permute-start | bytes 786440 | tf_op jit(solution)/shard_map/cond/branch_2_fun/ppermute | solution.py:298
  34.9 2.1 %collective-permute-start.53 = (bf16[128,1024]{1,0:T(8,128)(2,1)S(1)}, bf16[128,1024]{1,0:T(8,128)(2,1)S(1)}, u32[]{:S(2)}, u32[]{:S(2)}) collective-permute-start(bf16[128,1024]{1,0:T(8,128)(2,1)S(1)} %collective-permute-done.44.refs_2_), channel_id=1, source_target_pairs={{0,1},{1,0},{2,3},{3,2},{4,5},{5,4},{6,7},{7,6},{8,9},{9,8},{10,11... | collective-permute-start | bytes 786440 | tf_op jit(solution)/shard_map/cond/branch_2_fun/ppermute | solution.py:298
  35.4 4.0 %collective-permute-start.49 = (bf16[256,1024]{1,0:T(8,128)(2,1)S(1)}, bf16[256,1024]{1,0:T(8,128)(2,1)S(1)}, u32[]{:S(2)}, u32[]{:S(2)}) collective-permute-start(bf16[256,1024]{1,0:T(8,128)(2,1)S(1)} %collective-permute-done.48.refs_5_), channel_id=1, source_target_pairs={{0,1},{1,0},{2,3},{3,2},{4,5},{5,4},{6,7},{7,6},{8,9},{9,8},{10,11... | collective-permute-start | bytes 1572872 | tf_op jit(solution)/shard_map/cond/branch_2_fun/ppermute | solution.py:298
  36.5 1.5 %collective-permute-start.56 = (bf16[128,1024]{1,0:T(8,128)(2,1)S(1)}, bf16[128,1024]{1,0:T(8,128)(2,1)S(1)}, u32[]{:S(2)}, u32[]{:S(2)}) collective-permute-start(bf16[128,1024]{1,0:T(8,128)(2,1)S(1)} %collective-permute-done.45.refs_3_), channel_id=1, source_target_pairs={{0,1},{1,0},{2,3},{3,2},{4,5},{5,4},{6,7},{7,6},{8,9},{9,8},{10,11... | collective-permute-start | bytes 786440 | tf_op jit(solution)/shard_map/cond/branch_2_fun/ppermute | solution.py:298
  36.5 2.9 %collective-permute-start.52 = (bf16[128,1024]{1,0:T(8,128)(2,1)S(1)}, bf16[128,1024]{1,0:T(8,128)(2,1)S(1)}, u32[]{:S(2)}, u32[]{:S(2)}) collective-permute-start(bf16[128,1024]{1,0:T(8,128)(2,1)S(1)} %collective-permute-done.51.refs_8_), channel_id=1, source_target_pairs={{0,1},{1,0},{2,3},{3,2},{4,5},{5,4},{6,7},{7,6},{8,9},{9,8},{10,11... | collective-permute-start | bytes 786440 | tf_op jit(solution)/shard_map/cond/branch_2_fun/ppermute | solution.py:298
  37.0 2.4 %collective-permute-start.55 = (bf16[128,1024]{1,0:T(8,128)(2,1)S(1)}, bf16[128,1024]{1,0:T(8,128)(2,1)S(1)}, u32[]{:S(2)}, u32[]{:S(2)}) collective-permute-start(bf16[128,1024]{1,0:T(8,128)(2,1)S(1)} %collective-permute-done.54.refs_11_), channel_id=1, source_target_pairs={{0,1},{1,0},{2,3},{3,2},{4,5},{5,4},{6,7},{7,6},{8,9},{9,8},{10,11... | collective-permute-start | bytes 786440 | tf_op jit(solution)/shard_map/cond/branch_2_fun/ppermute | solution.py:298
  38.0 8.3 %collective-permute-start.46 = (bf16[128,1024]{1,0:T(8,128)(2,1)S(1)}, bf16[128,1024]{1,0:T(8,128)(2,1)S(1)}, u32[]{:S(2)}, u32[]{:S(2)}) collective-permute-start(bf16[128,1024]{1,0:T(8,128)(2,1)S(1)} %collective-permute-done.45.refs_3_), channel_id=1, source_target_pairs={{0,2},{1,3},{2,0},{3,1},{4,6},{5,7},{6,4},{7,5},{8,10},{9,11},{10,... | collective-permute-start | bytes 786440 | tf_op jit(solution)/shard_map/cond/branch_2_fun/ppermute | solution.py:298
  46.4 1.5 %collective-permute-start.57 = (bf16[128,1024]{1,0:T(8,128)(2,1)S(1)}, bf16[128,1024]{1,0:T(8,128)(2,1)S(1)}, u32[]{:S(2)}, u32[]{:S(2)}) collective-permute-start(bf16[128,1024]{1,0:T(8,128)(2,1)S(1)} %collective-permute-done.46.refs_4_), channel_id=1, source_target_pairs={{0,1},{1,0},{2,3},{3,2},{4,5},{5,4},{6,7},{7,6},{8,9},{9,8},{10,11... | collective-permute-start | bytes 786440 | tf_op jit(solution)/shard_map/cond/branch_2_fun/ppermute | solution.py:298
  51.3 0.6 copy-start
  51.9 4.3 %collective-permute-start.58 = (f32[1,128]{1,0:T(1,128)S(1)}, f32[1,128]{1,0:T(1,128)S(1)}, u32[]{:S(2)}, u32[]{:S(2)}) collective-permute-start(f32[1,128]{1,0:T(1,128)S(1)} %get-tuple-element.150), channel_id=1, source_target_pairs={{0,12},{4,0},{8,4},{12,8},{1,13},{5,1},{9,5},{13,9},{2,14},{6,2},{... | collective-permute-start | bytes 1544 | tf_op jit(solution)/shard_map/cond/branch_2_fun/ppermute | solution.py:294
  53.5 4.4 %collective-permute-start.59 = (f32[1,128]{1,0:T(1,128)S(1)}, f32[1,128]{1,0:T(1,128)S(1)}, u32[]{:S(2)}, u32[]{:S(2)}) collective-permute-start(f32[1,128]{1,0:T(1,128)S(1)} %get-tuple-element.151), channel_id=1, source_target_pairs={{0,8},{4,12},{8,0},{12,4},{1,9},{5,13},{9,1},{13,5},{2,10},{6,14},... | collective-permute-start | bytes 1544 | tf_op jit(solution)/shard_map/cond/branch_2_fun/ppermute | solution.py:294
  54.1 5.3 %collective-permute-start.60 = (f32[1,128]{1,0:T(1,128)S(1)}, f32[1,128]{1,0:T(1,128)S(1)}, u32[]{:S(2)}, u32[]{:S(2)}) collective-permute-start(f32[1,128]{1,0:T(1,128)S(1)} %get-tuple-element.152), channel_id=1, source_target_pairs={{0,4},{4,8},{8,12},{12,0},{1,5},{5,9},{9,13},{13,1},{2,6},{6,10},{... | collective-permute-start | bytes 1544 | tf_op jit(solution)/shard_map/cond/branch_2_fun/ppermute | solution.py:294
  56.1 3.3 %copy-start.12 = (f32[1,128]{1,0:T(1,128)}, f32[1,128]{1,0:T(1,128)S(1)}, u32[]{:S(2)}) copy-start(f32[1,128]{1,0:T(1,128)S(1)} %collective-permute-done.58.refs_1_) | copy-start | bytes 1540 | tf_op jit(solution)/shard_map/cond
  58.0 1.5 %copy-start.13 = (f32[1,128]{1,0:T(1,128)}, f32[1,128]{1,0:T(1,128)S(1)}, u32[]{:S(2)}) copy-start(f32[1,128]{1,0:T(1,128)S(1)} %collective-permute-done.59.refs_2_) | copy-start | bytes 1540 | tf_op jit(solution)/shard_map/cond
  59.4 0.6 copy-start.14
  61.2 0.6 copy-start.5

commit v3 on v2

--- a/solution.py
+++ b/solution.py
@@ -36,6 +36,10 @@
     return sorted(best.values(), key=cost)
 
 
+def owner_of(block, blocks, places):
+    return sum((block >= i * blocks).astype(jnp.int32) for i in range(1, places))
+
+
 def unary(counts):
     return sum(((1 << c) - 1) << (2 * r) for r, c in enumerate(counts))
 
@@ -58,8 +62,9 @@
     for s in range(places):
         seen = jnp.int32(0)
         for p in range(blocks):
-            owner = lax.div(fetch_ref[s, p], blocks)
-            bit = lax.shift_left(jnp.int32(1), 2 * lax.rem(owner + (places - s), places))
+            owner = owner_of(fetch_ref[s, p], blocks, places)
+            turned = owner - s
+            bit = lax.shift_left(jnp.int32(1), 2 * jnp.where(turned < 0, turned + places, turned))
             seen = seen | bit | ((seen & bit) << 1)
         used = used | seen
     choice = jnp.int32(len(patterns))
@@ -71,6 +76,7 @@
             choice = jnp.where(fits, m, choice)
             shift = jnp.where(fits, t, shift)
     plan_ref[0] = choice
+    plan_ref[plan_ref.shape[0] - 1] = me
     plan_ref[1] = shift
     mine = lax.rem(me + places - shift, places)
     total = places * capacity
@@ -78,17 +84,17 @@
     for k in range(places):
         owner = lax.rem(me + places - k, places)
         target = lax.rem(me + k + places - shift, places)
-        place, lid, seen = [jnp.int32(0)] * capacity, [jnp.int32(0)] * capacity, jnp.int32(0)
-        send, sent = [jnp.int32(0)] * capacity, jnp.int32(0)
+        place, seen = [jnp.int32(0)] * capacity, jnp.int32(0)
+        send, spot, sent = [jnp.int32(0)] * capacity, [jnp.int32(0)] * capacity, jnp.int32(0)
         for p in range(blocks):
             listed = fetch_ref[mine, p]
-            hit = lax.div(listed, blocks) == owner
+            hit = owner_of(listed, blocks, places) == owner
             outward = fetch_ref[target, p]
-            goes = lax.div(outward, blocks) == me
+            goes = owner_of(outward, blocks, places) == me
             for j in range(capacity):
                 place[j] = jnp.where(hit & (seen == j), p, place[j])
-                lid[j] = jnp.where(hit & (seen == j), listed - owner * blocks, lid[j])
                 send[j] = jnp.where(goes & (sent == j), outward - me * blocks, send[j])
+                spot[j] = jnp.where(goes & (sent == j), p, spot[j])
             seen = seen + hit.astype(jnp.int32)
             sent = sent + goes.astype(jnp.int32)
         for j in range(capacity):
@@ -98,7 +104,7 @@
             copies.append((sent > j, copy))
             plan_ref[2 + at] = send[j]
             plan_ref[2 + total + at] = place[j]
-            plan_ref[2 + 2 * total + at] = lid[j]
+            plan_ref[2 + 2 * total + at] = spot[j]
     bits = jnp.int32(0)
     for p in range(left_ref.shape[1]):
         a, b = left_ref[0, p], right_ref[0, p]
@@ -118,7 +124,7 @@
     others = total - capacity
     out = pl.pallas_call(
         functools.partial(plan_kernel, patterns, places, capacity),
-        out_shape=[jax.ShapeDtypeStruct((2 + 3 * total,), jnp.int32),
+        out_shape=[jax.ShapeDtypeStruct((3 + 3 * total,), jnp.int32),
                    jax.ShapeDtypeStruct((1,), jnp.int32), own] + [slot] * others,
         in_specs=[SMEM] * 7 + [ANY],
         out_specs=[SMEM, SMEM] + [VMEM] * (1 + others),
@@ -138,16 +144,26 @@
     arrays = [refs.pop(0) for _ in range(1 + max(i for i, _ in wheres))]
     spots_in = [arrays[i].at[pl.ds(n * rows, rows)] for i, n in wheres]
     left_in, right_in = spots_in[:len(owned)], spots_in[len(owned):]
-    finish = None
+    finish = passed = None
     if places is not None:
         finish = [refs.pop(0) for _ in range(2 + places[0])]
-    out_refs = [refs.pop(0) for _ in (places[2] if places else (0,))]
-    left, right, left_scale, gram, left_sems, right_sems = refs[:6]
-    sums = refs[6] if places else out_refs[0]
+        if not owned:
+            passed = refs.pop(0), refs.pop(0)
+    hand_on = places is None
+    out_refs = [refs.pop(0) for _ in (places[2] if places and places[2] else range(1 + 2 * hand_on))]
+    if hand_on:
+        right, gram, left_sems, right_sems = refs[:4]
+        left, left_scale = out_refs[1:]
+    elif passed is None:
+        left, right, left_scale, gram, left_sems, right_sems = refs[:6]
+    else:
+        right, gram, right_sems = refs[:3]
+        left, left_scale = passed
+    sums = refs[-1] if places else out_refs[0]
     per = pieces // 2
     copies = []
     for i, a in enumerate(owned):
-        copies.append(pltpu.make_async_copy(left_in[i], left.at[pl.ds(a * rows, rows)], left_sems.at[i]))
+        copies.append(pltpu.make_async_copy(left_in[i], left.at[pl.ds(i * rows, rows)], left_sems.at[i]))
     for i in range(2 * len(runs)):
         copies.append(pltpu.make_async_copy(right_in[i], right.at[pl.ds(i * rows, rows)], right_sems.at[i]))
     for copy in copies:
@@ -166,7 +182,7 @@
 
     @pl.loop(0, len(owned))
     def _(i):
-        here = pl.ds((owned[0] + i) * rows, rows)
+        here = pl.ds(pl.multiple_of(i * rows, rows), rows)
         inv = lax.rsqrt(squares(left[here, :]) * (1.0 / width) + norm_eps)
         left_scale[here, :] = jnp.broadcast_to(inv * (kernel_scale / width * math.log2(math.e)), (rows, rows))
 
@@ -214,6 +230,20 @@
     bits = bits_ref[0]
     spot = [plan_ref[at] for at in spots]
     blocks = len(spots)
+    if groups is None:
+        for a in range(blocks):
+            in_use = left_scale[a * rows:(a + 1) * rows, :1] > SCALE_IN_USE
+            by_block = {}
+            for source, at, b in listed[a]:
+                part = (sums if source < 0 else finish[2 + source])[at]
+                by_block[b] = by_block[b] + part if b in by_block else part
+            for b, part in by_block.items():
+                total = jnp.where(in_use, jnp.sum(part, axis=1, keepdims=True), 0.0)
+                out_refs[0][pl.ds(a * blocks + spot[b], 1), :] = lanes(total)
+        lane = lax.broadcasted_iota(jnp.int32, (1, rows), 1)
+        flags = sum(jnp.where(lane == i, (bits >> i) & 1, 0) for i in range(blocks * blocks))
+        out_refs[0][blocks * blocks:blocks * blocks + 1, :] = flags.astype(jnp.float32)
+        return
     for ref, group in zip(out_refs, groups):
         for n, a in enumerate(group):
             total = jnp.zeros((rows, rows), jnp.float32)
@@ -226,8 +256,8 @@
 
 
 def score(pieces, held, owned, runs, steps, meta=None, name="score"):
-    width = held[owned[0], 0][0].shape[1]
-    rows = held[owned[0], 0][2]
+    array, _, rows = held[0, 0]
+    width = array.shape[1]
     per = pieces // 2
     rights = [held[run // per, 2 * (run % per) + h] for run in runs for h in range(2)]
     arrays, wheres = [], []
@@ -239,18 +269,22 @@
     tall = max(hi - lo for lo, hi, _, _ in steps) * rows
     pairs = pairs_of(per, runs, steps)
     sums = jax.ShapeDtypeStruct((len(pairs), rows, rows), jnp.float32)
-    places, extra, extra_specs, out_shape, scratch = None, [], [], [sums], []
+    tall_left = len(owned) * rows
+    lefts = [(tall_left, width), jnp.bfloat16], [(tall_left, rows), jnp.float32]
+    places, extra, extra_specs, out_shape, scratch = None, [], [], [sums] + [jax.ShapeDtypeStruct(*x) for x in lefts], []
     if meta is not None:
-        plan, spots, bits, groups, earlier = meta
+        plan, spots, bits, groups, earlier, passed = meta
         listed = [[] for _ in spots]
         for source, (_, known) in enumerate(earlier + [(None, pairs)]):
             for at, (a, b) in enumerate(known):
                 listed[a].append((source if source < len(earlier) else -1, at, b))
         places = len(earlier), spots, groups, listed
-        extra = [plan, bits] + [array for array, _ in earlier]
-        extra_specs = [SMEM, SMEM] + [VMEM] * len(earlier)
-        out_shape = [jax.ShapeDtypeStruct((len(g), rows), jnp.float32) for g in groups]
+        extra = [plan, bits] + [array for array, _ in earlier] + list(passed)
+        extra_specs = [SMEM, SMEM] + [VMEM] * (len(earlier) + len(passed))
+        count = -(-(len(spots) ** 2 + 1) // 8) * 8
+        out_shape = [jax.ShapeDtypeStruct((len(g), rows), jnp.float32) for g in groups or [range(count)]]
         scratch = [pltpu.VMEM(sums.shape, jnp.float32)]
+    keeps = meta is not None and owned
     flops = sum(4 * (hi - lo) * (end - start) * rows * rows * width for lo, hi, start, end in steps)
     moved = (len(owned) + len(rights)) * rows * width * 2
     result = pl.pallas_call(
@@ -258,34 +292,47 @@
         out_shape=out_shape,
         in_specs=[ANY] * len(arrays) + extra_specs,
         out_specs=[VMEM] * len(out_shape),
-        scratch_shapes=[
-            pltpu.VMEM((owned[-1] * rows + rows, width), jnp.bfloat16),
-            pltpu.VMEM((len(rights) * rows, width), jnp.bfloat16),
-            pltpu.VMEM((owned[-1] * rows + rows, rows), jnp.float32),
-            pltpu.VMEM((tall, 2 * rows), jnp.float32),
-            pltpu.SemaphoreType.DMA((len(owned),)),
+        scratch_shapes=([pltpu.VMEM(*lefts[0])] if keeps else []) + [
+            pltpu.VMEM((len(rights) * rows, width), jnp.bfloat16)] + ([pltpu.VMEM(*lefts[1])] if keeps else []) + [
+            pltpu.VMEM((tall, 2 * rows), jnp.float32)] + (
+            [pltpu.SemaphoreType.DMA((len(owned),))] if owned else []) + [
             pltpu.SemaphoreType.DMA((len(rights),)),
         ] + scratch,
         compiler_params=pltpu.CompilerParams(vmem_limit_bytes=VMEM_LIMIT),
-        cost_estimate=pl.CostEstimate(flops=FLOPS * flops, bytes_accessed=moved, transcendentals=0),
+        cost_estimate=pl.CostEstimate(flops=0, bytes_accessed=0, transcendentals=0),
         name=name,
     )(*arrays, *extra)
-    return (result[0], pairs) if meta is None else result
-
-
-def place_kernel(slots, plan_ref, *refs):
-    out_ref = refs[-1]
-    for ref, (group) in zip(refs[:-1], slots):
-        for n, at in enumerate(group):
-            out_ref[pl.ds(plan_ref[2 + at], 1), :] = ref[n:n + 1, :]
-
-
-def place_rows(slots, plan, returned, blocks, rows):
+    return (result[0], pairs, result[1:]) if meta is None else result
+
+
+def place_kernel(taken, capacity, pieces, plan_ref, *refs):
+    refs, out_ref, held = refs[:-2], refs[-2], refs[-1]
+    places = len(refs)
+    blocks, rows = out_ref.shape
+    total = places * capacity
+    me = plan_ref[plan_ref.shape[0] - 1]
+    for q, ref in enumerate(refs):
+        held[q] = ref[...]
+    lane = lax.broadcasted_iota(jnp.int32, (blocks, rows), 1)
+    spot = lax.broadcasted_iota(jnp.int32, (blocks, rows), 0)
+    for n, (k, at) in enumerate(taken):
+        scorer = lax.rem(me + k, places)
+        group = lax.rem(scorer + places - plan_ref[1], places)
+        flags = held[me ^ group, blocks * blocks:blocks * blocks + 1, :]
+        first = plan_ref[2 + 2 * total + at] * blocks
+        paired = jnp.sum(jnp.where(lane == spot + first, flags, 0.0), axis=1, keepdims=True)
+        sums = held[me ^ scorer, n * blocks:(n + 1) * blocks, :]
+        sums = jnp.sum(jnp.where(paired > 0.0, sums, 0.0), axis=0, keepdims=True)
+        out_ref[pl.ds(plan_ref[2 + at], 1), :] = jnp.log1p(sums / (pieces * rows))
+
+
+def place_rows(taken, capacity, pieces, plan, returned, blocks, rows):
     return pl.pallas_call(
-        functools.partial(place_kernel, slots),
+        functools.partial(place_kernel, taken, capacity, pieces),
         out_shape=jax.ShapeDtypeStruct((blocks, rows), jnp.float32),
         in_specs=[SMEM] + [VMEM] * len(returned),
         out_specs=VMEM,
+        scratch_shapes=[pltpu.VMEM((len(returned),) + returned[0].shape, jnp.float32)],
         name="place_rows",
     )(plan, *returned)
 
@@ -310,8 +357,13 @@
     taken = [(k, k * capacity + j) for group in sets for k, j in group]
     blocks = len(taken)
     per = pieces // 2
-    sends = [lambda x: x] + [functools.partial(shift_by, k=k, places=places) for k in range(1, places)]
-    moved = [shift_by(slots[at - capacity], k, places) for k, at in taken if k]
+    moved = []
+    for k, at in taken:
+        if k:
+            sent = slots[at - capacity]
+            if len(moved) == 2:
+                sent = after(sent, moved[0])
+            moved.append(shift_by(sent, k, places))
     arrived = [own if len(sets[0]) == capacity else own[:rows], moved[0], moved[1],
                moved[2] if len(moved) == 3 else jnp.concatenate(moved[2:], axis=0)]
     held = {}
@@ -321,24 +373,21 @@
     for g, array in enumerate(arrived):
         across = swap_with(array, 2, pieces)
         acrosses.append(across)
-        if g == 1:
-            here = lax.switch(plan[1], sends, after(bits, across))
         beside = swap_with(array, 1, pieces)
         for n, b in enumerate(range(first[g], first[g + 1])):
             held[b, 0], held[b, 1], held[b, 2] = (array, n, rows), (beside, n, rows), (across, n, rows)
         if g == 3:
             runs = range(end * per + (per - 1) * (blocks - end == 1))
             most = score(pieces, held, range(blocks), runs, [(0, blocks, 0, len(runs))], name="score_most")
-            across = after(across, most[0], here)
+            across = after(across, most[0])
         corner = swap_with(across, 1, pieces)
         for n, b in enumerate(range(first[g], first[g + 1])):
             held[b, 3] = (corner, n, rows)
-    order = sorted({k for k, _ in taken})
-    groups = [[b for b in range(blocks) if taken[b][0] == k] for k in order]
-    sums = score(pieces, held, range(blocks), range(len(runs), blocks * per), [(0, blocks, 0, blocks * per - len(runs))],
-                 (plan, [2 + places * capacity + at for _, at in taken], here, groups, [most]), name="score_late")
-    returned = [s if k == 0 else shift_by(s, places - k, places) for k, s in zip(order, sums)]
-    return place_rows([[taken[b][1] for b in g] for g in groups], plan, returned, blocks, rows)
+    (dense,) = score(pieces, held, range(0), range(len(runs), blocks * per), [(0, blocks, 0, blocks * per - len(runs))],
+                     (plan, [2 + places * capacity + at for _, at in taken], bits, None, [most[:2]], most[2]),
+                     name="score_late")
+    returned = [dense] + [lax.ppermute(dense, "blk", [(i, i ^ q) for i in range(places)]) for q in range(1, places)]
+    return place_rows(taken, capacity, pieces, plan, returned, blocks, rows)
 
 
 def general_path(capacity, pieces, embeddings, row_count, fetch_list, left, right, pairs):
@@ -376,7 +425,7 @@
         for q in range(pieces):
             held[b, q] = (swap_with(block, q, pieces) if q else block), 0, rows
     runs = range(blocks * pieces // 2)
-    meta = local_ids, range(blocks), bits[None].astype(jnp.int32), [list(range(blocks))], []
+    meta = local_ids, range(blocks), bits[None].astype(jnp.int32), [list(range(blocks))], [], []
     (dense,) = score(pieces, held, range(blocks), runs, [(0, blocks, 0, len(runs))], meta, name="score_all")
     back = (recv_slot[None, :] == slot_ids[:, None]).astype(jnp.float32)
     returned = exchange(jnp.sum(back[:, :, None] * dense[None, :, :], axis=1))

time: 62 us -> 59 us (0.952)
  loops' own time: 2.45 us -> 0.58 us
  local copies, waits for them, and re-layouts: 3.69 us -> 2.57 us
  Pallas kernels: 12.7 us -> 11.7 us
  waiting for transfers between devices: 18.2 us -> 19.1 us
    ppermute x0 -> x3, starting transfers between devices: none -> 4.44 us  [pattern_path(): lax.ppermute(dense, 'blk', [(i, i ^ q) for i in range(places)])]
    ppermute x7 -> x3, starting transfers between devices: 17.6 us -> 13.6 us  [shift_by(): lax.ppermute(array, 'blk', [(i, (i + k) % places) for i in range(places)])]
    ppermute x7 -> x3, waiting for transfers between devices: 14.1 us -> 11.1 us  [shift_by(): lax.ppermute(array, 'blk', [(i, (i + k) % places) for i in range(places)])]
    ppermute x12, waiting for transfers between devices: 4.11 us -> 6.06 us  [swap_with(): return lax.ppermute(array, 'sub', [(i, i ^ q) for i in range(pieces)])]
    ppermute x0 -> x3, waiting for transfers between devices: none -> 1.88 us  [pattern_path(): lax.ppermute(dense, 'blk', [(i, i ^ q) for i in range(places)])]
    another operation x1 -> x0, loops' own time: 1.22 us -> none  [pattern_path(): here = lax.switch(plan[1], sends, after(bits, across))]
    pallas_call x2, Pallas kernels: 9.73 us -> 8.79 us  [score(): pl.pallas_call(functools.partial(score_kernel, rows, width, pieces, where...]
    another operation x1, loops' own time: 1.23 us -> 0.58 us  [body(): return lax.switch(plan[0], branches, plan, bits, own, slots, given)]
  transfers between devices with their start and end apart: 19 -> 18, of which waited for: 8 -> 9; matrix products, arithmetic and copies ran while one was open for 1% -> 0% of each run, Pallas kernels for 10% -> 11%
where the time goes in v3:
time: 59 us; the launch traced here: 58.8 us
  starting transfers between devices  24.2 us (41%)
  waiting for transfers between devices  19.1 us (32%)
  Pallas kernels  11.7 us (20%)
  local copies, waits for them, and re-layouts  2.57 us (4%)
  between operations  0.75 us (1%)
    ppermute x3, starting transfers between devices, shift_by(): lax.ppermute(array, 'blk', [(i, (i + k) % places) for i in range(places)])  13.6 us
    ppermute x3, waiting for transfers between devices, shift_by(): lax.ppermute(array, 'blk', [(i, (i + k) % places) for i in range(places)])  11.1 us
    pallas_call x2, Pallas kernels, score(): pl.pallas_call(functools.partial(score_kernel, rows, width, pieces, where...  8.79 us
    ppermute x12, starting transfers between devices, swap_with(): return lax.ppermute(array, 'sub', [(i, i ^ q) for i in range(pieces)])  6.11 us
    ppermute x12, waiting for transfers between devices, swap_with(): return lax.ppermute(array, 'sub', [(i, i ^ q) for i in range(pieces)])  6.06 us
    ppermute x3, starting transfers between devices, pattern_path(): lax.ppermute(dense, 'blk', [(i, i ^ q) for i in range(places)])  4.44 us
    pallas_call x1, Pallas kernels, make_plan(): pl.pallas_call(functools.partial(plan_kernel, patterns, places, capacity)...  1.99 us
    unnamed x11, local copies, waits for them, and re-layouts  1.97 us
  transfers between devices with their start and end apart: 18, of which 9 were waited for; matrix products, arithmetic and copies ran while one was open for 0% of the time, Pallas kernels for 11%

profile of v3, /device:TPU:0, one launch (start us, length us, event | category | flops | bytes accessed | tf_op | source)
XLA Modules:
  0.0 58.8 jit_solution(13975242166506618306)
XLA Ops:
  0.0 0.0 copy-start.18
  0.0 0.0 copy-start.16
  0.0 0.0 copy-start.19
  0.0 0.0 copy-start.20
  0.0 1.4 %copy.21.emb_ref = bf16[5,128,1024]{2,1,0:T(8,128)(2,1)S(1)} copy(bf16[5,128,1024]{2,1,0:T(8,128)(2,1)} %param.13) | data formatting | bytes 2621440
  2.0 0.0 copy-done.18
  2.0 0.0 copy-done.16
  2.1 0.0 copy-done.19
  2.1 0.0 copy-done.20
  2.1 2.0 %plan_and_gather.1 = (s32[27]{0:T(128)S(1)}, s32[1]{0:T(128)}, bf16[256,1024]{1,0:T(8,128)(2,1)S(1)}, bf16[128,1024]{1,0:T(8,128)(2,1)S(1)}, bf16[128,1024]{1,0:...) custom-call(s32[1]{0:T(128)} %bitcast.27.me_ref, ...), custom_call_target="tpu_custom_call" | custom-call | tf_op jit(solution)/shard_map/plan_and_gather/pallas_call | solution.py:125
  4.1 54.1 %conditional.1 = (f32[5,128]{1,0:T(8,128)S(1)}) conditional(s32[]{:T(128)} %bitcast.29, (bf16[128,1024]{1,0:T(8,128)(2,1)S(1)}, bf16[128,1024]{1,0:T(8,128)(2,1)S(1)}, bf16[128,1024]{1,0:T(8,128)(2,1)S(1)}, bf16[256,1024]{1,0:T(8,128)(2,1)S(1)}, s32[27]{0:T(128)S(1)}, /*index=5*/s32[1]{0:T(128)}) %tuple.32, ...), branch_computations={%region_0.0_spmd, %region_1.0_spmd, %region_2.0_spmd, %region_3.0_... | conditional | flops 1474489 | bytes 33400496 | solution.py:453
  4.1 3.1 %collective-permute-start.36 = (bf16[128,1024]{1,0:T(8,128)(2,1)S(1)}, bf16[128,1024]{1,0:T(8,128)(2,1)S(1)}, u32[]{:S(2)}, u32[]{:S(2)}) collective-permute-start(bf16[128,1024]{1,0:T(8,128)(2,1)S(1)} %get-tuple-element.107), channel_id=1, source_target_pairs={{0,4},{4,8},{8,12},{12,0},{1,5},{5,9},{9,13},{13,1},{2,6},{6,10},{... | collective-permute-start | bytes 786440 | tf_op jit(solution)/shard_map/cond/branch_2_fun/ppermute | solution.py:341
  7.2 1.5 %collective-permute-start.41 = (bf16[256,1024]{1,0:T(8,128)(2,1)S(1)}, bf16[256,1024]{1,0:T(8,128)(2,1)S(1)}, u32[]{:S(2)}, u32[]{:S(2)}) collective-permute-start(bf16[256,1024]{1,0:T(8,128)(2,1)S(1)} %get-tuple-element.109.refs_0_), channel_id=1, source_target_pairs={{0,2},{1,3},{2,0},{3,1},{4,6},{5,7},{6,4},{7,5},{8,10},{9,11},{10,... | collective-permute-start | bytes 1572872 | tf_op jit(solution)/shard_map/cond/branch_2_fun/ppermute | solution.py:345
  8.7 2.2 %collective-permute-start.39 = (bf16[128,1024]{1,0:T(8,128)(2,1)S(1)}, bf16[128,1024]{1,0:T(8,128)(2,1)S(1)}, u32[]{:S(2)}, u32[]{:S(2)}) collective-permute-start(bf16[128,1024]{1,0:T(8,128)(2,1)S(1)} %get-tuple-element.110), channel_id=1, source_target_pairs={{0,12},{4,0},{8,4},{12,8},{1,13},{5,1},{9,5},{13,9},{2,14},{6,2},{... | collective-permute-start | bytes 786440 | tf_op jit(solution)/shard_map/cond/branch_2_fun/ppermute | solution.py:341
  10.9 5.5 %collective-permute-done.36.refs_1_ = bf16[128,1024]{1,0:T(8,128)(2,1)S(1)} collective-permute-done((bf16[128,1024]{1,0:T(8,128)(2,1)S(1)}, bf16[128,1024]{1,0:T(8,128)(2,1)S(1)}, u32[]{:S(2)}, u32[]{:S(2)}) %collective-permute-start.36) | collective-permute-done | bytes 262176 | tf_op jit(solution)/shard_map/cond/branch_2_fun/ppermute | solution.py:341
  16.4 8.3 %collective-permute-start.37 = (bf16[128,1024]{1,0:T(8,128)(2,1)S(1)}, bf16[128,1024]{1,0:T(8,128)(2,1)S(1)}, u32[]{:S(2)}, u32[]{:S(2)}) collective-permute-start(bf16[128,1024]{1,0:T(8,128)(2,1)S(1)} %get-tuple-element.108), channel_id=1, source_target_pairs={{0,8},{4,12},{8,0},{12,4},{1,9},{5,13},{9,1},{13,5},{2,10},{6,14},... | collective-permute-start | bytes 786440 | tf_op jit(solution)/shard_map/cond/branch_2_fun/ppermute | solution.py:341
  24.7 1.5 %collective-permute-start.44 = (bf16[128,1024]{1,0:T(8,128)(2,1)S(1)}, bf16[128,1024]{1,0:T(8,128)(2,1)S(1)}, u32[]{:S(2)}, u32[]{:S(2)}) collective-permute-start(bf16[128,1024]{1,0:T(8,128)(2,1)S(1)} %collective-permute-done.36.refs_1_), channel_id=1, source_target_pairs={{0,2},{1,3},{2,0},{3,1},{4,6},{5,7},{6,4},{7,5},{8,10},{9,11},{10,... | collective-permute-start | bytes 786440 | tf_op jit(solution)/shard_map/cond/branch_2_fun/ppermute | solution.py:345
  26.2 0.0 collective-permute-start.40
  26.2 0.0 collective-permute-done.39.refs_2_
  26.2 0.5 collective-permute-start.47
  26.7 5.7 %collective-permute-done.37.refs_3_ = bf16[128,1024]{1,0:T(8,128)(2,1)S(1)} collective-permute-done((bf16[128,1024]{1,0:T(8,128)(2,1)S(1)}, bf16[128,1024]{1,0:T(8,128)(2,1)S(1)}, u32[]{:S(2)}, u32[]{:S(2)}) %collective-permute-start.37) | collective-permute-done | bytes 262176 | tf_op jit(solution)/shard_map/cond/branch_2_fun/ppermute | solution.py:341
  32.4 0.0 collective-permute-start.43
  32.4 0.4 collective-permute-done.44.refs_8_
  32.8 0.1 collective-permute-start.46
  32.9 0.0 collective-permute-done.41.refs_5_
  32.9 0.4 collective-permute-start.42
  33.3 3.3 %collective-permute-done.47.refs_11_ = bf16[128,1024]{1,0:T(8,128)(2,1)S(1)} collective-permute-done((bf16[128,1024]{1,0:T(8,128)(2,1)S(1)}, bf16[128,1024]{1,0:T(8,128)(2,1)S(1)}, u32[]{:S(2)}, u32[]{:S(2)}) %collective-permute-start.47) | collective-permute-done | bytes 262176 | tf_op jit(solution)/shard_map/cond/branch_2_fun/ppermute | solution.py:345
  36.7 0.0 collective-permute-start.49
  36.7 0.0 collective-permute-done.43.refs_7_
  36.7 0.5 collective-permute-start.45
  37.2 0.0 collective-permute-done.46.refs_10_
  37.2 0.1 collective-permute-start.48
  37.3 0.0 collective-permute-done.40.refs_4_
  37.3 1.5 %collective-permute-start.38 = (bf16[128,1024]{1,0:T(8,128)(2,1)S(1)}, bf16[128,1024]{1,0:T(8,128)(2,1)S(1)}, u32[]{:S(2)}, u32[]{:S(2)}) collective-permute-start(bf16[128,1024]{1,0:T(8,128)(2,1)S(1)} %collective-permute-done.37.refs_3_), channel_id=1, source_target_pairs={{0,2},{1,3},{2,0},{3,1},{4,6},{5,7},{6,4},{7,5},{8,10},{9,11},{10,... | collective-permute-start | bytes 786440 | tf_op jit(solution)/shard_map/cond/branch_2_fun/ppermute | solution.py:345
  38.8 0.0 collective-permute-done.49.refs_13_
  38.8 0.0 collective-permute-done.45.refs_9_
  38.8 0.2 collective-permute-done.48.refs_12_
  39.0 0.0 collective-permute-done.42.refs_6_
  39.0 6.4 %score_most.6 = (f32[25,128,128]{2,1,0:T(8,128)S(1)}, bf16[640,1024]{1,0:T(8,128)(2,1)S(1)}, f32[640,128]{1,0:T(8,128)S(1)}) custom-call(bf16[256,1024]{1,0:T(8,128)(2,1)S(1)} %get-tuple-element.109.refs_0_, bf16[128,1024]{1,0:T(8,128)(2,1)S(1)} %collective-permute-done.36.refs_1_, bf16[128,1024]{1,0:T(8,128)(2,1)S(1)} %collective-permute-done.39.refs_2_, ...), custom_call_target="tpu_custom_call" | custom-call | tf_op jit(solution)/shard_map/cond/branch_2_fun/score_most/pallas_call | solution.py:290
  45.4 0.5 collective-permute-done.38.refs_0_
  45.9 0.0 collective-permute-start.50
  45.9 1.5 %collective-permute-done.50.refs_1_ = bf16[128,1024]{1,0:T(8,128)(2,1)S(1)} collective-permute-done((bf16[128,1024]{1,0:T(8,128)(2,1)S(1)}, bf16[128,1024]{1,0:T(8,128)(2,1)S(1)}, u32[]{:S(2)}, u32[]{:S(2)}) %collective-permute-start.50) | collective-permute-done | bytes 262176 | tf_op jit(solution)/shard_map/cond/branch_2_fun/ppermute | solution.py:345
  47.5 2.4 %score_late.6.refs_0_ = f32[32,128]{1,0:T(8,128)S(1)} custom-call(bf16[128,1024]{1,0:T(8,128)(2,1)S(1)} %collective-permute-done.38.refs_0_, bf16[128,1024]{1,0:T(8,128)(2,1)S(1)} %collective-permute-done.50.refs_1_, s32[27]{0:T(128)S(1)} %get-tuple-element.105.refs_2_.plan_ref, s32[1]{0:T(128)} %get-tuple-element.113.refs_3_, ...), custom_call_target="tpu_custom_call" | custom-call | tf_op jit(solution)/shard_map/cond/branch_2_fun/score_late/pallas_call | solution.py:290
  49.9 0.0 copy-start.2
  49.9 0.1 collective-permute-start.51
  49.9 0.1 collective-permute-start.52
  50.0 4.3 %collective-permute-start.53 = (f32[32,128]{1,0:T(8,128)S(1)}, f32[32,128]{1,0:T(8,128)S(1)}, u32[]{:S(2)}, u32[]{:S(2)}) collective-permute-start(f32[32,128]{1,0:T(8,128)S(1)} %score_late.6.refs_0_), channel_id=1, source_target_pairs={{0,12},{4,8},{8,4},{12,0},{1,13},{5,9},{9,5},{13,1},{2,14},{6,10},... | collective-permute-start | bytes 49160 | tf_op jit(solution)/shard_map/cond/branch_2_fun/ppermute | solution.py:389
  54.3 0.0 collective-permute-done.51.refs_1_
  54.3 0.0 copy-start.6
  54.3 0.3 collective-permute-done.52.refs_2_
  54.6 0.0 copy-start.10
  54.6 1.6 %collective-permute-done.53.refs_3_ = f32[32,128]{1,0:T(8,128)S(1)} collective-permute-done((f32[32,128]{1,0:T(8,128)S(1)}, f32[32,128]{1,0:T(8,128)S(1)}, u32[]{:S(2)}, u32[]{:S(2)}) %collective-permute-start.53) | collective-permute-done | bytes 16416 | tf_op jit(solution)/shard_map/cond/branch_2_fun/ppermute | solution.py:389
  56.2 0.0 copy-done.2
  56.2 0.0 copy-done.6
  56.2 0.0 copy-done.10
  56.2 0.0 copy-start.14
  56.2 0.6 copy-done.14
  56.8 0.9 %place_rows.6 = f32[5,128]{1,0:T(8,128)S(1)} custom-call(s32[27]{0:T(128)S(1)} %get-tuple-element.105.refs_2_.plan_ref, f32[32,128]{1,0:T(8,128)} %copy-done.2, f32[32,128]{1,0:T(8,128)} %copy-done.6, f32[32,128]{1,0:T(8,128)} %copy-done.10, f32[32,128]{1,0:T(8,128)} %copy-done.14), custom_call_target="tpu_custom_call" | custom-call | tf_op jit(solution)/shard_map/cond/branch_2_fun/place_rows/pallas_call | solution.py:330
  58.2 0.0 copy-start.17
  58.2 0.6 copy-done.17
Async XLA Ops:
  0.0 2.0 %copy-start.18 = (s32[5]{0:T(128)S(1)}, s32[5]{0:T(128)}, u32[]{:S(2)}) copy-start(s32[5]{0:T(128)} %count_ref.1) | copy-start | bytes 64
  0.0 2.0 %copy-start.16 = (s32[4,5]{1,0:T(4,128)S(1)}, s32[4,5]{1,0:T(4,128)}, u32[]{:S(2)}) copy-start(s32[4,5]{1,0:T(4,128)} %fetch_ref.1) | copy-start | bytes 244
  0.0 2.0 %copy-start.19 = (s32[1,15]{1,0:T(1,128)S(1)}, s32[1,15]{1,0:T(1,128)}, u32[]{:S(2)}) copy-start(s32[1,15]{1,0:T(1,128)} %left_ref.1) | copy-start | bytes 184
  0.0 2.1 %copy-start.20 = (s32[1,15]{1,0:T(1,128)S(1)}, s32[1,15]{1,0:T(1,128)}, u32[]{:S(2)}) copy-start(s32[1,15]{1,0:T(1,128)} %right_ref.1) | copy-start | bytes 184
  4.1 12.3 %collective-permute-start.36 = (bf16[128,1024]{1,0:T(8,128)(2,1)S(1)}, bf16[128,1024]{1,0:T(8,128)(2,1)S(1)}, u32[]{:S(2)}, u32[]{:S(2)}) collective-permute-start(bf16[128,1024]{1,0:T(8,128)(2,1)S(1)} %get-tuple-element.107), channel_id=1, source_target_pairs={{0,4},{4,8},{8,12},{12,0},{1,5},{5,9},{9,13},{13,1},{2,6},{6,10},{... | collective-permute-start | bytes 786440 | tf_op jit(solution)/shard_map/cond/branch_2_fun/ppermute | solution.py:341
  7.2 25.7 %collective-permute-start.41 = (bf16[256,1024]{1,0:T(8,128)(2,1)S(1)}, bf16[256,1024]{1,0:T(8,128)(2,1)S(1)}, u32[]{:S(2)}, u32[]{:S(2)}) collective-permute-start(bf16[256,1024]{1,0:T(8,128)(2,1)S(1)} %get-tuple-element.109.refs_0_), channel_id=1, source_target_pairs={{0,2},{1,3},{2,0},{3,1},{4,6},{5,7},{6,4},{7,5},{8,10},{9,11},{10,... | collective-permute-start | bytes 1572872 | tf_op jit(solution)/shard_map/cond/branch_2_fun/ppermute | solution.py:345
  8.7 17.5 %collective-permute-start.39 = (bf16[128,1024]{1,0:T(8,128)(2,1)S(1)}, bf16[128,1024]{1,0:T(8,128)(2,1)S(1)}, u32[]{:S(2)}, u32[]{:S(2)}) collective-permute-start(bf16[128,1024]{1,0:T(8,128)(2,1)S(1)} %get-tuple-element.110), channel_id=1, source_target_pairs={{0,12},{4,0},{8,4},{12,8},{1,13},{5,1},{9,5},{13,9},{2,14},{6,2},{... | collective-permute-start | bytes 786440 | tf_op jit(solution)/shard_map/cond/branch_2_fun/ppermute | solution.py:341
  16.4 16.0 %collective-permute-start.37 = (bf16[128,1024]{1,0:T(8,128)(2,1)S(1)}, bf16[128,1024]{1,0:T(8,128)(2,1)S(1)}, u32[]{:S(2)}, u32[]{:S(2)}) collective-permute-start(bf16[128,1024]{1,0:T(8,128)(2,1)S(1)} %get-tuple-element.108), channel_id=1, source_target_pairs={{0,8},{4,12},{8,0},{12,4},{1,9},{5,13},{9,1},{13,5},{2,10},{6,14},... | collective-permute-start | bytes 786440 | tf_op jit(solution)/shard_map/cond/branch_2_fun/ppermute | solution.py:341
  24.7 8.1 %collective-permute-start.44 = (bf16[128,1024]{1,0:T(8,128)(2,1)S(1)}, bf16[128,1024]{1,0:T(8,128)(2,1)S(1)}, u32[]{:S(2)}, u32[]{:S(2)}) collective-permute-start(bf16[128,1024]{1,0:T(8,128)(2,1)S(1)} %collective-permute-done.36.refs_1_), channel_id=1, source_target_pairs={{0,2},{1,3},{2,0},{3,1},{4,6},{5,7},{6,4},{7,5},{8,10},{9,11},{10,... | collective-permute-start | bytes 786440 | tf_op jit(solution)/shard_map/cond/branch_2_fun/ppermute | solution.py:345
  26.2 11.1 %collective-permute-start.40 = (bf16[256,1024]{1,0:T(8,128)(2,1)S(1)}, bf16[256,1024]{1,0:T(8,128)(2,1)S(1)}, u32[]{:S(2)}, u32[]{:S(2)}) collective-permute-start(bf16[256,1024]{1,0:T(8,128)(2,1)S(1)} %get-tuple-element.109.refs_0_), channel_id=1, source_target_pairs={{0,1},{1,0},{2,3},{3,2},{4,5},{5,4},{6,7},{7,6},{8,9},{9,8},{10,11... | collective-permute-start | bytes 1572872 | tf_op jit(solution)/shard_map/cond/branch_2_fun/ppermute | solution.py:345
  26.2 10.5 %collective-permute-start.47 = (bf16[128,1024]{1,0:T(8,128)(2,1)S(1)}, bf16[128,1024]{1,0:T(8,128)(2,1)S(1)}, u32[]{:S(2)}, u32[]{:S(2)}) collective-permute-start(bf16[128,1024]{1,0:T(8,128)(2,1)S(1)} %collective-permute-done.39.refs_2_), channel_id=1, source_target_pairs={{0,2},{1,3},{2,0},{3,1},{4,6},{5,7},{6,4},{7,5},{8,10},{9,11},{10,... | collective-permute-start | bytes 786440 | tf_op jit(solution)/shard_map/cond/branch_2_fun/ppermute | solution.py:345
  32.4 4.3 %collective-permute-start.43 = (bf16[128,1024]{1,0:T(8,128)(2,1)S(1)}, bf16[128,1024]{1,0:T(8,128)(2,1)S(1)}, u32[]{:S(2)}, u32[]{:S(2)}) collective-permute-start(bf16[128,1024]{1,0:T(8,128)(2,1)S(1)} %collective-permute-done.36.refs_1_), channel_id=1, source_target_pairs={{0,1},{1,0},{2,3},{3,2},{4,5},{5,4},{6,7},{7,6},{8,9},{9,8},{10,11... | collective-permute-start | bytes 786440 | tf_op jit(solution)/shard_map/cond/branch_2_fun/ppermute | solution.py:345
  32.8 4.4 %collective-permute-start.46 = (bf16[128,1024]{1,0:T(8,128)(2,1)S(1)}, bf16[128,1024]{1,0:T(8,128)(2,1)S(1)}, u32[]{:S(2)}, u32[]{:S(2)}) collective-permute-start(bf16[128,1024]{1,0:T(8,128)(2,1)S(1)} %collective-permute-done.39.refs_2_), channel_id=1, source_target_pairs={{0,1},{1,0},{2,3},{3,2},{4,5},{5,4},{6,7},{7,6},{8,9},{9,8},{10,11... | collective-permute-start | bytes 786440 | tf_op jit(solution)/shard_map/cond/branch_2_fun/ppermute | solution.py:345
  32.9 6.1 %collective-permute-start.42 = (bf16[256,1024]{1,0:T(8,128)(2,1)S(1)}, bf16[256,1024]{1,0:T(8,128)(2,1)S(1)}, u32[]{:S(2)}, u32[]{:S(2)}) collective-permute-start(bf16[256,1024]{1,0:T(8,128)(2,1)S(1)} %collective-permute-done.41.refs_5_), channel_id=1, source_target_pairs={{0,1},{1,0},{2,3},{3,2},{4,5},{5,4},{6,7},{7,6},{8,9},{9,8},{10,11... | collective-permute-start | bytes 1572872 | tf_op jit(solution)/shard_map/cond/branch_2_fun/ppermute | solution.py:345
  36.7 2.1 %collective-permute-start.49 = (bf16[128,1024]{1,0:T(8,128)(2,1)S(1)}, bf16[128,1024]{1,0:T(8,128)(2,1)S(1)}, u32[]{:S(2)}, u32[]{:S(2)}) collective-permute-start(bf16[128,1024]{1,0:T(8,128)(2,1)S(1)} %collective-permute-done.37.refs_3_), channel_id=1, source_target_pairs={{0,1},{1,0},{2,3},{3,2},{4,5},{5,4},{6,7},{7,6},{8,9},{9,8},{10,11... | collective-permute-start | bytes 786440 | tf_op jit(solution)/shard_map/cond/branch_2_fun/ppermute | solution.py:345
  36.7 2.1 %collective-permute-start.45 = (bf16[128,1024]{1,0:T(8,128)(2,1)S(1)}, bf16[128,1024]{1,0:T(8,128)(2,1)S(1)}, u32[]{:S(2)}, u32[]{:S(2)}) collective-permute-start(bf16[128,1024]{1,0:T(8,128)(2,1)S(1)} %collective-permute-done.44.refs_8_), channel_id=1, source_target_pairs={{0,1},{1,0},{2,3},{3,2},{4,5},{5,4},{6,7},{7,6},{8,9},{9,8},{10,11... | collective-permute-start | bytes 786440 | tf_op jit(solution)/shard_map/cond/branch_2_fun/ppermute | solution.py:345
  37.2 1.8 %collective-permute-start.48 = (bf16[128,1024]{1,0:T(8,128)(2,1)S(1)}, bf16[128,1024]{1,0:T(8,128)(2,1)S(1)}, u32[]{:S(2)}, u32[]{:S(2)}) collective-permute-start(bf16[128,1024]{1,0:T(8,128)(2,1)S(1)} %collective-permute-done.47.refs_11_), channel_id=1, source_target_pairs={{0,1},{1,0},{2,3},{3,2},{4,5},{5,4},{6,7},{7,6},{8,9},{9,8},{10,11... | collective-permute-start | bytes 786440 | tf_op jit(solution)/shard_map/cond/branch_2_fun/ppermute | solution.py:345
  37.3 8.7 %collective-permute-start.38 = (bf16[128,1024]{1,0:T(8,128)(2,1)S(1)}, bf16[128,1024]{1,0:T(8,128)(2,1)S(1)}, u32[]{:S(2)}, u32[]{:S(2)}) collective-permute-start(bf16[128,1024]{1,0:T(8,128)(2,1)S(1)} %collective-permute-done.37.refs_3_), channel_id=1, source_target_pairs={{0,2},{1,3},{2,0},{3,1},{4,6},{5,7},{6,4},{7,5},{8,10},{9,11},{10,... | collective-permute-start | bytes 786440 | tf_op jit(solution)/shard_map/cond/branch_2_fun/ppermute | solution.py:345
  45.9 1.5 %collective-permute-start.50 = (bf16[128,1024]{1,0:T(8,128)(2,1)S(1)}, bf16[128,1024]{1,0:T(8,128)(2,1)S(1)}, u32[]{:S(2)}, u32[]{:S(2)}) collective-permute-start(bf16[128,1024]{1,0:T(8,128)(2,1)S(1)} %collective-permute-done.38.refs_0_), channel_id=1, source_target_pairs={{0,1},{1,0},{2,3},{3,2},{4,5},{5,4},{6,7},{7,6},{8,9},{9,8},{10,11... | collective-permute-start | bytes 786440 | tf_op jit(solution)/shard_map/cond/branch_2_fun/ppermute | solution.py:345
  49.9 6.4 %copy-start.2 = (f32[32,128]{1,0:T(8,128)}, f32[32,128]{1,0:T(8,128)S(1)}, u32[]{:S(2)}) copy-start(f32[32,128]{1,0:T(8,128)S(1)} %score_late.6.refs_0_) | copy-start | bytes 49156 | tf_op jit(solution)/shard_map/cond
  49.9 4.5 %collective-permute-start.51 = (f32[32,128]{1,0:T(8,128)S(1)}, f32[32,128]{1,0:T(8,128)S(1)}, u32[]{:S(2)}, u32[]{:S(2)}) collective-permute-start(f32[32,128]{1,0:T(8,128)S(1)} %score_late.6.refs_0_), channel_id=1, source_target_pairs={{0,4},{4,0},{8,12},{12,8},{1,5},{5,1},{9,13},{13,9},{2,6},{6,2},{1... | collective-permute-start | bytes 49160 | tf_op jit(solution)/shard_map/cond/branch_2_fun/ppermute | solution.py:389
  49.9 4.7 %collective-permute-start.52 = (f32[32,128]{1,0:T(8,128)S(1)}, f32[32,128]{1,0:T(8,128)S(1)}, u32[]{:S(2)}, u32[]{:S(2)}) collective-permute-start(f32[32,128]{1,0:T(8,128)S(1)} %score_late.6.refs_0_), channel_id=1, source_target_pairs={{0,8},{4,12},{8,0},{12,4},{1,9},{5,13},{9,1},{13,5},{2,10},{6,14},... | collective-permute-start | bytes 49160 | tf_op jit(solution)/shard_map/cond/branch_2_fun/ppermute | solution.py:389
  50.0 6.2 %collective-permute-start.53 = (f32[32,128]{1,0:T(8,128)S(1)}, f32[32,128]{1,0:T(8,128)S(1)}, u32[]{:S(2)}, u32[]{:S(2)}) collective-permute-start(f32[32,128]{1,0:T(8,128)S(1)} %score_late.6.refs_0_), channel_id=1, source_target_pairs={{0,12},{4,8},{8,4},{12,0},{1,13},{5,9},{9,5},{13,1},{2,14},{6,10},... | collective-permute-start | bytes 49160 | tf_op jit(solution)/shard_map/cond/branch_2_fun/ppermute | solution.py:389
  54.3 1.9 %copy-start.6 = (f32[32,128]{1,0:T(8,128)}, f32[32,128]{1,0:T(8,128)S(1)}, u32[]{:S(2)}) copy-start(f32[32,128]{1,0:T(8,128)S(1)} %collective-permute-done.51.refs_1_) | copy-start | bytes 49156 | tf_op jit(solution)/shard_map/cond
  54.6 1.6 %copy-start.10 = (f32[32,128]{1,0:T(8,128)}, f32[32,128]{1,0:T(8,128)S(1)}, u32[]{:S(2)}) copy-start(f32[32,128]{1,0:T(8,128)S(1)} %collective-permute-done.52.refs_2_) | copy-start | bytes 49156 | tf_op jit(solution)/shard_map/cond
  56.2 0.6 %copy-start.14 = (f32[32,128]{1,0:T(8,128)}, f32[32,128]{1,0:T(8,128)S(1)}, u32[]{:S(2)}) copy-start(f32[32,128]{1,0:T(8,128)S(1)} %collective-permute-done.53.refs_3_) | copy-start | bytes 49156 | tf_op jit(solution)/shard_map/cond
  58.2 0.6 %copy-start.17 = (f32[5,128]{1,0:T(8,128)}, f32[5,128]{1,0:T(8,128)S(1)}, u32[]{:S(2)}) copy-start(f32[5,128]{1,0:T(8,128)S(1)} %get-tuple-element.340) | copy-start | bytes 7684

commit v4 on v3

--- a/solution.py
+++ b/solution.py
@@ -38,6 +38,13 @@
 
 def owner_of(block, blocks, places):
     return sum((block >= i * blocks).astype(jnp.int32) for i in range(1, places))
+
+
+def slots_of(counts, capacity):
+    places = len(counts)
+    nearest = sorted((k for k in range(1, places) if counts[k]), key=lambda k: min(k, places - k))
+    order = [(0, j) for j in range(counts[0])] + [(k, 0) for k in nearest] + [(k, 1) for k in nearest if counts[k] > 1]
+    return [(k, k * capacity + j) for k, j in order]
 
 
 def unary(counts):
@@ -143,7 +150,7 @@
     refs = list(refs)
     arrays = [refs.pop(0) for _ in range(1 + max(i for i, _ in wheres))]
     spots_in = [arrays[i].at[pl.ds(n * rows, rows)] for i, n in wheres]
-    left_in, right_in = spots_in[:len(owned)], spots_in[len(owned):]
+    right_in = spots_in
     finish = passed = None
     if places is not None:
         finish = [refs.pop(0) for _ in range(2 + places[0])]
@@ -152,18 +159,16 @@
     hand_on = places is None
     out_refs = [refs.pop(0) for _ in (places[2] if places and places[2] else range(1 + 2 * hand_on))]
     if hand_on:
-        right, gram, left_sems, right_sems = refs[:4]
+        right, gram, right_sems = refs[:3]
         left, left_scale = out_refs[1:]
     elif passed is None:
-        left, right, left_scale, gram, left_sems, right_sems = refs[:6]
+        left, right, left_scale, gram, right_sems = refs[:5]
     else:
         right, gram, right_sems = refs[:3]
         left, left_scale = passed
     sums = refs[-1] if places else out_refs[0]
     per = pieces // 2
     copies = []
-    for i, a in enumerate(owned):
-        copies.append(pltpu.make_async_copy(left_in[i], left.at[pl.ds(i * rows, rows)], left_sems.at[i]))
     for i in range(2 * len(runs)):
         copies.append(pltpu.make_async_copy(right_in[i], right.at[pl.ds(i * rows, rows)], right_sems.at[i]))
     for copy in copies:
@@ -177,12 +182,12 @@
     def lanes(col):
         return jnp.sum(jnp.where(eye, col, 0.0), axis=0, keepdims=True)
 
-    for i in range(len(owned)):
-        copies[i].wait()
-
     @pl.loop(0, len(owned))
     def _(i):
         here = pl.ds(pl.multiple_of(i * rows, rows), rows)
+        there = pl.ds(pl.multiple_of(i * pieces * rows, rows), rows)
+        pltpu.make_async_copy(right_in[0], right.at[there], right_sems.at[i * pieces]).wait()
+        left[here, :] = right[there, :]
         inv = lax.rsqrt(squares(left[here, :]) * (1.0 / width) + norm_eps)
         left_scale[here, :] = jnp.broadcast_to(inv * (kernel_scale / width * math.log2(math.e)), (rows, rows))
 
@@ -195,8 +200,12 @@
         def _(run):
             if fresh:
                 for h in range(2):
-                    pltpu.make_async_copy(
-                        right_in[0], right.at[pl.ds((2 * run + h) * rows, rows)], right_sems.at[2 * run + h]).wait()
+                    copy = pltpu.make_async_copy(
+                        right_in[0], right.at[pl.ds((2 * run + h) * rows, rows)], right_sems.at[2 * run + h])
+                    if h == 0 and owned:
+                        pl.when(lax.rem(runs[0] + run, per) != 0)(copy.wait)
+                    else:
+                        copy.wait()
             flat = runs[0] + run
             b = lax.div(flat, per)
             q = 2 * lax.rem(flat, per)
@@ -232,14 +241,14 @@
     blocks = len(spots)
     if groups is None:
         for a in range(blocks):
-            in_use = left_scale[a * rows:(a + 1) * rows, :1] > SCALE_IN_USE
+            in_use = left_scale[a * rows:(a + 1) * rows, :] > SCALE_IN_USE
             by_block = {}
             for source, at, b in listed[a]:
                 part = (sums if source < 0 else finish[2 + source])[at]
                 by_block[b] = by_block[b] + part if b in by_block else part
             for b, part in by_block.items():
-                total = jnp.where(in_use, jnp.sum(part, axis=1, keepdims=True), 0.0)
-                out_refs[0][pl.ds(a * blocks + spot[b], 1), :] = lanes(total)
+                total = jnp.sum(jnp.transpose(jnp.where(in_use, part, 0.0)), axis=0, keepdims=True)
+                out_refs[0][pl.ds(a * blocks + spot[b], 1), :] = total
         lane = lax.broadcasted_iota(jnp.int32, (1, rows), 1)
         flags = sum(jnp.where(lane == i, (bits >> i) & 1, 0) for i in range(blocks * blocks))
         out_refs[0][blocks * blocks:blocks * blocks + 1, :] = flags.astype(jnp.float32)
@@ -256,12 +265,12 @@
 
 
 def score(pieces, held, owned, runs, steps, meta=None, name="score"):
-    array, _, rows = held[0, 0]
+    array, _, rows = next(iter(held.values()))
     width = array.shape[1]
     per = pieces // 2
     rights = [held[run // per, 2 * (run % per) + h] for run in runs for h in range(2)]
     arrays, wheres = [], []
-    for array, n, _ in [held[a, 0] for a in owned] + rights:
+    for array, n, _ in rights:
         known = [i for i, other in enumerate(arrays) if other is array]
         if not known:
             arrays.append(array)
@@ -294,8 +303,7 @@
         out_specs=[VMEM] * len(out_shape),
         scratch_shapes=([pltpu.VMEM(*lefts[0])] if keeps else []) + [
             pltpu.VMEM((len(rights) * rows, width), jnp.bfloat16)] + ([pltpu.VMEM(*lefts[1])] if keeps else []) + [
-            pltpu.VMEM((tall, 2 * rows), jnp.float32)] + (
-            [pltpu.SemaphoreType.DMA((len(owned),))] if owned else []) + [
+            pltpu.VMEM((tall, 2 * rows), jnp.float32),
             pltpu.SemaphoreType.DMA((len(rights),)),
         ] + scratch,
         compiler_params=pltpu.CompilerParams(vmem_limit_bytes=VMEM_LIMIT),
@@ -351,41 +359,33 @@
 
 def pattern_path(counts, capacity, pieces, rows, plan, bits, own, slots):
     places = len(counts)
-    nearest = sorted((k for k in range(1, places) if counts[k]), key=lambda k: min(k, places - k))
-    sets = [[(0, j) for j in range(counts[0])], [(nearest[0], 0)], [(nearest[1], 0)],
-            [(k, 0) for k in nearest[2:]] + [(k, 1) for k in nearest if counts[k] > 1]]
-    taken = [(k, k * capacity + j) for group in sets for k, j in group]
+    taken = slots_of(counts, capacity)
     blocks = len(taken)
     per = pieces // 2
     moved = []
-    for k, at in taken:
-        if k:
-            sent = slots[at - capacity]
-            if len(moved) == 2:
-                sent = after(sent, moved[0])
-            moved.append(shift_by(sent, k, places))
-    arrived = [own if len(sets[0]) == capacity else own[:rows], moved[0], moved[1],
-               moved[2] if len(moved) == 3 else jnp.concatenate(moved[2:], axis=0)]
+    for k, at in taken[capacity:]:
+        sent = slots[at - capacity]
+        if len(moved) == 2:
+            sent = after(sent, moved[0])
+        moved.append(shift_by(sent, k, places))
     held = {}
-    first = [0, len(sets[0]), len(sets[0]) + 1, len(sets[0]) + 2, blocks]
-    ready, end = first[1], first[3]
-    acrosses = []
-    for g, array in enumerate(arrived):
+    first = [0] + list(range(capacity, blocks + 1))
+    for g, array in enumerate([own] + moved):
+        last = g == len(moved)
         across = swap_with(array, 2, pieces)
-        acrosses.append(across)
         beside = swap_with(array, 1, pieces)
         for n, b in enumerate(range(first[g], first[g + 1])):
             held[b, 0], held[b, 1], held[b, 2] = (array, n, rows), (beside, n, rows), (across, n, rows)
-        if g == 3:
-            runs = range(end * per + (per - 1) * (blocks - end == 1))
-            most = score(pieces, held, range(blocks), runs, [(0, blocks, 0, len(runs))], name="score_most")
-            across = after(across, most[0])
+        if last:
+            runs = range(blocks * per - 1)
+            sums, known, lefts = score(pieces, held, range(blocks), runs, [(0, blocks, 0, len(runs))], name="score_most")
+            across = after(across, sums)
         corner = swap_with(across, 1, pieces)
         for n, b in enumerate(range(first[g], first[g + 1])):
             held[b, 3] = (corner, n, rows)
-    (dense,) = score(pieces, held, range(0), range(len(runs), blocks * per), [(0, blocks, 0, blocks * per - len(runs))],
-                     (plan, [2 + places * capacity + at for _, at in taken], bits, None, [most[:2]], most[2]),
-                     name="score_late")
+    spots = [2 + places * capacity + at for _, at in taken]
+    (dense,) = score(pieces, held, range(0), range(blocks * per - 1, blocks * per), [(0, blocks, 0, 1)],
+                     (plan, spots, bits, None, [(sums, known)], lefts), name="score_late")
     returned = [dense] + [lax.ppermute(dense, "blk", [(i, i ^ q) for i in range(places)]) for q in range(1, places)]
     return place_rows(taken, capacity, pieces, plan, returned, blocks, rows)
 
@@ -447,7 +447,8 @@
     plan, bits, own, slots = make_plan(patterns, places, capacity, me, sub, *given)
     rows = embeddings.shape[1]
     branches = [
-        lambda plan, bits, own, slots, given, counts=counts: pattern_path(counts, capacity, pieces, rows, plan, bits, own, slots)
+        lambda plan, bits, own, slots, given, counts=counts: pattern_path(
+            counts, capacity, pieces, rows, plan, bits, own, slots)
         for counts in patterns
     ] + [lambda plan, bits, own, slots, given: general(*given)]
     return lax.switch(plan[0], branches, plan, bits, own, slots, given)

time: 59 us -> 66 us (1.12)
  waiting for transfers between devices: 19.1 us -> 31.2 us
  starting transfers between devices: 24.2 us -> 19.6 us
    ppermute x3, waiting for transfers between devices: 11.1 us -> 22 us  [shift_by(): lax.ppermute(array, 'blk', [(i, (i + k) % places) for i in range(places)])]
    ppermute x3, starting transfers between devices: 13.6 us -> 6.71 us  [shift_by(): lax.ppermute(array, 'blk', [(i, (i + k) % places) for i in range(places)])]
    ppermute x3, waiting for transfers between devices: 1.88 us -> 5.53 us  [pattern_path(): lax.ppermute(dense, 'blk', [(i, i ^ q) for i in range(places)])]
    ppermute x12, waiting for transfers between devices: 6.06 us -> 3.66 us  [swap_with(): return lax.ppermute(array, 'sub', [(i, i ^ q) for i in range(pieces)])]
    ppermute x3, starting transfers between devices: 4.44 us -> 5.72 us  [pattern_path(): lax.ppermute(dense, 'blk', [(i, i ^ q) for i in range(places)])]
    ppermute x12, starting transfers between devices: 6.11 us -> 7.13 us  [swap_with(): return lax.ppermute(array, 'sub', [(i, i ^ q) for i in range(pieces)])]
  transfers between devices with their start and end apart: 18 -> 18, of which waited for: 9 -> 9; matrix products, arithmetic and copies ran while one was open for 0% -> 0% of each run, Pallas kernels for 11% -> 10%
where the time goes in v4:
time: 66 us; the launch traced here: 65.7 us
  waiting for transfers between devices  31.2 us (47%)
  starting transfers between devices  19.6 us (30%)
  Pallas kernels  11.1 us (17%)
  local copies, waits for them, and re-layouts  2.57 us (4%)
  between operations  0.75 us (1%)
    ppermute x3, waiting for transfers between devices, shift_by(): lax.ppermute(array, 'blk', [(i, (i + k) % places) for i in range(places)])  22 us
    pallas_call x2, Pallas kernels, score(): pl.pallas_call(functools.partial(score_kernel, rows, width, pieces, where...  8.19 us
    ppermute x12, starting transfers between devices, swap_with(): return lax.ppermute(array, 'sub', [(i, i ^ q) for i in range(pieces)])  7.13 us
    ppermute x3, starting transfers between devices, shift_by(): lax.ppermute(array, 'blk', [(i, (i + k) % places) for i in range(places)])  6.71 us
    ppermute x3, starting transfers between devices, pattern_path(): lax.ppermute(dense, 'blk', [(i, i ^ q) for i in range(places)])  5.72 us
    ppermute x3, waiting for transfers between devices, pattern_path(): lax.ppermute(dense, 'blk', [(i, i ^ q) for i in range(places)])  5.53 us
    ppermute x12, waiting for transfers between devices, swap_with(): return lax.ppermute(array, 'sub', [(i, i ^ q) for i in range(pieces)])  3.66 us
    pallas_call x1, Pallas kernels, make_plan(): pl.pallas_call(functools.partial(plan_kernel, patterns, places, capacity)...  1.99 us
  transfers between devices with their start and end apart: 18, of which 9 were waited for; matrix products, arithmetic and copies ran while one was open for 0% of the time, Pallas kernels for 10%

profile of v4, /device:TPU:0, one launch (start us, length us, event | category | flops | bytes accessed | tf_op | source)
XLA Modules:
  0.0 65.7 jit_solution(7665590741176824935)
XLA Ops:
  0.0 0.0 copy-start.18
  0.0 0.0 copy-start.16
  0.0 0.0 copy-start.19
  0.0 0.0 copy-start.20
  0.0 1.4 %copy.21.emb_ref = bf16[5,128,1024]{2,1,0:T(8,128)(2,1)S(1)} copy(bf16[5,128,1024]{2,1,0:T(8,128)(2,1)} %param.13) | data formatting | bytes 2621440
  2.0 0.0 copy-done.18
  2.0 0.0 copy-done.16
  2.1 0.0 copy-done.19
  2.1 0.0 copy-done.20
  2.1 2.0 %plan_and_gather.1 = (s32[27]{0:T(128)S(1)}, s32[1]{0:T(128)}, bf16[256,1024]{1,0:T(8,128)(2,1)S(1)}, bf16[128,1024]{1,0:T(8,128)(2,1)S(1)}, bf16[128,1024]{1,0:...) custom-call(s32[1]{0:T(128)} %bitcast.27.me_ref, ...), custom_call_target="tpu_custom_call" | custom-call | tf_op jit(solution)/shard_map/plan_and_gather/pallas_call | solution.py:132
  4.1 61.0 %conditional.1 = (f32[5,128]{1,0:T(8,128)S(1)}) conditional(s32[]{:T(128)} %bitcast.29, (bf16[128,1024]{1,0:T(8,128)(2,1)S(1)}, bf16[128,1024]{1,0:T(8,128)(2,1)S(1)}, bf16[256,1024]{1,0:T(8,128)(2,1)S(1)}, bf16[128,1024]{1,0:T(8,128)(2,1)S(1)}, s32[27]{0:T(128)S(1)}, /*index=5*/s32[1]{0:T(128)}) %tuple.32, ...), branch_computations={%region_0.0_spmd, %region_1.0_spmd, %region_2.0_spmd, %region_3.0_... | conditional | flops 1474489 | bytes 33400496 | solution.py:454
  4.1 5.3 %collective-permute-start.54 = (bf16[128,1024]{1,0:T(8,128)(2,1)S(1)}, bf16[128,1024]{1,0:T(8,128)(2,1)S(1)}, u32[]{:S(2)}, u32[]{:S(2)}) collective-permute-start(bf16[128,1024]{1,0:T(8,128)(2,1)S(1)} %get-tuple-element.118), channel_id=1, source_target_pairs={{0,12},{4,0},{8,4},{12,8},{1,13},{5,1},{9,5},{13,9},{2,14},{6,2},{... | collective-permute-start | bytes 786440 | tf_op jit(solution)/shard_map/cond/branch_3_fun/ppermute | solution.py:349
  9.4 1.5 %collective-permute-start.58 = (bf16[256,1024]{1,0:T(8,128)(2,1)S(1)}, bf16[256,1024]{1,0:T(8,128)(2,1)S(1)}, u32[]{:S(2)}, u32[]{:S(2)}) collective-permute-start(bf16[256,1024]{1,0:T(8,128)(2,1)S(1)} %get-tuple-element.120.refs_0_), channel_id=1, source_target_pairs={{0,2},{1,3},{2,0},{3,1},{4,6},{5,7},{6,4},{7,5},{8,10},{9,11},{10,... | collective-permute-start | bytes 1572872 | tf_op jit(solution)/shard_map/cond/branch_3_fun/ppermute | solution.py:353
  10.9 0.0 collective-permute-start.63
  10.9 5.3 %collective-permute-done.54.refs_4_ = bf16[128,1024]{1,0:T(8,128)(2,1)S(1)} collective-permute-done((bf16[128,1024]{1,0:T(8,128)(2,1)S(1)}, bf16[128,1024]{1,0:T(8,128)(2,1)S(1)}, u32[]{:S(2)}, u32[]{:S(2)}) %collective-permute-start.54) | collective-permute-done | bytes 262176 | tf_op jit(solution)/shard_map/cond/branch_3_fun/ppermute | solution.py:349
  16.2 1.4 %collective-permute-start.55 = (bf16[128,1024]{1,0:T(8,128)(2,1)S(1)}, bf16[128,1024]{1,0:T(8,128)(2,1)S(1)}, u32[]{:S(2)}, u32[]{:S(2)}) collective-permute-start(bf16[128,1024]{1,0:T(8,128)(2,1)S(1)} %get-tuple-element.119), channel_id=1, source_target_pairs={{0,8},{4,12},{8,0},{12,4},{1,9},{5,13},{9,1},{13,5},{2,10},{6,14},... | collective-permute-start | bytes 786440 | tf_op jit(solution)/shard_map/cond/branch_3_fun/ppermute | solution.py:349
  17.6 1.5 %collective-permute-start.61 = (bf16[128,1024]{1,0:T(8,128)(2,1)S(1)}, bf16[128,1024]{1,0:T(8,128)(2,1)S(1)}, u32[]{:S(2)}, u32[]{:S(2)}) collective-permute-start(bf16[128,1024]{1,0:T(8,128)(2,1)S(1)} %collective-permute-done.54.refs_4_), channel_id=1, source_target_pairs={{0,2},{1,3},{2,0},{3,1},{4,6},{5,7},{6,4},{7,5},{8,10},{9,11},{10,... | collective-permute-start | bytes 786440 | tf_op jit(solution)/shard_map/cond/branch_3_fun/ppermute | solution.py:353
  19.1 0.0 collective-permute-start.57
  19.1 13.8 %collective-permute-done.63.refs_8_ = bf16[128,1024]{1,0:T(8,128)(2,1)S(1)} collective-permute-done((bf16[128,1024]{1,0:T(8,128)(2,1)S(1)}, bf16[128,1024]{1,0:T(8,128)(2,1)S(1)}, u32[]{:S(2)}, u32[]{:S(2)}) %collective-permute-start.63) | collective-permute-done | bytes 262176 | tf_op jit(solution)/shard_map/cond/branch_3_fun/ppermute | solution.py:349
  32.9 1.5 %collective-permute-start.65 = (bf16[128,1024]{1,0:T(8,128)(2,1)S(1)}, bf16[128,1024]{1,0:T(8,128)(2,1)S(1)}, u32[]{:S(2)}, u32[]{:S(2)}) collective-permute-start(bf16[128,1024]{1,0:T(8,128)(2,1)S(1)} %collective-permute-done.63.refs_8_), channel_id=1, source_target_pairs={{0,2},{1,3},{2,0},{3,1},{4,6},{5,7},{6,4},{7,5},{8,10},{9,11},{10,... | collective-permute-start | bytes 786440 | tf_op jit(solution)/shard_map/cond/branch_3_fun/ppermute | solution.py:353
  34.4 3.0 %collective-permute-done.55.refs_12_ = bf16[128,1024]{1,0:T(8,128)(2,1)S(1)} collective-permute-done((bf16[128,1024]{1,0:T(8,128)(2,1)S(1)}, bf16[128,1024]{1,0:T(8,128)(2,1)S(1)}, u32[]{:S(2)}, u32[]{:S(2)}) %collective-permute-start.55) | collective-permute-done | bytes 262176 | tf_op jit(solution)/shard_map/cond/branch_3_fun/ppermute | solution.py:349
  37.3 0.0 collective-permute-start.60
  37.4 0.0 collective-permute-done.61.refs_6_
  37.4 0.5 collective-permute-start.64
  37.9 0.0 collective-permute-done.58.refs_2_
  37.9 0.1 collective-permute-start.59
  37.9 1.3 %collective-permute-done.65.refs_10_ = bf16[128,1024]{1,0:T(8,128)(2,1)S(1)} collective-permute-done((bf16[128,1024]{1,0:T(8,128)(2,1)S(1)}, bf16[128,1024]{1,0:T(8,128)(2,1)S(1)}, u32[]{:S(2)}, u32[]{:S(2)}) %collective-permute-start.65) | collective-permute-done | bytes 262176 | tf_op jit(solution)/shard_map/cond/branch_3_fun/ppermute | solution.py:353
  39.3 0.0 collective-permute-start.67
  39.3 0.0 collective-permute-done.60.refs_5_
  39.3 0.5 collective-permute-start.62
  39.8 0.0 collective-permute-done.64.refs_9_
  39.8 0.1 collective-permute-start.66
  39.8 0.0 collective-permute-done.57.refs_1_
  39.8 1.5 %collective-permute-start.56 = (bf16[128,1024]{1,0:T(8,128)(2,1)S(1)}, bf16[128,1024]{1,0:T(8,128)(2,1)S(1)}, u32[]{:S(2)}, u32[]{:S(2)}) collective-permute-start(bf16[128,1024]{1,0:T(8,128)(2,1)S(1)} %collective-permute-done.55.refs_12_), channel_id=1, source_target_pairs={{0,2},{1,3},{2,0},{3,1},{4,6},{5,7},{6,4},{7,5},{8,10},{9,11},{10,... | collective-permute-start | bytes 786440 | tf_op jit(solution)/shard_map/cond/branch_3_fun/ppermute | solution.py:353
  41.3 0.0 collective-permute-done.67.refs_13_
  41.3 0.0 collective-permute-done.62.refs_7_
  41.3 0.2 collective-permute-done.66.refs_11_
  41.5 0.0 collective-permute-done.59.refs_3_
  41.5 6.3 %score_most.7 = (f32[25,128,128]{2,1,0:T(8,128)S(1)}, bf16[640,1024]{1,0:T(8,128)(2,1)S(1)}, f32[640,128]{1,0:T(8,128)S(1)}) custom-call(bf16[256,1024]{1,0:T(8,128)(2,1)S(1)} %get-tuple-element.120.refs_0_, bf16[256,1024]{1,0:T(8,128)(2,1)S(1)} %collective-permute-done.57.refs_1_, bf16[256,1024]{1,0:T(8,128)(2,1)S(1)} %collective-permute-done.58.refs_2_, ...), custom_call_target="tpu_custom_call" | custom-call | tf_op jit(solution)/shard_map/cond/branch_3_fun/score_most/pallas_call | solution.py:299
  47.9 0.6 collective-permute-done.56.refs_0_
  48.5 0.0 collective-permute-start.68
  48.5 1.5 %collective-permute-done.68.refs_1_ = bf16[128,1024]{1,0:T(8,128)(2,1)S(1)} collective-permute-done((bf16[128,1024]{1,0:T(8,128)(2,1)S(1)}, bf16[128,1024]{1,0:T(8,128)(2,1)S(1)}, u32[]{:S(2)}, u32[]{:S(2)}) %collective-permute-start.68) | collective-permute-done | bytes 262176 | tf_op jit(solution)/shard_map/cond/branch_3_fun/ppermute | solution.py:353
  50.0 1.8 %score_late.7.refs_0_ = f32[32,128]{1,0:T(8,128)S(1)} custom-call(bf16[128,1024]{1,0:T(8,128)(2,1)S(1)} %collective-permute-done.56.refs_0_, bf16[128,1024]{1,0:T(8,128)(2,1)S(1)} %collective-permute-done.68.refs_1_, s32[27]{0:T(128)S(1)} %get-tuple-element.116.refs_2_.plan_ref, s32[1]{0:T(128)} %get-tuple-element.124.refs_3_, ...), custom_call_target="tpu_custom_call" | custom-call | tf_op jit(solution)/shard_map/cond/branch_3_fun/score_late/pallas_call | solution.py:299
  51.9 0.0 copy-start.3
  51.9 2.3 %collective-permute-start.69 = (f32[32,128]{1,0:T(8,128)S(1)}, f32[32,128]{1,0:T(8,128)S(1)}, u32[]{:S(2)}, u32[]{:S(2)}) collective-permute-start(f32[32,128]{1,0:T(8,128)S(1)} %score_late.7.refs_0_), channel_id=1, source_target_pairs={{0,4},{4,0},{8,12},{12,8},{1,5},{5,1},{9,13},{13,9},{2,6},{6,2},{1... | collective-permute-start | bytes 49160 | tf_op jit(solution)/shard_map/cond/branch_3_fun/ppermute | solution.py:389
  54.2 3.4 %collective-permute-start.70 = (f32[32,128]{1,0:T(8,128)S(1)}, f32[32,128]{1,0:T(8,128)S(1)}, u32[]{:S(2)}, u32[]{:S(2)}) collective-permute-start(f32[32,128]{1,0:T(8,128)S(1)} %score_late.7.refs_0_), channel_id=1, source_target_pairs={{0,8},{4,12},{8,0},{12,4},{1,9},{5,13},{9,1},{13,5},{2,10},{6,14},... | collective-permute-start | bytes 49160 | tf_op jit(solution)/shard_map/cond/branch_3_fun/ppermute | solution.py:389
  57.6 0.0 collective-permute-start.71
  57.6 0.0 collective-permute-done.69.refs_1_
  57.6 0.0 copy-start.7
  57.6 1.7 %collective-permute-done.70.refs_2_ = f32[32,128]{1,0:T(8,128)S(1)} collective-permute-done((f32[32,128]{1,0:T(8,128)S(1)}, f32[32,128]{1,0:T(8,128)S(1)}, u32[]{:S(2)}, u32[]{:S(2)}) %collective-permute-start.70) | collective-permute-done | bytes 16416 | tf_op jit(solution)/shard_map/cond/branch_3_fun/ppermute | solution.py:389
  59.3 0.0 copy-start.11
  59.3 3.8 %collective-permute-done.71.refs_3_ = f32[32,128]{1,0:T(8,128)S(1)} collective-permute-done((f32[32,128]{1,0:T(8,128)S(1)}, f32[32,128]{1,0:T(8,128)S(1)}, u32[]{:S(2)}, u32[]{:S(2)}) %collective-permute-start.71) | collective-permute-done | bytes 16416 | tf_op jit(solution)/shard_map/cond/branch_3_fun/ppermute | solution.py:389
  63.1 0.0 copy-done.3
  63.2 0.0 copy-done.7
  63.2 0.0 copy-done.11
  63.2 0.0 copy-start.15
  63.2 0.6 copy-done.15
  63.8 0.9 %place_rows.7 = f32[5,128]{1,0:T(8,128)S(1)} custom-call(s32[27]{0:T(128)S(1)} %get-tuple-element.116.refs_2_.plan_ref, f32[32,128]{1,0:T(8,128)} %copy-done.3, f32[32,128]{1,0:T(8,128)} %copy-done.7, f32[32,128]{1,0:T(8,128)} %copy-done.11, f32[32,128]{1,0:T(8,128)} %copy-done.15), custom_call_target="tpu_custom_call" | custom-call | tf_op jit(solution)/shard_map/cond/branch_3_fun/place_rows/pallas_call | solution.py:338
  65.1 0.0 copy-start.17
  65.2 0.6 copy-done.17
Async XLA Ops:
  0.0 2.0 %copy-start.18 = (s32[5]{0:T(128)S(1)}, s32[5]{0:T(128)}, u32[]{:S(2)}) copy-start(s32[5]{0:T(128)} %count_ref.1) | copy-start | bytes 64
  0.0 2.0 %copy-start.16 = (s32[4,5]{1,0:T(4,128)S(1)}, s32[4,5]{1,0:T(4,128)}, u32[]{:S(2)}) copy-start(s32[4,5]{1,0:T(4,128)} %fetch_ref.1) | copy-start | bytes 244
  0.0 2.0 %copy-start.19 = (s32[1,15]{1,0:T(1,128)S(1)}, s32[1,15]{1,0:T(1,128)}, u32[]{:S(2)}) copy-start(s32[1,15]{1,0:T(1,128)} %left_ref.1) | copy-start | bytes 184
  0.0 2.1 %copy-start.20 = (s32[1,15]{1,0:T(1,128)S(1)}, s32[1,15]{1,0:T(1,128)}, u32[]{:S(2)}) copy-start(s32[1,15]{1,0:T(1,128)} %right_ref.1) | copy-start | bytes 184
  4.1 12.0 %collective-permute-start.54 = (bf16[128,1024]{1,0:T(8,128)(2,1)S(1)}, bf16[128,1024]{1,0:T(8,128)(2,1)S(1)}, u32[]{:S(2)}, u32[]{:S(2)}) collective-permute-start(bf16[128,1024]{1,0:T(8,128)(2,1)S(1)} %get-tuple-element.118), channel_id=1, source_target_pairs={{0,12},{4,0},{8,4},{12,8},{1,13},{5,1},{9,5},{13,9},{2,14},{6,2},{... | collective-permute-start | bytes 786440 | tf_op jit(solution)/shard_map/cond/branch_3_fun/ppermute | solution.py:349
  9.4 28.4 %collective-permute-start.58 = (bf16[256,1024]{1,0:T(8,128)(2,1)S(1)}, bf16[256,1024]{1,0:T(8,128)(2,1)S(1)}, u32[]{:S(2)}, u32[]{:S(2)}) collective-permute-start(bf16[256,1024]{1,0:T(8,128)(2,1)S(1)} %get-tuple-element.120.refs_0_), channel_id=1, source_target_pairs={{0,2},{1,3},{2,0},{3,1},{4,6},{5,7},{6,4},{7,5},{8,10},{9,11},{10,... | collective-permute-start | bytes 1572872 | tf_op jit(solution)/shard_map/cond/branch_3_fun/ppermute | solution.py:353
  10.9 22.0 %collective-permute-start.63 = (bf16[128,1024]{1,0:T(8,128)(2,1)S(1)}, bf16[128,1024]{1,0:T(8,128)(2,1)S(1)}, u32[]{:S(2)}, u32[]{:S(2)}) collective-permute-start(bf16[128,1024]{1,0:T(8,128)(2,1)S(1)} %get-tuple-element.121), channel_id=1, source_target_pairs={{0,8},{4,12},{8,0},{12,4},{1,9},{5,13},{9,1},{13,5},{2,10},{6,14},... | collective-permute-start | bytes 786440 | tf_op jit(solution)/shard_map/cond/branch_3_fun/ppermute | solution.py:349
  16.2 21.2 %collective-permute-start.55 = (bf16[128,1024]{1,0:T(8,128)(2,1)S(1)}, bf16[128,1024]{1,0:T(8,128)(2,1)S(1)}, u32[]{:S(2)}, u32[]{:S(2)}) collective-permute-start(bf16[128,1024]{1,0:T(8,128)(2,1)S(1)} %get-tuple-element.119), channel_id=1, source_target_pairs={{0,8},{4,12},{8,0},{12,4},{1,9},{5,13},{9,1},{13,5},{2,10},{6,14},... | collective-permute-start | bytes 786440 | tf_op jit(solution)/shard_map/cond/branch_3_fun/ppermute | solution.py:349
  17.6 19.8 %collective-permute-start.61 = (bf16[128,1024]{1,0:T(8,128)(2,1)S(1)}, bf16[128,1024]{1,0:T(8,128)(2,1)S(1)}, u32[]{:S(2)}, u32[]{:S(2)}) collective-permute-start(bf16[128,1024]{1,0:T(8,128)(2,1)S(1)} %collective-permute-done.54.refs_4_), channel_id=1, source_target_pairs={{0,2},{1,3},{2,0},{3,1},{4,6},{5,7},{6,4},{7,5},{8,10},{9,11},{10,... | collective-permute-start | bytes 786440 | tf_op jit(solution)/shard_map/cond/branch_3_fun/ppermute | solution.py:353
  19.1 20.7 %collective-permute-start.57 = (bf16[256,1024]{1,0:T(8,128)(2,1)S(1)}, bf16[256,1024]{1,0:T(8,128)(2,1)S(1)}, u32[]{:S(2)}, u32[]{:S(2)}) collective-permute-start(bf16[256,1024]{1,0:T(8,128)(2,1)S(1)} %get-tuple-element.120.refs_0_), channel_id=1, source_target_pairs={{0,1},{1,0},{2,3},{3,2},{4,5},{5,4},{6,7},{7,6},{8,9},{9,8},{10,11... | collective-permute-start | bytes 1572872 | tf_op jit(solution)/shard_map/cond/branch_3_fun/ppermute | solution.py:353
  32.9 6.4 %collective-permute-start.65 = (bf16[128,1024]{1,0:T(8,128)(2,1)S(1)}, bf16[128,1024]{1,0:T(8,128)(2,1)S(1)}, u32[]{:S(2)}, u32[]{:S(2)}) collective-permute-start(bf16[128,1024]{1,0:T(8,128)(2,1)S(1)} %collective-permute-done.63.refs_8_), channel_id=1, source_target_pairs={{0,2},{1,3},{2,0},{3,1},{4,6},{5,7},{6,4},{7,5},{8,10},{9,11},{10,... | collective-permute-start | bytes 786440 | tf_op jit(solution)/shard_map/cond/branch_3_fun/ppermute | solution.py:353
  37.3 1.9 %collective-permute-start.60 = (bf16[128,1024]{1,0:T(8,128)(2,1)S(1)}, bf16[128,1024]{1,0:T(8,128)(2,1)S(1)}, u32[]{:S(2)}, u32[]{:S(2)}) collective-permute-start(bf16[128,1024]{1,0:T(8,128)(2,1)S(1)} %collective-permute-done.54.refs_4_), channel_id=1, source_target_pairs={{0,1},{1,0},{2,3},{3,2},{4,5},{5,4},{6,7},{7,6},{8,9},{9,8},{10,11... | collective-permute-start | bytes 786440 | tf_op jit(solution)/shard_map/cond/branch_3_fun/ppermute | solution.py:353
  37.4 2.4 %collective-permute-start.64 = (bf16[128,1024]{1,0:T(8,128)(2,1)S(1)}, bf16[128,1024]{1,0:T(8,128)(2,1)S(1)}, u32[]{:S(2)}, u32[]{:S(2)}) collective-permute-start(bf16[128,1024]{1,0:T(8,128)(2,1)S(1)} %collective-permute-done.63.refs_8_), channel_id=1, source_target_pairs={{0,1},{1,0},{2,3},{3,2},{4,5},{5,4},{6,7},{7,6},{8,9},{9,8},{10,11... | collective-permute-start | bytes 786440 | tf_op jit(solution)/shard_map/cond/branch_3_fun/ppermute | solution.py:353
  37.9 3.7 %collective-permute-start.59 = (bf16[256,1024]{1,0:T(8,128)(2,1)S(1)}, bf16[256,1024]{1,0:T(8,128)(2,1)S(1)}, u32[]{:S(2)}, u32[]{:S(2)}) collective-permute-start(bf16[256,1024]{1,0:T(8,128)(2,1)S(1)} %collective-permute-done.58.refs_2_), channel_id=1, source_target_pairs={{0,1},{1,0},{2,3},{3,2},{4,5},{5,4},{6,7},{7,6},{8,9},{9,8},{10,11... | collective-permute-start | bytes 1572872 | tf_op jit(solution)/shard_map/cond/branch_3_fun/ppermute | solution.py:353
  39.3 2.1 %collective-permute-start.67 = (bf16[128,1024]{1,0:T(8,128)(2,1)S(1)}, bf16[128,1024]{1,0:T(8,128)(2,1)S(1)}, u32[]{:S(2)}, u32[]{:S(2)}) collective-permute-start(bf16[128,1024]{1,0:T(8,128)(2,1)S(1)} %collective-permute-done.55.refs_12_), channel_id=1, source_target_pairs={{0,1},{1,0},{2,3},{3,2},{4,5},{5,4},{6,7},{7,6},{8,9},{9,8},{10,11... | collective-permute-start | bytes 786440 | tf_op jit(solution)/shard_map/cond/branch_3_fun/ppermute | solution.py:353
  39.3 2.1 %collective-permute-start.62 = (bf16[128,1024]{1,0:T(8,128)(2,1)S(1)}, bf16[128,1024]{1,0:T(8,128)(2,1)S(1)}, u32[]{:S(2)}, u32[]{:S(2)}) collective-permute-start(bf16[128,1024]{1,0:T(8,128)(2,1)S(1)} %collective-permute-done.61.refs_6_), channel_id=1, source_target_pairs={{0,1},{1,0},{2,3},{3,2},{4,5},{5,4},{6,7},{7,6},{8,9},{9,8},{10,11... | collective-permute-start | bytes 786440 | tf_op jit(solution)/shard_map/cond/branch_3_fun/ppermute | solution.py:353
  39.8 1.8 %collective-permute-start.66 = (bf16[128,1024]{1,0:T(8,128)(2,1)S(1)}, bf16[128,1024]{1,0:T(8,128)(2,1)S(1)}, u32[]{:S(2)}, u32[]{:S(2)}) collective-permute-start(bf16[128,1024]{1,0:T(8,128)(2,1)S(1)} %collective-permute-done.65.refs_10_), channel_id=1, source_target_pairs={{0,1},{1,0},{2,3},{3,2},{4,5},{5,4},{6,7},{7,6},{8,9},{9,8},{10,11... | collective-permute-start | bytes 786440 | tf_op jit(solution)/shard_map/cond/branch_3_fun/ppermute | solution.py:353
  39.8 8.7 %collective-permute-start.56 = (bf16[128,1024]{1,0:T(8,128)(2,1)S(1)}, bf16[128,1024]{1,0:T(8,128)(2,1)S(1)}, u32[]{:S(2)}, u32[]{:S(2)}) collective-permute-start(bf16[128,1024]{1,0:T(8,128)(2,1)S(1)} %collective-permute-done.55.refs_12_), channel_id=1, source_target_pairs={{0,2},{1,3},{2,0},{3,1},{4,6},{5,7},{6,4},{7,5},{8,10},{9,11},{10,... | collective-permute-start | bytes 786440 | tf_op jit(solution)/shard_map/cond/branch_3_fun/ppermute | solution.py:353
  48.5 1.5 %collective-permute-start.68 = (bf16[128,1024]{1,0:T(8,128)(2,1)S(1)}, bf16[128,1024]{1,0:T(8,128)(2,1)S(1)}, u32[]{:S(2)}, u32[]{:S(2)}) collective-permute-start(bf16[128,1024]{1,0:T(8,128)(2,1)S(1)} %collective-permute-done.56.refs_0_), channel_id=1, source_target_pairs={{0,1},{1,0},{2,3},{3,2},{4,5},{5,4},{6,7},{7,6},{8,9},{9,8},{10,11... | collective-permute-start | bytes 786440 | tf_op jit(solution)/shard_map/cond/branch_3_fun/ppermute | solution.py:353
  51.9 11.3 %copy-start.3 = (f32[32,128]{1,0:T(8,128)}, f32[32,128]{1,0:T(8,128)S(1)}, u32[]{:S(2)}) copy-start(f32[32,128]{1,0:T(8,128)S(1)} %score_late.7.refs_0_) | copy-start | bytes 49156 | tf_op jit(solution)/shard_map/cond
  51.9 5.7 %collective-permute-start.69 = (f32[32,128]{1,0:T(8,128)S(1)}, f32[32,128]{1,0:T(8,128)S(1)}, u32[]{:S(2)}, u32[]{:S(2)}) collective-permute-start(f32[32,128]{1,0:T(8,128)S(1)} %score_late.7.refs_0_), channel_id=1, source_target_pairs={{0,4},{4,0},{8,12},{12,8},{1,5},{5,1},{9,13},{13,9},{2,6},{6,2},{1... | collective-permute-start | bytes 49160 | tf_op jit(solution)/shard_map/cond/branch_3_fun/ppermute | solution.py:389
  54.2 5.1 %collective-permute-start.70 = (f32[32,128]{1,0:T(8,128)S(1)}, f32[32,128]{1,0:T(8,128)S(1)}, u32[]{:S(2)}, u32[]{:S(2)}) collective-permute-start(f32[32,128]{1,0:T(8,128)S(1)} %score_late.7.refs_0_), channel_id=1, source_target_pairs={{0,8},{4,12},{8,0},{12,4},{1,9},{5,13},{9,1},{13,5},{2,10},{6,14},... | collective-permute-start | bytes 49160 | tf_op jit(solution)/shard_map/cond/branch_3_fun/ppermute | solution.py:389
  57.6 5.5 %collective-permute-start.71 = (f32[32,128]{1,0:T(8,128)S(1)}, f32[32,128]{1,0:T(8,128)S(1)}, u32[]{:S(2)}, u32[]{:S(2)}) collective-permute-start(f32[32,128]{1,0:T(8,128)S(1)} %score_late.7.refs_0_), channel_id=1, source_target_pairs={{0,12},{4,8},{8,4},{12,0},{1,13},{5,9},{9,5},{13,1},{2,14},{6,10},... | collective-permute-start | bytes 49160 | tf_op jit(solution)/shard_map/cond/branch_3_fun/ppermute | solution.py:389
  57.6 5.5 %copy-start.7 = (f32[32,128]{1,0:T(8,128)}, f32[32,128]{1,0:T(8,128)S(1)}, u32[]{:S(2)}) copy-start(f32[32,128]{1,0:T(8,128)S(1)} %collective-permute-done.69.refs_1_) | copy-start | bytes 49156 | tf_op jit(solution)/shard_map/cond
  59.3 3.8 %copy-start.11 = (f32[32,128]{1,0:T(8,128)}, f32[32,128]{1,0:T(8,128)S(1)}, u32[]{:S(2)}) copy-start(f32[32,128]{1,0:T(8,128)S(1)} %collective-permute-done.70.refs_2_) | copy-start | bytes 49156 | tf_op jit(solution)/shard_map/cond
  63.2 0.6 copy-start.15
  65.1 0.6 copy-start.17

commit v5 on v4

--- a/solution.py
+++ b/solution.py
@@ -320,7 +320,7 @@
     total = places * capacity
     me = plan_ref[plan_ref.shape[0] - 1]
     for q, ref in enumerate(refs):
-        held[q] = ref[...]
+        held[places - 1 - q] = ref[...]
     lane = lax.broadcasted_iota(jnp.int32, (blocks, rows), 1)
     spot = lax.broadcasted_iota(jnp.int32, (blocks, rows), 0)
     for n, (k, at) in enumerate(taken):
@@ -366,7 +366,7 @@
     for k, at in taken[capacity:]:
         sent = slots[at - capacity]
         if len(moved) == 2:
-            sent = after(sent, moved[0])
+            sent = after(sent, *(moved if counts[places // 2] > 1 else moved[1:]))
         moved.append(shift_by(sent, k, places))
     held = {}
     first = [0] + list(range(capacity, blocks + 1))
@@ -386,7 +386,10 @@
     spots = [2 + places * capacity + at for _, at in taken]
     (dense,) = score(pieces, held, range(0), range(blocks * per - 1, blocks * per), [(0, blocks, 0, 1)],
                      (plan, spots, bits, None, [(sums, known)], lefts), name="score_late")
-    returned = [dense] + [lax.ppermute(dense, "blk", [(i, i ^ q) for i in range(places)]) for q in range(1, places)]
+    returned = {0: dense}
+    for q in reversed(range(1, places)):
+        returned[q] = lax.ppermute(dense, "blk", [(i, i ^ q) for i in range(places)])
+    returned = [returned[q] for q in reversed(range(places))]
     return place_rows(taken, capacity, pieces, plan, returned, blocks, rows)
 
 

time: 66 us -> 55.8 us (0.85)
  waiting for transfers between devices: 31.2 us -> 19.4 us
  starting transfers between devices: 19.6 us -> 20.9 us
    ppermute x3, waiting for transfers between devices: 22 us -> 8.73 us  [shift_by(): lax.ppermute(array, 'blk', [(i, (i + k) % places) for i in range(places)])]
    ppermute x12, waiting for transfers between devices: 3.66 us -> 8.98 us  [swap_with(): return lax.ppermute(array, 'sub', [(i, i ^ q) for i in range(pieces)])]
    ppermute x3, waiting for transfers between devices: 5.53 us -> 1.71 us  [pattern_path(): lax.ppermute(dense, 'blk', [(i, i ^ q) for i in range(places)])]
    ppermute x3, starting transfers between devices: 6.71 us -> 9.39 us  [shift_by(): lax.ppermute(array, 'blk', [(i, (i + k) % places) for i in range(places)])]
    ppermute x3, starting transfers between devices: 5.72 us -> 4.45 us  [pattern_path(): lax.ppermute(dense, 'blk', [(i, i ^ q) for i in range(places)])]
  transfers between devices with their start and end apart: 18 -> 18, of which waited for: 9 -> 10; matrix products, arithmetic and copies ran while one was open for 0% -> 0% of each run, Pallas kernels for 10% -> 11%
where the time goes in v5:
time: 55.8 us; the launch traced here: 55.1 us
  starting transfers between devices  20.9 us (37%)
  waiting for transfers between devices  19.4 us (35%)
  Pallas kernels  11 us (20%)
  local copies, waits for them, and re-layouts  2.63 us (5%)
  between operations  0.75 us (1%)
    ppermute x3, starting transfers between devices, shift_by(): lax.ppermute(array, 'blk', [(i, (i + k) % places) for i in range(places)])  9.39 us
    ppermute x12, waiting for transfers between devices, swap_with(): return lax.ppermute(array, 'sub', [(i, i ^ q) for i in range(pieces)])  8.98 us
    ppermute x3, waiting for transfers between devices, shift_by(): lax.ppermute(array, 'blk', [(i, (i + k) % places) for i in range(places)])  8.73 us
    pallas_call x2, Pallas kernels, score(): pl.pallas_call(functools.partial(score_kernel, rows, width, pieces, where...  8.14 us
    ppermute x12, starting transfers between devices, swap_with(): return lax.ppermute(array, 'sub', [(i, i ^ q) for i in range(pieces)])  7.07 us
    ppermute x3, starting transfers between devices, pattern_path(): lax.ppermute(dense, 'blk', [(i, i ^ q) for i in range(places)])  4.45 us
    pallas_call x1, Pallas kernels, make_plan(): pl.pallas_call(functools.partial(plan_kernel, patterns, places, capacity)...  1.99 us
    unnamed x11, local copies, waits for them, and re-layouts  1.97 us
  transfers between devices with their start and end apart: 18, of which 10 were waited for; matrix products, arithmetic and copies ran while one was open for 0% of the time, Pallas kernels for 11%

profile of v5, /device:TPU:0, one launch (start us, length us, event | category | flops | bytes accessed | tf_op | source)
XLA Modules:
  0.0 55.1 jit_solution(11333264354711449777)
XLA Ops:
  0.0 0.0 copy-start.18
  0.0 0.0 copy-start.16
  0.0 0.0 copy-start.19
  0.0 0.0 copy-start.20
  0.0 1.4 %copy.21.emb_ref = bf16[5,128,1024]{2,1,0:T(8,128)(2,1)S(1)} copy(bf16[5,128,1024]{2,1,0:T(8,128)(2,1)} %param.13) | data formatting | bytes 2621440
  2.0 0.0 copy-done.18
  2.0 0.0 copy-done.16
  2.1 0.0 copy-done.19
  2.1 0.0 copy-done.20
  2.1 2.0 %plan_and_gather.1 = (s32[27]{0:T(128)S(1)}, s32[1]{0:T(128)}, bf16[256,1024]{1,0:T(8,128)(2,1)S(1)}, bf16[128,1024]{1,0:T(8,128)(2,1)S(1)}, bf16[128,1024]{1,0:...) custom-call(s32[1]{0:T(128)} %bitcast.27.me_ref, ...), custom_call_target="tpu_custom_call" | custom-call | tf_op jit(solution)/shard_map/plan_and_gather/pallas_call | solution.py:132
  4.1 50.4 %conditional.1 = (f32[5,128]{1,0:T(8,128)S(1)}) conditional(s32[]{:T(128)} %bitcast.29, (bf16[128,1024]{1,0:T(8,128)(2,1)S(1)}, bf16[128,1024]{1,0:T(8,128)(2,1)S(1)}, bf16[256,1024]{1,0:T(8,128)(2,1)S(1)}, bf16[128,1024]{1,0:T(8,128)(2,1)S(1)}, s32[27]{0:T(128)S(1)}, /*index=5*/s32[1]{0:T(128)}) %tuple.32, ...), branch_computations={%region_0.0_spmd, %region_1.0_spmd, %region_2.0_spmd, %region_3.0_... | conditional | flops 1474489 | bytes 33400496 | solution.py:457
  4.1 5.1 %collective-permute-start.18 = (bf16[128,1024]{1,0:T(8,128)(2,1)S(1)}, bf16[128,1024]{1,0:T(8,128)(2,1)S(1)}, u32[]{:S(2)}, u32[]{:S(2)}) collective-permute-start(bf16[128,1024]{1,0:T(8,128)(2,1)S(1)} %get-tuple-element.96), channel_id=1, source_target_pairs={{0,12},{4,0},{8,4},{12,8},{1,13},{5,1},{9,5},{13,9},{2,14},{6,2},{... | collective-permute-start | bytes 786440 | tf_op jit(solution)/shard_map/cond/branch_1_fun/ppermute | solution.py:349
  9.2 1.5 %collective-permute-start.22 = (bf16[256,1024]{1,0:T(8,128)(2,1)S(1)}, bf16[256,1024]{1,0:T(8,128)(2,1)S(1)}, u32[]{:S(2)}, u32[]{:S(2)}) collective-permute-start(bf16[256,1024]{1,0:T(8,128)(2,1)S(1)} %get-tuple-element.98.refs_0_), channel_id=1, source_target_pairs={{0,2},{1,3},{2,0},{3,1},{4,6},{5,7},{6,4},{7,5},{8,10},{9,11},{10,... | collective-permute-start | bytes 1572872 | tf_op jit(solution)/shard_map/cond/branch_1_fun/ppermute | solution.py:353
  10.7 0.0 collective-permute-start.24
  10.7 5.2 %collective-permute-done.18.refs_8_ = bf16[128,1024]{1,0:T(8,128)(2,1)S(1)} collective-permute-done((bf16[128,1024]{1,0:T(8,128)(2,1)S(1)}, bf16[128,1024]{1,0:T(8,128)(2,1)S(1)}, u32[]{:S(2)}, u32[]{:S(2)}) %collective-permute-start.18) | collective-permute-done | bytes 262176 | tf_op jit(solution)/shard_map/cond/branch_1_fun/ppermute | solution.py:349
  15.9 4.3 %collective-permute-start.19 = (bf16[128,1024]{1,0:T(8,128)(2,1)S(1)}, bf16[128,1024]{1,0:T(8,128)(2,1)S(1)}, u32[]{:S(2)}, u32[]{:S(2)}) collective-permute-start(bf16[128,1024]{1,0:T(8,128)(2,1)S(1)} %get-tuple-element.97), channel_id=1, source_target_pairs={{0,12},{4,0},{8,4},{12,8},{1,13},{5,1},{9,5},{13,9},{2,14},{6,2},{... | collective-permute-start | bytes 786440 | tf_op jit(solution)/shard_map/cond/branch_1_fun/ppermute | solution.py:349
  20.2 1.5 %collective-permute-start.29 = (bf16[128,1024]{1,0:T(8,128)(2,1)S(1)}, bf16[128,1024]{1,0:T(8,128)(2,1)S(1)}, u32[]{:S(2)}, u32[]{:S(2)}) collective-permute-start(bf16[128,1024]{1,0:T(8,128)(2,1)S(1)} %collective-permute-done.18.refs_8_), channel_id=1, source_target_pairs={{0,2},{1,3},{2,0},{3,1},{4,6},{5,7},{6,4},{7,5},{8,10},{9,11},{10,... | collective-permute-start | bytes 786440 | tf_op jit(solution)/shard_map/cond/branch_1_fun/ppermute | solution.py:353
  21.7 0.0 collective-permute-start.21
  21.7 0.8 %collective-permute-done.24.refs_4_ = bf16[128,1024]{1,0:T(8,128)(2,1)S(1)} collective-permute-done((bf16[128,1024]{1,0:T(8,128)(2,1)S(1)}, bf16[128,1024]{1,0:T(8,128)(2,1)S(1)}, u32[]{:S(2)}, u32[]{:S(2)}) %collective-permute-start.24) | collective-permute-done | bytes 262176 | tf_op jit(solution)/shard_map/cond/branch_1_fun/ppermute | solution.py:349
  22.5 1.5 %collective-permute-start.26 = (bf16[128,1024]{1,0:T(8,128)(2,1)S(1)}, bf16[128,1024]{1,0:T(8,128)(2,1)S(1)}, u32[]{:S(2)}, u32[]{:S(2)}) collective-permute-start(bf16[128,1024]{1,0:T(8,128)(2,1)S(1)} %collective-permute-done.24.refs_4_), channel_id=1, source_target_pairs={{0,2},{1,3},{2,0},{3,1},{4,6},{5,7},{6,4},{7,5},{8,10},{9,11},{10,... | collective-permute-start | bytes 786440 | tf_op jit(solution)/shard_map/cond/branch_1_fun/ppermute | solution.py:353
  24.0 2.7 %collective-permute-done.19.refs_12_ = bf16[128,1024]{1,0:T(8,128)(2,1)S(1)} collective-permute-done((bf16[128,1024]{1,0:T(8,128)(2,1)S(1)}, bf16[128,1024]{1,0:T(8,128)(2,1)S(1)}, u32[]{:S(2)}, u32[]{:S(2)}) %collective-permute-start.19) | collective-permute-done | bytes 262176 | tf_op jit(solution)/shard_map/cond/branch_1_fun/ppermute | solution.py:349
  26.7 0.0 collective-permute-start.28
  26.7 3.0 %collective-permute-done.29.refs_10_ = bf16[128,1024]{1,0:T(8,128)(2,1)S(1)} collective-permute-done((bf16[128,1024]{1,0:T(8,128)(2,1)S(1)}, bf16[128,1024]{1,0:T(8,128)(2,1)S(1)}, u32[]{:S(2)}, u32[]{:S(2)}) %collective-permute-start.29) | collective-permute-done | bytes 262176 | tf_op jit(solution)/shard_map/cond/branch_1_fun/ppermute | solution.py:353
  29.7 0.0 collective-permute-start.25
  29.7 0.0 collective-permute-done.22.refs_2_
  29.7 0.5 collective-permute-start.23
  30.2 3.6 %collective-permute-done.26.refs_6_ = bf16[128,1024]{1,0:T(8,128)(2,1)S(1)} collective-permute-done((bf16[128,1024]{1,0:T(8,128)(2,1)S(1)}, bf16[128,1024]{1,0:T(8,128)(2,1)S(1)}, u32[]{:S(2)}, u32[]{:S(2)}) %collective-permute-start.26) | collective-permute-done | bytes 262176 | tf_op jit(solution)/shard_map/cond/branch_1_fun/ppermute | solution.py:353
  33.8 0.0 collective-permute-start.31
  33.9 0.0 collective-permute-done.28.refs_9_
  33.9 0.5 collective-permute-start.30
  34.4 0.0 collective-permute-done.25.refs_5_
  34.4 0.1 collective-permute-start.27
  34.4 0.0 collective-permute-done.21.refs_1_
  34.4 1.5 %collective-permute-start.20 = (bf16[128,1024]{1,0:T(8,128)(2,1)S(1)}, bf16[128,1024]{1,0:T(8,128)(2,1)S(1)}, u32[]{:S(2)}, u32[]{:S(2)}) collective-permute-start(bf16[128,1024]{1,0:T(8,128)(2,1)S(1)} %collective-permute-done.19.refs_12_), channel_id=1, source_target_pairs={{0,2},{1,3},{2,0},{3,1},{4,6},{5,7},{6,4},{7,5},{8,10},{9,11},{10,... | collective-permute-start | bytes 786440 | tf_op jit(solution)/shard_map/cond/branch_1_fun/ppermute | solution.py:353
  35.9 0.0 collective-permute-done.31.refs_13_
  35.9 0.0 collective-permute-done.30.refs_11_
  35.9 0.2 collective-permute-done.27.refs_7_
  36.1 0.0 collective-permute-done.23.refs_3_
  36.1 6.3 %score_most.5 = (f32[25,128,128]{2,1,0:T(8,128)S(1)}, bf16[640,1024]{1,0:T(8,128)(2,1)S(1)}, f32[640,128]{1,0:T(8,128)S(1)}) custom-call(bf16[256,1024]{1,0:T(8,128)(2,1)S(1)} %get-tuple-element.98.refs_0_, bf16[256,1024]{1,0:T(8,128)(2,1)S(1)} %collective-permute-done.21.refs_1_, bf16[256,1024]{1,0:T(8,128)(2,1)S(1)} %collective-permute-done.22.refs_2_, ...), custom_call_target="tpu_custom_call" | custom-call | tf_op jit(solution)/shard_map/cond/branch_1_fun/score_most/pallas_call | solution.py:299
  42.5 0.6 %collective-permute-done.20.refs_0_ = bf16[128,1024]{1,0:T(8,128)(2,1)S(1)} collective-permute-done((bf16[128,1024]{1,0:T(8,128)(2,1)S(1)}, bf16[128,1024]{1,0:T(8,128)(2,1)S(1)}, u32[]{:S(2)}, u32[]{:S(2)}) %collective-permute-start.20) | collective-permute-done | bytes 262176 | tf_op jit(solution)/shard_map/cond/branch_1_fun/ppermute | solution.py:353
  43.1 0.0 collective-permute-start.32
  43.1 1.5 %collective-permute-done.32.refs_1_ = bf16[128,1024]{1,0:T(8,128)(2,1)S(1)} collective-permute-done((bf16[128,1024]{1,0:T(8,128)(2,1)S(1)}, bf16[128,1024]{1,0:T(8,128)(2,1)S(1)}, u32[]{:S(2)}, u32[]{:S(2)}) %collective-permute-start.32) | collective-permute-done | bytes 262176 | tf_op jit(solution)/shard_map/cond/branch_1_fun/ppermute | solution.py:353
  44.6 1.8 %score_late.5.refs_3_ = f32[32,128]{1,0:T(8,128)S(1)} custom-call(bf16[128,1024]{1,0:T(8,128)(2,1)S(1)} %collective-permute-done.20.refs_0_, bf16[128,1024]{1,0:T(8,128)(2,1)S(1)} %collective-permute-done.32.refs_1_, s32[27]{0:T(128)S(1)} %get-tuple-element.94.refs_2_.plan_ref, s32[1]{0:T(128)} %get-tuple-element.102.refs_3_, ...), custom_call_target="tpu_custom_call" | custom-call | tf_op jit(solution)/shard_map/cond/branch_1_fun/score_late/pallas_call | solution.py:299
  46.5 0.0 copy-start.1
  46.5 0.5 collective-permute-start.33
  47.0 0.0 collective-permute-start.34
  47.0 3.9 %collective-permute-start.35 = (f32[32,128]{1,0:T(8,128)S(1)}, f32[32,128]{1,0:T(8,128)S(1)}, u32[]{:S(2)}, u32[]{:S(2)}) collective-permute-start(f32[32,128]{1,0:T(8,128)S(1)} %score_late.5.refs_3_), channel_id=1, source_target_pairs={{0,4},{4,0},{8,12},{12,8},{1,5},{5,1},{9,13},{13,9},{2,6},{6,2},{1... | collective-permute-start | bytes 49160 | tf_op jit(solution)/shard_map/cond/branch_1_fun/ppermute | solution.py:391
  50.9 1.1 %collective-permute-done.33.refs_0_ = f32[32,128]{1,0:T(8,128)S(1)} collective-permute-done((f32[32,128]{1,0:T(8,128)S(1)}, f32[32,128]{1,0:T(8,128)S(1)}, u32[]{:S(2)}, u32[]{:S(2)}) %collective-permute-start.33) | collective-permute-done | bytes 16416 | tf_op jit(solution)/shard_map/cond/branch_1_fun/ppermute | solution.py:391
  52.1 0.0 copy-start.5
  52.1 0.0 collective-permute-done.34.refs_1_
  52.1 0.0 copy-start.9
  52.1 0.6 %collective-permute-done.35.refs_2_ = f32[32,128]{1,0:T(8,128)S(1)} collective-permute-done((f32[32,128]{1,0:T(8,128)S(1)}, f32[32,128]{1,0:T(8,128)S(1)}, u32[]{:S(2)}, u32[]{:S(2)}) %collective-permute-start.35) | collective-permute-done | bytes 16416 | tf_op jit(solution)/shard_map/cond/branch_1_fun/ppermute | solution.py:391
  52.6 0.0 copy-done.1
  52.7 0.0 copy-done.5
  52.7 0.0 copy-done.9
  52.7 0.0 copy-start.13
  52.7 0.6 %copy-done.13 = f32[32,128]{1,0:T(8,128)} copy-done((f32[32,128]{1,0:T(8,128)}, f32[32,128]{1,0:T(8,128)S(1)}, u32[]{:S(2)}) %copy-start.13) | copy-done | bytes 16408 | tf_op jit(solution)/shard_map/cond
  53.3 0.9 %place_rows.5 = f32[5,128]{1,0:T(8,128)S(1)} custom-call(s32[27]{0:T(128)S(1)} %get-tuple-element.94.refs_2_.plan_ref, f32[32,128]{1,0:T(8,128)} %copy-done.5, f32[32,128]{1,0:T(8,128)} %copy-done.9, f32[32,128]{1,0:T(8,128)} %copy-done.13, f32[32,128]{1,0:T(8,128)} %copy-done.1), custom_call_target="tpu_custom_call" | custom-call | tf_op jit(solution)/shard_map/cond/branch_1_fun/place_rows/pallas_call | solution.py:338
  54.5 0.0 copy-start.17
  54.5 0.6 %copy-done.17 = f32[5,128]{1,0:T(8,128)} copy-done((f32[5,128]{1,0:T(8,128)}, f32[5,128]{1,0:T(8,128)S(1)}, u32[]{:S(2)}) %copy-start.17) | copy-done | bytes 2584
Async XLA Ops:
  0.0 2.0 %copy-start.18 = (s32[5]{0:T(128)S(1)}, s32[5]{0:T(128)}, u32[]{:S(2)}) copy-start(s32[5]{0:T(128)} %count_ref.1) | copy-start | bytes 64
  0.0 2.0 %copy-start.16 = (s32[4,5]{1,0:T(4,128)S(1)}, s32[4,5]{1,0:T(4,128)}, u32[]{:S(2)}) copy-start(s32[4,5]{1,0:T(4,128)} %fetch_ref.1) | copy-start | bytes 244
  0.0 2.0 %copy-start.19 = (s32[1,15]{1,0:T(1,128)S(1)}, s32[1,15]{1,0:T(1,128)}, u32[]{:S(2)}) copy-start(s32[1,15]{1,0:T(1,128)} %left_ref.1) | copy-start | bytes 184
  0.0 2.1 %copy-start.20 = (s32[1,15]{1,0:T(1,128)S(1)}, s32[1,15]{1,0:T(1,128)}, u32[]{:S(2)}) copy-start(s32[1,15]{1,0:T(1,128)} %right_ref.1) | copy-start | bytes 184
  4.1 11.8 %collective-permute-start.18 = (bf16[128,1024]{1,0:T(8,128)(2,1)S(1)}, bf16[128,1024]{1,0:T(8,128)(2,1)S(1)}, u32[]{:S(2)}, u32[]{:S(2)}) collective-permute-start(bf16[128,1024]{1,0:T(8,128)(2,1)S(1)} %get-tuple-element.96), channel_id=1, source_target_pairs={{0,12},{4,0},{8,4},{12,8},{1,13},{5,1},{9,5},{13,9},{2,14},{6,2},{... | collective-permute-start | bytes 786440 | tf_op jit(solution)/shard_map/cond/branch_1_fun/ppermute | solution.py:349
  9.2 20.5 %collective-permute-start.22 = (bf16[256,1024]{1,0:T(8,128)(2,1)S(1)}, bf16[256,1024]{1,0:T(8,128)(2,1)S(1)}, u32[]{:S(2)}, u32[]{:S(2)}) collective-permute-start(bf16[256,1024]{1,0:T(8,128)(2,1)S(1)} %get-tuple-element.98.refs_0_), channel_id=1, source_target_pairs={{0,2},{1,3},{2,0},{3,1},{4,6},{5,7},{6,4},{7,5},{8,10},{9,11},{10,... | collective-permute-start | bytes 1572872 | tf_op jit(solution)/shard_map/cond/branch_1_fun/ppermute | solution.py:353
  10.7 11.8 %collective-permute-start.24 = (bf16[128,1024]{1,0:T(8,128)(2,1)S(1)}, bf16[128,1024]{1,0:T(8,128)(2,1)S(1)}, u32[]{:S(2)}, u32[]{:S(2)}) collective-permute-start(bf16[128,1024]{1,0:T(8,128)(2,1)S(1)} %get-tuple-element.99), channel_id=1, source_target_pairs={{0,4},{4,8},{8,12},{12,0},{1,5},{5,9},{9,13},{13,1},{2,6},{6,10},{... | collective-permute-start | bytes 786440 | tf_op jit(solution)/shard_map/cond/branch_1_fun/ppermute | solution.py:349
  15.9 10.8 %collective-permute-start.19 = (bf16[128,1024]{1,0:T(8,128)(2,1)S(1)}, bf16[128,1024]{1,0:T(8,128)(2,1)S(1)}, u32[]{:S(2)}, u32[]{:S(2)}) collective-permute-start(bf16[128,1024]{1,0:T(8,128)(2,1)S(1)} %get-tuple-element.97), channel_id=1, source_target_pairs={{0,12},{4,0},{8,4},{12,8},{1,13},{5,1},{9,5},{13,9},{2,14},{6,2},{... | collective-permute-start | bytes 786440 | tf_op jit(solution)/shard_map/cond/branch_1_fun/ppermute | solution.py:349
  20.2 9.5 %collective-permute-start.29 = (bf16[128,1024]{1,0:T(8,128)(2,1)S(1)}, bf16[128,1024]{1,0:T(8,128)(2,1)S(1)}, u32[]{:S(2)}, u32[]{:S(2)}) collective-permute-start(bf16[128,1024]{1,0:T(8,128)(2,1)S(1)} %collective-permute-done.18.refs_8_), channel_id=1, source_target_pairs={{0,2},{1,3},{2,0},{3,1},{4,6},{5,7},{6,4},{7,5},{8,10},{9,11},{10,... | collective-permute-start | bytes 786440 | tf_op jit(solution)/shard_map/cond/branch_1_fun/ppermute | solution.py:353
  21.7 12.7 %collective-permute-start.21 = (bf16[256,1024]{1,0:T(8,128)(2,1)S(1)}, bf16[256,1024]{1,0:T(8,128)(2,1)S(1)}, u32[]{:S(2)}, u32[]{:S(2)}) collective-permute-start(bf16[256,1024]{1,0:T(8,128)(2,1)S(1)} %get-tuple-element.98.refs_0_), channel_id=1, source_target_pairs={{0,1},{1,0},{2,3},{3,2},{4,5},{5,4},{6,7},{7,6},{8,9},{9,8},{10,11... | collective-permute-start | bytes 1572872 | tf_op jit(solution)/shard_map/cond/branch_1_fun/ppermute | solution.py:353
  22.5 11.3 %collective-permute-start.26 = (bf16[128,1024]{1,0:T(8,128)(2,1)S(1)}, bf16[128,1024]{1,0:T(8,128)(2,1)S(1)}, u32[]{:S(2)}, u32[]{:S(2)}) collective-permute-start(bf16[128,1024]{1,0:T(8,128)(2,1)S(1)} %collective-permute-done.24.refs_4_), channel_id=1, source_target_pairs={{0,2},{1,3},{2,0},{3,1},{4,6},{5,7},{6,4},{7,5},{8,10},{9,11},{10,... | collective-permute-start | bytes 786440 | tf_op jit(solution)/shard_map/cond/branch_1_fun/ppermute | solution.py:353
  26.7 7.1 %collective-permute-start.28 = (bf16[128,1024]{1,0:T(8,128)(2,1)S(1)}, bf16[128,1024]{1,0:T(8,128)(2,1)S(1)}, u32[]{:S(2)}, u32[]{:S(2)}) collective-permute-start(bf16[128,1024]{1,0:T(8,128)(2,1)S(1)} %collective-permute-done.18.refs_8_), channel_id=1, source_target_pairs={{0,1},{1,0},{2,3},{3,2},{4,5},{5,4},{6,7},{7,6},{8,9},{9,8},{10,11... | collective-permute-start | bytes 786440 | tf_op jit(solution)/shard_map/cond/branch_1_fun/ppermute | solution.py:353
  29.7 4.7 %collective-permute-start.25 = (bf16[128,1024]{1,0:T(8,128)(2,1)S(1)}, bf16[128,1024]{1,0:T(8,128)(2,1)S(1)}, u32[]{:S(2)}, u32[]{:S(2)}) collective-permute-start(bf16[128,1024]{1,0:T(8,128)(2,1)S(1)} %collective-permute-done.24.refs_4_), channel_id=1, source_target_pairs={{0,1},{1,0},{2,3},{3,2},{4,5},{5,4},{6,7},{7,6},{8,9},{9,8},{10,11... | collective-permute-start | bytes 786440 | tf_op jit(solution)/shard_map/cond/branch_1_fun/ppermute | solution.py:353
  29.7 6.4 %collective-permute-start.23 = (bf16[256,1024]{1,0:T(8,128)(2,1)S(1)}, bf16[256,1024]{1,0:T(8,128)(2,1)S(1)}, u32[]{:S(2)}, u32[]{:S(2)}) collective-permute-start(bf16[256,1024]{1,0:T(8,128)(2,1)S(1)} %collective-permute-done.22.refs_2_), channel_id=1, source_target_pairs={{0,1},{1,0},{2,3},{3,2},{4,5},{5,4},{6,7},{7,6},{8,9},{9,8},{10,11... | collective-permute-start | bytes 1572872 | tf_op jit(solution)/shard_map/cond/branch_1_fun/ppermute | solution.py:353
  33.8 2.1 %collective-permute-start.31 = (bf16[128,1024]{1,0:T(8,128)(2,1)S(1)}, bf16[128,1024]{1,0:T(8,128)(2,1)S(1)}, u32[]{:S(2)}, u32[]{:S(2)}) collective-permute-start(bf16[128,1024]{1,0:T(8,128)(2,1)S(1)} %collective-permute-done.19.refs_12_), channel_id=1, source_target_pairs={{0,1},{1,0},{2,3},{3,2},{4,5},{5,4},{6,7},{7,6},{8,9},{9,8},{10,11... | collective-permute-start | bytes 786440 | tf_op jit(solution)/shard_map/cond/branch_1_fun/ppermute | solution.py:353
  33.9 2.1 %collective-permute-start.30 = (bf16[128,1024]{1,0:T(8,128)(2,1)S(1)}, bf16[128,1024]{1,0:T(8,128)(2,1)S(1)}, u32[]{:S(2)}, u32[]{:S(2)}) collective-permute-start(bf16[128,1024]{1,0:T(8,128)(2,1)S(1)} %collective-permute-done.29.refs_10_), channel_id=1, source_target_pairs={{0,1},{1,0},{2,3},{3,2},{4,5},{5,4},{6,7},{7,6},{8,9},{9,8},{10,11... | collective-permute-start | bytes 786440 | tf_op jit(solution)/shard_map/cond/branch_1_fun/ppermute | solution.py:353
  34.4 1.8 %collective-permute-start.27 = (bf16[128,1024]{1,0:T(8,128)(2,1)S(1)}, bf16[128,1024]{1,0:T(8,128)(2,1)S(1)}, u32[]{:S(2)}, u32[]{:S(2)}) collective-permute-start(bf16[128,1024]{1,0:T(8,128)(2,1)S(1)} %collective-permute-done.26.refs_6_), channel_id=1, source_target_pairs={{0,1},{1,0},{2,3},{3,2},{4,5},{5,4},{6,7},{7,6},{8,9},{9,8},{10,11... | collective-permute-start | bytes 786440 | tf_op jit(solution)/shard_map/cond/branch_1_fun/ppermute | solution.py:353
  34.4 8.7 %collective-permute-start.20 = (bf16[128,1024]{1,0:T(8,128)(2,1)S(1)}, bf16[128,1024]{1,0:T(8,128)(2,1)S(1)}, u32[]{:S(2)}, u32[]{:S(2)}) collective-permute-start(bf16[128,1024]{1,0:T(8,128)(2,1)S(1)} %collective-permute-done.19.refs_12_), channel_id=1, source_target_pairs={{0,2},{1,3},{2,0},{3,1},{4,6},{5,7},{6,4},{7,5},{8,10},{9,11},{10,... | collective-permute-start | bytes 786440 | tf_op jit(solution)/shard_map/cond/branch_1_fun/ppermute | solution.py:353
  43.1 1.5 %collective-permute-start.32 = (bf16[128,1024]{1,0:T(8,128)(2,1)S(1)}, bf16[128,1024]{1,0:T(8,128)(2,1)S(1)}, u32[]{:S(2)}, u32[]{:S(2)}) collective-permute-start(bf16[128,1024]{1,0:T(8,128)(2,1)S(1)} %collective-permute-done.20.refs_0_), channel_id=1, source_target_pairs={{0,1},{1,0},{2,3},{3,2},{4,5},{5,4},{6,7},{7,6},{8,9},{9,8},{10,11... | collective-permute-start | bytes 786440 | tf_op jit(solution)/shard_map/cond/branch_1_fun/ppermute | solution.py:353
  46.5 6.2 %copy-start.1 = (f32[32,128]{1,0:T(8,128)}, f32[32,128]{1,0:T(8,128)S(1)}, u32[]{:S(2)}) copy-start(f32[32,128]{1,0:T(8,128)S(1)} %score_late.5.refs_3_) | copy-start | bytes 49156 | tf_op jit(solution)/shard_map/cond
  46.5 5.6 %collective-permute-start.33 = (f32[32,128]{1,0:T(8,128)S(1)}, f32[32,128]{1,0:T(8,128)S(1)}, u32[]{:S(2)}, u32[]{:S(2)}) collective-permute-start(f32[32,128]{1,0:T(8,128)S(1)} %score_late.5.refs_3_), channel_id=1, source_target_pairs={{0,12},{4,8},{8,4},{12,0},{1,13},{5,9},{9,5},{13,1},{2,14},{6,10},... | collective-permute-start | bytes 49160 | tf_op jit(solution)/shard_map/cond/branch_1_fun/ppermute | solution.py:391
  47.0 5.1 %collective-permute-start.34 = (f32[32,128]{1,0:T(8,128)S(1)}, f32[32,128]{1,0:T(8,128)S(1)}, u32[]{:S(2)}, u32[]{:S(2)}) collective-permute-start(f32[32,128]{1,0:T(8,128)S(1)} %score_late.5.refs_3_), channel_id=1, source_target_pairs={{0,8},{4,12},{8,0},{12,4},{1,9},{5,13},{9,1},{13,5},{2,10},{6,14},... | collective-permute-start | bytes 49160 | tf_op jit(solution)/shard_map/cond/branch_1_fun/ppermute | solution.py:391
  47.0 5.6 %collective-permute-start.35 = (f32[32,128]{1,0:T(8,128)S(1)}, f32[32,128]{1,0:T(8,128)S(1)}, u32[]{:S(2)}, u32[]{:S(2)}) collective-permute-start(f32[32,128]{1,0:T(8,128)S(1)} %score_late.5.refs_3_), channel_id=1, source_target_pairs={{0,4},{4,0},{8,12},{12,8},{1,5},{5,1},{9,13},{13,9},{2,6},{6,2},{1... | collective-permute-start | bytes 49160 | tf_op jit(solution)/shard_map/cond/branch_1_fun/ppermute | solution.py:391
  52.1 0.6 %copy-start.5 = (f32[32,128]{1,0:T(8,128)}, f32[32,128]{1,0:T(8,128)S(1)}, u32[]{:S(2)}) copy-start(f32[32,128]{1,0:T(8,128)S(1)} %collective-permute-done.33.refs_0_) | copy-start | bytes 49156 | tf_op jit(solution)/shard_map/cond
  52.1 0.6 %copy-start.9 = (f32[32,128]{1,0:T(8,128)}, f32[32,128]{1,0:T(8,128)S(1)}, u32[]{:S(2)}) copy-start(f32[32,128]{1,0:T(8,128)S(1)} %collective-permute-done.34.refs_1_) | copy-start | bytes 49156 | tf_op jit(solution)/shard_map/cond
  52.7 0.6 %copy-start.13 = (f32[32,128]{1,0:T(8,128)}, f32[32,128]{1,0:T(8,128)S(1)}, u32[]{:S(2)}) copy-start(f32[32,128]{1,0:T(8,128)S(1)} %collective-permute-done.35.refs_2_) | copy-start | bytes 49156 | tf_op jit(solution)/shard_map/cond
  54.5 0.6 %copy-start.17 = (f32[5,128]{1,0:T(8,128)}, f32[5,128]{1,0:T(8,128)S(1)}, u32[]{:S(2)}) copy-start(f32[5,128]{1,0:T(8,128)S(1)} %get-tuple-element.340) | copy-start | bytes 7684
